TPU v7x, 32 devices: a whole 2x2x4 slice. The times are simulated.
32 devices in a mesh: dp: 8 (over y, x, core), mp: 4 (over z).
Axes of the slice: x: 2, y: 2, z: 4, core: 2. Of those that a mesh axis runs over, the one named last changes fastest.
Arguments:
- residual_in: bfloat16 [8192, 1024], P(('dp', 'mp')), may hold values from -6 to 6
- upstream: bfloat16 [8192, 1024], P(('dp', 'mp')), may hold values from -6 to 6
- layer_norm_gain: float32 [1024], replicated, may hold values from 0.1 to 1.9
- layer_norm_bias: float32 [1024], replicated, may hold values from -3 to 3
- attend_weight: bfloat16 [1024, 3072], replicated, may hold values from -0.1875 to 0.1875
- output_weight: bfloat16 [1024, 1024], replicated, may hold values from -1 to 1
- expand_weight: bfloat16 [1024, 4096], P(None, 'mp'), may hold values from -0.1875 to 0.1875
- expand_bias: float32 [4096], P('mp'), may hold values from -3 to 3
- shrink_weight: bfloat16 [4096, 1024], P('mp'), may hold values from -0.09375 to 0.09375
- shrink_bias: float32 [1024], replicated, may hold values from -3 to 3
- seq_lengths: int32 [8, 16], P('dp'), may hold values from 0 to 256, as said below
- terminal_pos: int32 [8, 16], P('dp', 'mp'), may hold values from 0 to 255, as said below
- window_offset: int32 [8, 16], P('dp', 'mp'), may hold values from 0 to 8191
Outputs:
- residual_out: bfloat16 [8192, 1024], P(('dp', 'mp'))
- residual_grad: float32 [8192, 1024], P(('dp', 'mp'))
- norm_gain_gradient: float32 [1024], replicated
- shift_grad: float32 [1024], replicated
- attend_grad: float32 [1024, 3072], P('dp')
- output_grad: float32 [1024, 1024], P('dp')
- expand_grad: float32 [1024, 4096], P('dp', 'mp')
- expand_bias_grad: float32 [4096], P('mp')
- shrink_grad: float32 [4096, 1024], P('mp', 'dp')
- shrink_bias_grad: float32 [1024], replicated
Inputs may be any that keep to these rules, and one draw needn't show every extreme that they name: `seq_lengths`: the lengths of one device's 4 slots sum to at most 256; its sequences fill its rows from the first in slot order and the remaining rows are padding; an empty slot has length 0. `terminal_pos`: below the slot's length; 0 for an empty slot.
All inputs are finite; a program needn't handle non-finite values.
Results may differ from a plain program's by a relative error of at most 0.015.
Values may be sent and summed in bfloat16 or wider, within the bound.
No kernel may reach another device: no remote copies, remote signals or barrier semaphores. Data moves between devices by JAX's collectives and lax.ppermute only.
A program may use at most 128 MiB of HBM per device.

v0:
```python
from functools import partial

import jax
import jax.numpy as jnp
from jax import lax
from jax.sharding import PartitionSpec as P

HEADS = 16
HEAD_DIM = 64
ROT = 32
SEQ_DEV = 4


EPSILON = 1e-05
NEGATIVE = -1e30


def layout(lengths_row, terminal_row, offset_row, tokens):
    seq_ends = jnp.cumsum(lengths_row)
    seq_starts = seq_ends - lengths_row
    places = jnp.arange(tokens, dtype=jnp.int32)
    seq_index = jnp.sum((places[:, None] >= seq_ends[None, :]).astype(jnp.int32), axis=1)
    member = seq_index[:, None] == jnp.arange(SEQ_DEV, dtype=jnp.int32)[None, :]
    local_index = places - jnp.sum(jnp.where(member, seq_starts[None, :], 0), axis=1)
    terminal = jnp.sum(jnp.where(member, terminal_row[None, :], 0), axis=1)
    offset = jnp.sum(jnp.where(member, offset_row[None, :], 0), axis=1)
    positions = jnp.where(local_index <= terminal, offset + local_index, local_index - terminal - 1)
    live_rows = (seq_index < SEQ_DEV).astype(jnp.float32)
    return (seq_index, positions.astype(jnp.float32), live_rows)


def rotary_tables(positions):
    pair_index = jnp.arange(HEAD_DIM, dtype=jnp.int32) // 2
    frequency = jnp.where(
        pair_index < ROT // 2, 10000.0 ** (-2.0 * pair_index.astype(jnp.float32) / ROT), 0.0
    )
    angles = positions[:, None] * frequency[None, :]
    parity = jnp.arange(HEAD_DIM, dtype=jnp.int32) % 2
    return (jnp.cos(angles), jnp.where(parity == 0, -jnp.sin(angles), jnp.sin(angles)))


def pair_swap(values):
    shape = values.shape
    return values.reshape(shape[0], shape[1], shape[2] // 2, 2)[..., ::-1].reshape(shape)


def rotate(values, cosine, signed_sine):
    return values * cosine[:, None, :] + pair_swap(values) * signed_sine[:, None, :]


def rotate_back(values, cosine, signed_sine):
    return values * cosine[:, None, :] + pair_swap(values * signed_sine[:, None, :])


def contract_rows(left, right):
    return lax.dot_general(
        left, right, (((0,), (0,)), ((), ())), preferred_element_type=jnp.float32
    )


def contract_cols(left, right):
    return lax.dot_general(
        left, right, (((1,), (1,)), ((), ())), preferred_element_type=jnp.float32
    )


def local(
    residual_in,
    upstream,
    layer_norm_gain,
    layer_norm_bias,
    attend_weight,
    output_weight,
    expand_weight,
    expand_bias,
    shrink_weight,
    shrink_bias,
    seq_lengths,
    terminal_pos,
    window_offset,
):
    tokens = residual_in.shape[0]
    width = residual_in.shape[1]
    data_ways = lax.axis_size("dp")
    length_row = seq_lengths[0]
    own_lengths = lax.dynamic_slice_in_dim(length_row, lax.axis_index("mp") * SEQ_DEV, SEQ_DEV)
    seq_index, positions, live_rows = layout(own_lengths, terminal_pos[0], window_offset[0], tokens)
    group_count = jnp.sum(length_row).astype(jnp.float32)
    total_count = lax.psum(group_count, "dp")
    group_weight = data_ways * group_count / total_count
    hidden = residual_in.astype(jnp.float32)
    row_mean = jnp.mean(hidden, axis=-1, keepdims=True)
    mean_removed = hidden - row_mean
    variance = jnp.mean(mean_removed * mean_removed, axis=-1, keepdims=True)
    inverse_deviation = lax.rsqrt(variance + EPSILON)
    standardized_input = mean_removed * inverse_deviation
    normalized_reduced = (standardized_input * layer_norm_gain + layer_norm_bias).astype(
        jnp.bfloat16
    )
    projected = jnp.dot(normalized_reduced, attend_weight, preferred_element_type=jnp.float32)
    query_part = projected[:, :width].reshape(tokens, HEADS, HEAD_DIM)
    key_part = projected[:, width : 2 * width].reshape(tokens, HEADS, HEAD_DIM)
    value_part = projected[:, 2 * width :].reshape(tokens, HEADS, HEAD_DIM)
    cosine, signed_sine = rotary_tables(positions)
    score_scale = HEAD_DIM ** (-0.5)
    queries = (rotate(query_part, cosine, signed_sine) * score_scale).astype(jnp.bfloat16)
    key_rows = rotate(key_part, cosine, signed_sine).astype(jnp.bfloat16)
    value_rows = value_part.astype(jnp.bfloat16)
    places = jnp.arange(tokens, dtype=jnp.int32)

    def block_mask():
        return (seq_index[None, :] == seq_index[:, None]) & (places[None, :] <= places[:, None])

    scores = jnp.einsum("qhd,khd->hqk", queries, key_rows, preferred_element_type=jnp.float32)
    scores = jnp.where(block_mask()[None], scores, NEGATIVE)
    row_max = jnp.max(scores, axis=-1, keepdims=True)
    exponent = jnp.exp(scores - row_max)
    row_total = jnp.sum(exponent, axis=-1, keepdims=True)
    probability = (exponent / row_total).astype(jnp.bfloat16)
    log_totals = row_max + jnp.log(row_total)
    attended_blocks = jnp.einsum(
        "hqk,khd->qhd", probability, value_rows, preferred_element_type=jnp.float32
    )
    attended_low = attended_blocks.reshape(tokens, width).astype(jnp.bfloat16)
    attention_out = jnp.dot(attended_low, output_weight, preferred_element_type=jnp.float32)
    gathered = lax.all_gather(normalized_reduced, "mp", axis=0, tiled=True)
    expanded = jnp.dot(gathered, expand_weight, preferred_element_type=jnp.float32) + expand_bias
    activated_low = jax.nn.gelu(expanded, approximate=True).astype(jnp.bfloat16)
    row_slice = activated_low
    mlp_out = (
        lax.psum_scatter(
            jnp.dot(row_slice, shrink_weight, preferred_element_type=jnp.float32).astype(
                jnp.bfloat16
            ),
            "mp",
            scatter_dimension=0,
            tiled=True,
        ).astype(jnp.float32)
        + shrink_bias
    )
    branch = attention_out + mlp_out
    residual_out = (hidden + live_rows[:, None] * branch).astype(jnp.bfloat16)
    scaled = upstream.astype(jnp.float32) * group_weight
    branch_grad = (scaled * live_rows[:, None]).astype(jnp.bfloat16)
    shrink_bias_grad = jnp.sum(branch_grad, axis=0, dtype=jnp.float32)
    output_grad = contract_rows(attended_low, branch_grad)
    attended_grad = (
        contract_cols(branch_grad, output_weight)
        .astype(jnp.bfloat16)
        .reshape(tokens, HEADS, HEAD_DIM)
    )
    gathered_grad = lax.all_gather(branch_grad, "mp", axis=0, tiled=True)
    shrink_turned = contract_rows(gathered_grad, activated_low)
    activated_grad = contract_cols(gathered_grad, shrink_weight)
    gelu_value, gelu_pullback = jax.vjp(partial(jax.nn.gelu, approximate=True), expanded)
    expanded_grad = gelu_pullback(activated_grad)[0].astype(jnp.bfloat16)
    expand_bias_grad = jnp.sum(expanded_grad, axis=0, dtype=jnp.float32)
    expand_grad = contract_rows(gathered, expanded_grad)
    row_slice = expanded_grad
    normed_grad_mlp = lax.psum_scatter(
        contract_cols(row_slice, expand_weight).astype(jnp.bfloat16),
        "mp",
        scatter_dimension=0,
        tiled=True,
    ).astype(jnp.float32)
    scores = jnp.einsum("qhd,khd->hqk", queries, key_rows, preferred_element_type=jnp.float32)
    probability = jnp.where(block_mask()[None], jnp.exp(scores - log_totals), 0.0)
    probability_low = probability.astype(jnp.bfloat16)
    probs_grad = jnp.einsum(
        "qhd,khd->hqk", attended_grad, value_rows, preferred_element_type=jnp.float32
    )
    row_dot = jnp.sum(probability * probs_grad, axis=-1, keepdims=True)
    scores_grad = (probability * (probs_grad - row_dot)).astype(jnp.bfloat16)
    query_grads = jnp.einsum(
        "hqk,khd->qhd", scores_grad, key_rows, preferred_element_type=jnp.float32
    )
    key_grad = jnp.einsum("hqk,qhd->khd", scores_grad, queries, preferred_element_type=jnp.float32)
    value_grad = jnp.einsum(
        "hqk,qhd->khd", probability_low, attended_grad, preferred_element_type=jnp.float32
    )
    query_back = rotate_back(query_grads * score_scale, cosine, signed_sine).reshape(tokens, width)
    key_back = rotate_back(key_grad, cosine, signed_sine).reshape(tokens, width)
    projected_grad = jnp.concatenate(
        [query_back, key_back, value_grad.reshape(tokens, width)], axis=1
    ).astype(jnp.bfloat16)
    attend_grad = contract_rows(normalized_reduced, projected_grad)
    normalized_gradient = contract_cols(projected_grad, attend_weight) + normed_grad_mlp
    norm_gain_gradient = jnp.sum(normalized_gradient * standardized_input, axis=0)
    shift_grad = jnp.sum(normalized_gradient, axis=0)
    standardized_gradient = normalized_gradient * layer_norm_gain
    residual_grad = scaled + inverse_deviation * (
        standardized_gradient
        - jnp.mean(standardized_gradient, axis=-1, keepdims=True)
        - standardized_input
        * jnp.mean(standardized_gradient * standardized_input, axis=-1, keepdims=True)
    )
    attention_mats = jnp.concatenate([attend_grad, output_grad], axis=1)
    small_local = jnp.concatenate([norm_gain_gradient, shift_grad, shrink_bias_grad])
    small_group, expand_bias_sum = lax.psum((small_local, expand_bias_grad), "dp")
    attention_piece, expand_piece, shrink_piece = (
        lax.psum_scatter(
            attention_mats.astype(jnp.bfloat16), "dp", scatter_dimension=0, tiled=True
        ).astype(jnp.float32),
        lax.psum_scatter(
            expand_grad.astype(jnp.bfloat16), "dp", scatter_dimension=0, tiled=True
        ).astype(jnp.float32),
        lax.psum_scatter(
            shrink_turned.astype(jnp.bfloat16), "dp", scatter_dimension=0, tiled=True
        ).astype(jnp.float32),
    )
    attention_total, small_total = (
        lax.psum(attention_piece.astype(jnp.bfloat16), "mp").astype(jnp.float32),
        lax.psum(small_group.astype(jnp.bfloat16), "mp").astype(jnp.float32),
    )
    attend_sum = attention_total[:, : 3 * width]
    output_sum = attention_total[:, 3 * width :]
    gain_sum = small_total[:width]
    shift_sum = small_total[width : 2 * width]
    shrink_bias_sum = small_total[2 * width :]
    shrink_sum = jnp.transpose(shrink_piece)
    return (
        residual_out,
        residual_grad,
        gain_sum,
        shift_sum,
        attend_sum,
        output_sum,
        expand_piece,
        expand_bias_sum,
        shrink_sum,
        shrink_bias_sum,
    )


def solution(mesh):
    in_specs = (
        P(("dp", "mp"), None),
        P(("dp", "mp"), None),
        P(),
        P(),
        P(),
        P(),
        P(None, "mp"),
        P("mp"),
        P("mp", None),
        P(),
        P("dp", None),
        P("dp", "mp"),
        P("dp", "mp"),
    )
    out_specs = (
        P(("dp", "mp"), None),
        P(("dp", "mp"), None),
        P(),
        P(),
        P("dp", None),
        P("dp", None),
        P("dp", "mp"),
        P("mp"),
        P("mp", "dp"),
        P(),
    )
    return jax.shard_map(local, mesh=mesh, in_specs=in_specs, out_specs=out_specs, check_vma=False)
```

profile of v0, /device:TPU:0, one launch (start us, length us, event | category | flops | bytes accessed | tf_op | source)
XLA Modules:
  0.0 430.8 jit_solution(1344377975571400342)
XLA Ops:
  9.9 2.1 fusion.28
  14.1 15.6 %psum.35 = f32[]{:T(128)} all-reduce(f32[]{:T(128)S(6)} %convert_element_type.138), channel_id=1, replica_groups=mesh['dp'=8,'mp'=4] {'dp'}, use_global_device_ids=true, to_apply=%region_11.12 | all-reduce | flops 1 | bytes 8 | tf_op jit(solution)/shard_map/psum | solution.py:89
  31.4 2.0 convert_reduce_fusion.2
  33.5 27.4 %all-gather.3.cloned.1.call-done = bf16[1024,1024]{1,0:T(8,128)(2,1)} async-done(((bf16[256,1024]{1,0:T(8,128)(2,1)}), bf16[1024,1024]{1,0:T(8,128)(2,1)}) %all-gather.3.cloned.1.call-update) | async-done | bytes 2097168 | tf_op jit(solution)/shard_map/all_gather | solution.py:126
  60.9 6.5 %fusion.48 = f32[1024,1024]{1,0:T(8,128)} fusion(bf16[1024,1024]{1,0:T(8,128)(2,1)} %all-gather.3.cloned.1.call-done, bf16[1024,1024]{1,0:T(8,128)(2,1)} %param.19), kind=kOutput, calls=%fused_computation.110 | convolution fusion | flops 2147483648 | bytes 8388608 | tf_op jit(solution)/shard_map/dot_general | solution.py:127
  67.4 40.3 %all-gather.5.cloned.1.call-done = bf16[1024,1024]{1,0:T(8,128)(2,1)} async-done(((bf16[256,1024]{1,0:T(8,128)(2,1)}), bf16[1024,1024]{1,0:T(8,128)(2,1)}) %all-gather.5.cloned.1.call-update) | async-done | bytes 2097168 | tf_op jit(solution)/shard_map/all_gather | solution.py:152
  107.7 6.7 %convolution_convert_fusion.1 = bf16[1024,1024]{1,0:T(8,128)(2,1)} fusion(bf16[1024,1024]{1,0:T(8,128)(2,1)} %all-gather.5.cloned.1.call-done, f32[1024,1024]{1,0:T(8,128)} %fusion.48, f32[1024]{0:T(1024)S(1)} %copy-done.35), kind=kOutput, calls=%fused_computation.26 | convolution fusion | flops 2159017984 | bytes 8392704 | tf_op jit(solution)/shard_map/dot_general | solution.py:56
  115.0 3.1 convolution_convert_fusion.6
  118.1 6.6 %fusion.47 = f32[256,3072]{1,0:T(8,128)} fusion(bf16[256,1024]{1,0:T(8,128)(2,1)S(1)} %copy-done.19, bf16[1024,3072]{1,0:T(8,128)(2,1)} %param.17), kind=kOutput, calls=%fused_computation.109 | convolution fusion | flops 1610612736 | bytes 9961472 | tf_op jit(solution)/shard_map/dot_general | solution.py:100
  124.7 5.1 %convert_reduce_fusion = (f32[1024]{0:T(1024)S(1)}, bf16[1024,1024]{1,0:T(8,128)(2,1)S(1)}) fusion(f32[1024,1024]{1,0:T(8,128)S(1)} %copy-done.36, f32[1024]{0:T(1024)S(1)} %copy-done.35, bf16[1024,1024]{1,0:T(8,128)(2,1)S(1)} %copy-done.34, bf16[1024,1024]{1,0:T(8,128)(2,1)S(1)} %copy-done), kind=kOutput, calls=%fused_computation.11 | convolution fusion | flops 2171599872 | bytes 10493952 | tf_op jit(solution)/shard_map/dot_general | solution.py:62
  131.2 3.8 convolution_convert_fusion.2
  135.2 3.1 fusion.45
  138.3 2.1 slice.42
  143.1 2.0 copy.49
  145.1 2.5 copy.50
  147.7 2.9 reshape_reshape.6
  150.6 6.0 %rev.12 = f32[256,16,32,2]{0,3,2,1:T(2,128)} reverse(f32[256,16,32,2]{0,3,2,1:T(2,128)} %reshape_reshape.6), dimensions={3} | reverse | bytes 2097152 | tf_op jit(solution)/shard_map/rev | solution.py:44
  156.7 3.0 reshape.248
  161.3 6.1 %rev.13 = f32[256,16,32,2]{0,3,2,1:T(2,128)} reverse(f32[256,16,32,2]{0,3,2,1:T(2,128)} %reshape_reshape.7), dimensions={3} | reverse | bytes 2097152 | tf_op jit(solution)/shard_map/rev | solution.py:44
  167.4 3.0 reshape.250
  171.0 2.4 add_convert_fusion.2
  175.0 1.9 copy-done.1
  177.7 3.7 convolution_convert_fusion.4
  181.7 3.6 multiply_reduce_fusion
  187.8 1.8 broadcast_multiply_fusion
  189.6 2.9 reshape.252
  192.5 6.1 %rev.14 = f32[256,16,32,2]{0,3,2,1:T(2,128)} reverse(f32[256,16,32,2]{0,3,2,1:T(2,128)} %reshape.252), dimensions={3} | reverse | bytes 2097152 | tf_op jit(solution)/shard_map/rev | solution.py:44
  198.6 2.9 reshape.253
  201.5 3.7 broadcast_multiply_fusion.1
  205.2 2.9 reshape.255
  208.0 6.0 %rev.15 = f32[256,16,32,2]{0,3,2,1:T(2,128)} reverse(f32[256,16,32,2]{0,3,2,1:T(2,128)} %reshape.255), dimensions={3} | reverse | bytes 2097152 | tf_op jit(solution)/shard_map/rev | solution.py:44
  214.1 2.9 reshape.256
  217.0 3.4 fusion.20
  220.5 2.1 convolution_convert_fusion.3
  225.3 4.6 %convolution_convert_fusion = bf16[1024,3072]{1,0:T(8,128)(2,1)} fusion(bf16[256,1024]{1,0:T(8,128)(2,1)S(1)} %copy-done.20, bf16[256,1024]{0,1:T(8,128)(2,1)S(1)} %bitcast.87, bf16[256,1024]{0,1:T(8,128)(2,1)S(1)} %bitcast.83, bf16[256,1024]{0,1:T(8,128)(2,1)S(1)} %bitcast.85), kind=kOutput, calls=%fused_computation.3 | convolution fusion | flops 1618477056 | bytes 8388608 | tf_op jit(solution)/shard_map/dot_general | solution.py:56
  229.9 7.6 %pad_maximum_fusion = bf16[1024,4096]{1,0:T(8,128)(2,1)} fusion(bf16[1024,1024]{1,0:T(8,128)(2,1)} %convolution_convert_fusion.3, bf16[1024,3072]{1,0:T(8,128)(2,1)} %convolution_convert_fusion), kind=kLoop, calls=%fused_computation | loop fusion | flops 16777216 | bytes 16777216 | tf_op jit(solution)/shard_map/concatenate | solution.py:197
  237.8 6.4 %convolution_convert_fusion.5 = bf16[1024,1024]{1,0:T(8,128)(2,1)} fusion(bf16[1024,1024]{1,0:T(8,128)(2,1)S(1)} %copy-done, f32[1024,1024]{1,0:T(8,128)} %fusion.48, f32[1024]{0:T(1024)S(1)} %copy-done.35), kind=kOutput, calls=%fused_computation.30 | convolution fusion | flops 2159017984 | bytes 8392704 | tf_op jit(solution)/shard_map/dot_general | solution.py:132
  246.4 1.8 convert_element_type.151
  248.2 6.3 %fusion.33 = (f32[1024]{0:T(1024)S(1)}, f32[256]{0:T(256)S(1)}, f32[256]{0:T(256)S(1)}, f32[1024]{0:T(1024)S(1)}, f32[256,1024]{1,0:T(8,128)}) fusion(bf16[256,1024]{1,0:T(8,128)(2,1)S(1)} %copy-done.5, f32[256]{0:T(256)S(1)} %add_rsqrt_fusion, f32[256]{0:T(256)S(1)} %broadcast_multiply_fusion.6, f32[1024]{0:T(1024)S(1)} %copy-done.27, ...), kind=kOutput, calls=%fused_computation.56 | convolution fusion | flops 1618474496 | bytes 9977856 | tf_op jit(solution)/shard_map/dot_general | solution.py:62
  254.5 24.8 %all-reduce = (bf16[3072]{0:T(1024)(128)(2,1)S(1)}, f32[1024]{0:T(1024)}) all-reduce(f32[3072]{0:T(1024)S(1)} %pad_maximum_fusion.4, f32[1024]{0:T(1024)S(1)} %get-tuple-element.49), channel_id=1, replica_groups=mesh['dp'=8,'mp'=4] {'dp'}, use_global_device_ids=true, to_apply=%region_19.20 | all-reduce | flops 4096 | bytes 26624 | tf_op jit(solution)/shard_map/psum | solution.py:199
  279.4 9.6 %psum.37 = bf16[3072]{0:T(1024)(128)(2,1)S(1)} all-reduce(bf16[3072]{0:T(1024)(128)(2,1)S(1)} %get-tuple-element.47), channel_id=1, replica_groups=mesh['dp'=8,'mp'=4] {'mp'}, use_global_device_ids=true, to_apply=%region_20.21 | all-reduce | flops 3072 | bytes 12288 | tf_op jit(solution)/shard_map/psum | solution.py:213
  289.0 30.6 %reduce-scatter.10.cloned.1.call-done = bf16[128,4096]{1,0:T(8,128)(2,1)} async-done(((bf16[1024,4096]{1,0:T(8,128)(2,1)}), bf16[128,4096]{1,0:T(8,128)(2,1)}) %reduce-scatter.10.cloned.1.call-update) | async-done | bytes 1048592 | tf_op jit(solution)/shard_map/reduce_scatter | solution.py:201
  320.3 2.8 fusion.32
  323.0 42.8 %reduce-scatter.6.cloned.1.call-done = bf16[256,1024]{1,0:T(8,128)(2,1)} async-done(((bf16[1024,1024]{1,0:T(8,128)(2,1)}), bf16[256,1024]{1,0:T(8,128)(2,1)}) %reduce-scatter.6.cloned.1.call-update) | async-done | bytes 524304 | tf_op jit(solution)/shard_map/reduce_scatter | solution.py:131
  365.8 3.3 fusion.19
  369.1 50.4 %all-reduce.3.cloned.1.call-done = bf16[128,4096]{1,0:T(8,128)(2,1)} async-done(((bf16[128,4096]{1,0:T(8,128)(2,1)}), bf16[128,4096]{1,0:T(8,128)(2,1)}) %all-reduce.3.cloned.1.call-update) | async-done | bytes 1048592 | tf_op jit(solution)/shard_map/psum | solution.py:212
  419.5 1.8 slice.39
  421.3 2.4 slice.38
  (127 shorter events, 23.0 us)
Async XLA Ops:
  7.2 117.6 %copy-start = (bf16[1024,1024]{1,0:T(8,128)(2,1)S(1)}, bf16[1024,1024]{1,0:T(8,128)(2,1)}, u32[]{:S(2)}) copy-start(bf16[1024,1024]{1,0:T(8,128)(2,1)} %param.21) | copy-start | bytes 6291460
  7.2 53.7 %all-gather.3.cloned.1.call-start = ((), (), s32[]{:S(2)}) async-start(), calls=%async_computation.5 | async-start | bytes 2621440 | tf_op jit(solution)/shard_map/all_gather | solution.py:126
  12.1 95.6 %all-gather.5.cloned.1.call-start = ((), (), s32[]{:S(2)}) async-start(), calls=%async_computation.7 | async-start | bytes 2621440 | tf_op jit(solution)/shard_map/all_gather | solution.py:152
  33.4 74.3 %copy-start.35 = (f32[1024]{0:T(1024)S(1)}, f32[1024]{0:T(1024)}, u32[]{:S(2)}) copy-start(f32[1024]{0:T(1024)} %param.20) | copy-start | bytes 12292
  33.4 210.9 %reduce-scatter.14.cloned.1.call-start = ((), (), s32[]{:S(2)}) async-start(), calls=%async_computation.12 | async-start | bytes 2359296 | tf_op jit(solution)/shard_map/reduce_scatter | solution.py:207
  67.4 47.6 %copy-start.6 = (bf16[256,1024]{1,0:T(8,128)(2,1)S(1)}, bf16[256,1024]{1,0:T(8,128)(2,1)}, u32[]{:S(2)}) copy-start(bf16[256,1024]{1,0:T(8,128)(2,1)} %get-tuple-element.52) | copy-start | bytes 1572868
  114.4 3.7 copy-start.19
  114.4 132.0 %reduce-scatter.12.cloned.1.call-start = ((), (), s32[]{:S(2)}) async-start(), calls=%async_computation.11 | async-start | bytes 2359296 | tf_op jit(solution)/shard_map/reduce_scatter | solution.py:204
  118.1 6.6 %copy-start.34 = (bf16[1024,1024]{1,0:T(8,128)(2,1)S(1)}, bf16[1024,1024]{1,0:T(8,128)(2,1)}, u32[]{:S(2)}) copy-start(bf16[1024,1024]{1,0:T(8,128)(2,1)} %all-gather.5.cloned.1.call-done) | copy-start | bytes 6291460
  118.1 6.6 %copy-start.36 = (f32[1024,1024]{1,0:T(8,128)S(1)}, f32[1024,1024]{1,0:T(8,128)}, u32[]{:S(2)}) copy-start(f32[1024,1024]{1,0:T(8,128)} %fusion.48) | copy-start | bytes 12582916
  124.7 6.5 %copy-start.33 = (bf16[1024,1024]{1,0:T(8,128)(2,1)S(1)}, bf16[1024,1024]{1,0:T(8,128)(2,1)}, u32[]{:S(2)}) copy-start(bf16[1024,1024]{1,0:T(8,128)(2,1)} %all-gather.3.cloned.1.call-done) | copy-start | bytes 6291460
  129.9 1.3 copy-start.37
  135.0 5.5 %copy-start.23 = (bf16[256,1024]{1,0:T(8,128)(2,1)S(1)}, bf16[256,1024]{1,0:T(8,128)(2,1)}, u32[]{:S(2)}) copy-start(bf16[256,1024]{1,0:T(8,128)(2,1)} %convolution_convert_fusion.6) | copy-start | bytes 1572868
  135.0 113.2 %reduce-scatter.8.cloned.1.call-start = ((), (), s32[]{:S(2)}) async-start(), calls=%async_computation.8 | async-start | bytes 2621440 | tf_op jit(solution)/shard_map/reduce_scatter | solution.py:160
  156.7 13.7 %copy-start.29 = (s32[1,16]{1,0:T(1,128)S(1)}, s32[1,16]{1,0:T(1,128)}, u32[]{:S(2)}) copy-start(s32[1,16]{1,0:T(1,128)} %param.23) | copy-start | bytes 196
  156.7 13.8 %copy-start.30 = (s32[1,4]{1,0:T(1,128)S(1)}, s32[1,4]{1,0:T(1,128)}, u32[]{:S(2)}) copy-start(s32[1,4]{1,0:T(1,128)} %param.25) | copy-start | bytes 52
  156.7 13.8 %copy-start.31 = (s32[1,4]{1,0:T(1,128)S(1)}, s32[1,4]{1,0:T(1,128)}, u32[]{:S(2)}) copy-start(s32[1,4]{1,0:T(1,128)} %param.24) | copy-start | bytes 52
  173.3 0.8 copy-start.9
  173.3 1.6 copy-start.11
  174.1 3.5 copy-start.32
  174.1 3.5 copy-start.38
  174.9 1.9 copy-start.1
  177.6 4.0 copy-start.8
  177.7 4.0 copy-start.17
  181.4 138.2 %reduce-scatter.10.cloned.1.call-start = ((), (), s32[]{:S(2)}) async-start(), calls=%async_computation.9 | async-start | bytes 9437184 | tf_op jit(solution)/shard_map/reduce_scatter | solution.py:201
  181.7 3.6 copy-start.2
  185.4 2.5 copy-start.12
  186.5 1.3 copy-start.4
  189.6 11.9 %copy-start.10 = (bf16[256,16,64]{0,2,1:T(8,128)(2,1)S(1)}, bf16[256,16,64]{0,2,1:T(8,128)(2,1)}, u32[]{:S(2)}) copy-start(bf16[256,16,64]{0,2,1:T(8,128)(2,1)} %copy-done.9) | copy-start | bytes 1572868
  205.2 11.8 %copy-start.18 = (bf16[256,1024]{0,1:T(8,128)(2,1)S(1)}, bf16[256,1024]{0,1:T(8,128)(2,1)}, u32[]{:S(2)}) copy-start(bf16[256,1024]{0,1:T(8,128)(2,1)} %copy.49) | copy-start | bytes 1572868
  217.0 3.5 copy-start.7
  217.0 5.6 %copy-start.13 = (f32[256,16,64]{0,2,1:T(8,128)S(1)}, f32[256,16,64]{0,2,1:T(8,128)}, u32[]{:S(2)}) copy-start(f32[256,16,64]{0,2,1:T(8,128)} %reshape.253) | copy-start | bytes 3145732
  217.0 5.6 %copy-start.14 = (f32[256,16,64]{0,2,1:T(8,128)S(1)}, f32[256,16,64]{0,2,1:T(8,128)}, u32[]{:S(2)}) copy-start(f32[256,16,64]{0,2,1:T(8,128)} %reshape.256) | copy-start | bytes 3145732
  217.0 5.6 %copy-start.15 = (f32[256,16,64]{0,2,1:T(8,128)S(1)}, f32[256,16,64]{0,2,1:T(8,128)}, u32[]{:S(2)}) copy-start(f32[256,16,64]{0,2,1:T(8,128)} %get-tuple-element.71) | copy-start | bytes 3145732
  217.0 5.6 %copy-start.16 = (f32[256,16,64]{0,2,1:T(8,128)S(1)}, f32[256,16,64]{0,2,1:T(8,128)}, u32[]{:S(2)}) copy-start(f32[256,16,64]{0,2,1:T(8,128)} %get-tuple-element.69) | copy-start | bytes 3145732
  220.4 2.1 copy-start.21
  220.4 3.2 copy-start.3
  222.6 2.7 copy-start.20
  223.7 0.8 copy-start.24
  223.7 1.0 copy-start.25
  224.5 0.8 copy-start.26
  237.5 128.3 %reduce-scatter.6.cloned.1.call-start = ((), (), s32[]{:S(2)}) async-start(), calls=%async_computation.6 | async-start | bytes 2621440 | tf_op jit(solution)/shard_map/reduce_scatter | solution.py:131
  244.2 4.0 copy-start.5
  244.2 4.0 copy-start.27
  244.3 175.2 %all-reduce.3.cloned.1.call-start = ((), (), s32[]{:S(2)}) async-start(), calls=%async_computation.10 | async-start | bytes 2097152 | tf_op jit(solution)/shard_map/psum | solution.py:212
  254.5 111.3 %copy-start.22 = (bf16[16,64,256]{2,1,0:T(8,128)(2,1)S(1)}, bf16[16,64,256]{2,1,0:T(8,128)(2,1)}, u32[]{:S(2)}) copy-start(bf16[16,64,256]{2,1,0:T(8,128)(2,1)} %copy-done.21) | copy-start | bytes 1572868
  254.5 111.3 %copy-start.28 = (f32[1024]{0:T(1024)S(1)}, f32[1024]{0:T(1024)}, u32[]{:S(2)}) copy-start(f32[1024]{0:T(1024)} %param.22) | copy-start | bytes 12292
Sparse Core Ops, SparseCore 0:
  12.2 48.6 all-gather.2
  63.0 44.6 all-gather.4
  114.5 39.9 reduce-scatter.13
  158.0 41.2 reduce-scatter.11
  201.4 43.8 reduce-scatter.7
  249.0 70.6 reduce-scatter.9
  321.9 43.8 reduce-scatter.5
  368.3 51.1 all-reduce.2
where the time goes:
time: 437 us; the launch traced here: 431 us
  waiting for transfers between devices  192 us (44%)
  matrix products  72.4 us (17%)
  local copies, waits for them, and re-layouts  72.1 us (16%)
  blocking collectives  50.1 us (11%)
  other arithmetic  26.9 us (6%)
  between operations  16.2 us (4%)
    psum x1, waiting for transfers between devices, local(): lax.psum(attention_piece.astype(jnp.bfloat16), 'mp').astype(jnp.float32)  50.4 us
    reduce_scatter x1, waiting for transfers between devices, local(): lax.psum_scatter(jnp.dot(row_slice, shrink_weight, preferred_element_type...  42.8 us
    all_gather x1, waiting for transfers between devices, local(): gathered_grad = lax.all_gather(branch_grad, 'mp', axis=0, tiled=True)  40.3 us
    reduce_scatter x1, waiting for transfers between devices, local(): lax.psum_scatter(attention_mats.astype(jnp.bfloat16), 'dp', scatter_dimen...  30.6 us
    all_gather x1, waiting for transfers between devices, local(): gathered = lax.all_gather(normalized_reduced, 'mp', axis=0, tiled=True)  27.4 us
    psum x1, blocking collectives, local(): lax.psum((small_local, expand_bias_grad), 'dp')  24.8 us
    rev x4, local copies, waits for them, and re-layouts, pair_swap(): values.reshape(shape[0], shape[1], shape[2] // 2, 2)[..., ::-1]  24.2 us
    dot_general x4, matrix products, contract_cols(): lax.dot_general(left, right, (((1,), (1,)), ((), ())), preferred_element_...  18.3 us
  transfers between devices with their start and end apart: 8, of which 5 were waited for; matrix products, arithmetic and copies ran while one was open for 35% of the time, Pallas kernels for 0%

commit v1 on v0

v1 whole, which is shorter than its diff:
```python
from functools import partial

import numpy as np

import jax
import jax.numpy as jnp
from jax import lax
from jax.experimental import pallas as pl
from jax.experimental.pallas import tpu as pltpu
from jax.sharding import PartitionSpec as P

HEADS = 16
HEAD_DIM = 64
ROT = 32
SEQ_DEV = 4
EPSILON = 1e-05
NEGATIVE = -1e30
LANES = 256
BF = jnp.bfloat16
F32 = jnp.float32
MIB = 1 << 20

CORE, CHIP, ZPOS, LIVE, COUNT, LENS, TERMS, OFFS = 0, 1, 2, 3, 4, 5, 9, 13


def nn(a, b):
    return lax.dot_general(a, b, (((1,), (0,)), ((), ())), preferred_element_type=F32)


def nt(a, b):
    return lax.dot_general(a, b, (((1,), (1,)), ((), ())), preferred_element_type=F32)


def call(kernel, meta, args, in_specs, outs, out_specs, scratch=(), grid=(1,), vmem=40, flops=0):
    moved = sum(int(np.prod(a.shape)) * a.dtype.itemsize for a in (*args, *jax.tree.leaves(outs)))
    return pl.pallas_call(
        kernel,
        grid_spec=pltpu.PrefetchScalarGridSpec(
            num_scalar_prefetch=1,
            grid=grid,
            in_specs=in_specs,
            out_specs=out_specs,
            scratch_shapes=list(scratch),
        ),
        out_shape=outs,
        compiler_params=pltpu.CompilerParams(vmem_limit_bytes=vmem * MIB),
        cost_estimate=pl.CostEstimate(flops=flops, bytes_accessed=moved, transcendentals=0),
    )(meta, *args)


def whole(shape):
    return pl.BlockSpec(shape, lambda i, meta: (0,) * len(shape))


ANY = pl.BlockSpec(memory_space=pl.ANY)


def struct(shape, dtype):
    return jax.ShapeDtypeStruct(shape, dtype)


def normalize(hidden):
    mean = jnp.mean(hidden, axis=-1, keepdims=True)
    removed = hidden - mean
    variance = jnp.mean(removed * removed, axis=-1, keepdims=True)
    inverse = lax.rsqrt(variance + EPSILON)
    return removed * inverse, inverse


def prepare_kernel(meta, x_ref, u_ref, gain_ref, bias_ref, tok_ref, sum_ref):
    rows, width = x_ref.shape
    step = 64
    live = meta[LIVE]
    count = meta[COUNT].astype(F32)
    total = jnp.zeros((1, width), F32)
    for r in range(0, rows, step):
        xhat, _ = normalize(x_ref[r : r + step, :].astype(F32))
        tok_ref[r : r + step, :] = (xhat * gain_ref[...] + bias_ref[...]).astype(BF)
        place = lax.broadcasted_iota(jnp.int32, (step, width), 0) + r
        grad = jnp.where(place < live, u_ref[r : r + step, :].astype(F32) * count, 0.0).astype(BF)
        tok_ref[rows + r : rows + r + step, :] = grad
        total = total + jnp.sum(grad.astype(F32), axis=0, keepdims=True)
    sum_ref[...] = total


def prepare(meta, x, u, gain, bias):
    rows, width = x.shape
    return call(
        prepare_kernel,
        meta,
        (x, u, gain, bias),
        [whole(x.shape), whole(x.shape), whole((1, width)), whole((1, width))],
        (struct((2 * rows, width), BF), struct((1, width), F32)),
        (whole((2 * rows, width)), whole((1, width))),
        vmem=16,
        flops=20 * rows * width,
    )


def slot_of(place, ends):
    index = jnp.zeros(place.shape, jnp.int32)
    for end in ends:
        index = index + (place >= end).astype(jnp.int32)
    return index


def attention_kernel(
    meta, tok_ref, freq_ref, wq_ref, wk_ref, wv_ref, wo_ref, out_ref, cos_ref, sin_ref, mask_ref
):
    rows = cos_ref.shape[0]
    lanes = cos_ref.shape[1]

    @pl.when(pl.program_id(0) == 0)
    def tables():
        ends, starts, end = [], [], 0
        for s in range(SEQ_DEV):
            starts.append(end)
            end = end + meta[LENS + s]
            ends.append(end)
        place = lax.broadcasted_iota(jnp.int32, (rows, lanes), 0)
        index = slot_of(place, ends)
        start = jnp.zeros(place.shape, jnp.int32)
        terminal = jnp.zeros(place.shape, jnp.int32)
        offset = jnp.zeros(place.shape, jnp.int32)
        for s in range(SEQ_DEV):
            here = index == s
            start = jnp.where(here, starts[s], start)
            terminal = jnp.where(here, meta[TERMS + s], terminal)
            offset = jnp.where(here, meta[OFFS + s], offset)
        local = place - start
        position = jnp.where(local <= terminal, offset + local, local - terminal - 1)
        angle = position.astype(F32) * freq_ref[...]
        parity = lax.broadcasted_iota(jnp.int32, (rows, lanes), 1) % 2
        sine = jnp.sin(angle)
        cos_ref[...] = jnp.cos(angle)
        sin_ref[...] = jnp.where(parity == 0, -sine, sine)
        key = lax.broadcasted_iota(jnp.int32, (rows, rows), 0)
        query = lax.broadcasted_iota(jnp.int32, (rows, rows), 1)
        allowed = (slot_of(key, ends) == slot_of(query, ends)) & (key <= query)
        mask_ref[...] = jnp.where(allowed, 0.0, NEGATIVE)

    even = lax.broadcasted_iota(jnp.int32, (rows, lanes), 1) % 2 == 0

    def swap(v):
        return jnp.where(even, pltpu.roll(v, lanes - 1, 1), pltpu.roll(v, 1, 1))

    def turn(v):
        return v * cos_ref[...] + swap(v) * sin_ref[...]

    def turn_back(v):
        return v * cos_ref[...] - swap(v) * sin_ref[...]

    scale = HEAD_DIM ** (-0.5)
    normed = tok_ref[:rows, :]
    queries = (turn(nn(normed, wq_ref[...])) * scale).astype(BF)
    keys = turn(nn(normed, wk_ref[...])).astype(BF)
    values = nn(normed, wv_ref[...]).astype(BF)
    grads = nt(tok_ref[rows:, :], wo_ref[...]).astype(BF)
    keys_t = keys.T
    values_t = values.T
    pair = 2 * HEAD_DIM
    lane = lax.broadcasted_iota(jnp.int32, (rows, pair), 1)
    attended_t, query_grad_t, key_grads, value_grads = [], [], [], []
    for p in range(lanes // pair):
        cols = slice(p * pair, (p + 1) * pair)
        q2, k2, v2, g2 = queries[:, cols], keys[:, cols], values[:, cols], grads[:, cols]
        key_grad = jnp.zeros((rows, pair), F32)
        value_grad = jnp.zeros((rows, pair), F32)
        for h in range(2):
            mine = (lane >= h * HEAD_DIM) & (lane < (h + 1) * HEAD_DIM)
            qh = jnp.where(mine, q2, jnp.zeros_like(q2))
            gh = jnp.where(mine, g2, jnp.zeros_like(g2))
            head = slice(p * pair + h * HEAD_DIM, p * pair + (h + 1) * HEAD_DIM)
            scores = nt(k2, qh) + mask_ref[...]
            exponent = jnp.exp(scores - jnp.max(scores, axis=0, keepdims=True))
            probs = exponent / jnp.sum(exponent, axis=0, keepdims=True)
            probs_low = probs.astype(BF)
            attended_t.append(nn(values_t[head, :], probs_low))
            probs_grad = nt(v2, gh)
            row_dot = jnp.sum(probs * probs_grad, axis=0, keepdims=True)
            scores_grad = (probs * (probs_grad - row_dot)).astype(BF)
            query_grad_t.append(nn(keys_t[head, :], scores_grad))
            key_grad = key_grad + nn(scores_grad, qh)
            value_grad = value_grad + nn(probs_low, gh)
        key_grads.append(key_grad)
        value_grads.append(value_grad)
    out_ref[0] = jnp.concatenate(attended_t, axis=0).T.astype(BF)
    out_ref[1] = turn_back(jnp.concatenate(query_grad_t, axis=0).T * scale).astype(BF)
    out_ref[2] = turn_back(jnp.concatenate(key_grads, axis=1)).astype(BF)
    out_ref[3] = jnp.concatenate(value_grads, axis=1).astype(BF)


def attention(meta, tok, attend_weight, output_weight):
    rows, width = tok.shape[0] // 2, tok.shape[1]
    blocks = width // LANES
    pair = np.arange(LANES) % HEAD_DIM // 2
    freq = np.where(pair < ROT // 2, 10000.0 ** (-2.0 * pair / ROT), 0.0)[None].astype(np.float32)
    column = lambda p: pl.BlockSpec((width, LANES), lambda i, meta: (0, p * blocks + i))
    return call(
        attention_kernel,
        meta,
        (tok, jnp.asarray(freq), attend_weight, attend_weight, attend_weight, output_weight),
        [
            whole(tok.shape),
            whole((1, LANES)),
            column(0),
            column(1),
            column(2),
            pl.BlockSpec((LANES, width), lambda i, meta: (i, 0)),
        ],
        struct((4, rows, width), BF),
        pl.BlockSpec((4, rows, LANES), lambda i, meta: (0, 0, i)),
        scratch=[
            pltpu.VMEM((rows, LANES), F32),
            pltpu.VMEM((rows, LANES), F32),
            pltpu.VMEM((rows, rows), F32),
        ],
        grid=(blocks,),
        flops=2 * rows * width * (4 * width + 7 * rows * 4),
    )


def attention_back_kernel(meta, sb_ref, wa_ref, wo_ref, grad_ref, out_ref):
    width = sb_ref.shape[2]
    grad = nt(sb_ref[1], wa_ref[:, :width])
    grad = grad + nt(sb_ref[2], wa_ref[:, width : 2 * width])
    grad_ref[...] = grad + nt(sb_ref[3], wa_ref[:, 2 * width :])
    out_ref[...] = nn(sb_ref[0], wo_ref[...])


def attention_back(meta, sb, attend_weight, output_weight):
    _, rows, width = sb.shape
    block = pl.BlockSpec((rows, LANES), lambda i, meta: (0, i))
    return call(
        attention_back_kernel,
        meta,
        (sb, attend_weight, output_weight),
        [
            whole(sb.shape),
            pl.BlockSpec((LANES, 3 * width), lambda i, meta: (i, 0)),
            pl.BlockSpec((width, LANES), lambda i, meta: (0, i)),
        ],
        (struct((rows, width), F32), struct((rows, width), F32)),
        (block, block),
        grid=(width // LANES,),
        flops=8 * rows * width * width,
    )


def with_bit(n, bit):
    return [j for j in range(n) if j >> bit & 1]


def without_bit(n, bit):
    return [j for j in range(n) if not j >> bit & 1]


def attention_grads_kernel(chips, depth, meta, t0, t1, s0, s1, ps, pk, qs, qk, ln, la, acc, sem):
    rows, width = s0.shape[1:]
    chunk = width // chips
    half = chunk // 2
    cols = 4 * width // depth
    core = meta[CORE]
    for s, (tok, sb) in enumerate(((t0, s0), (t1, s1))):
        for k in range(chips):
            for ref, dst in ((tok, ln), (sb.at[0], la)):
                if half % 128 == 0:
                    start = pl.multiple_of(k * chunk + core * half, 128)
                    piece = ref[0:rows, pl.ds(start, half)]
                else:
                    both = ref[0:rows, k * chunk : (k + 1) * chunk].astype(F32)
                    piece = jnp.where(core == 0, both[:, :half], both[:, half:]).astype(BF)
                dst[k * half : (k + 1) * half, s * rows : (s + 1) * rows] = piece.T
    for a in range(depth):
        part, off = a * cols // width, a * cols % width
        span = slice(off, off + cols)
        if part < 3:
            left, right0, right1 = ln, s0[1 + part, :, span], s1[1 + part, :, span]
        else:
            left, right0, right1 = la, t0[rows:, span], t1[rows:, span]
        for k in range(chips):
            own = slice(k * half, (k + 1) * half)
            tile = nn(left[own, :rows], right0) + nn(left[own, rows:], right1)
            acc[meta[CHIP] ^ k, meta[ZPOS] ^ a] = tile.astype(BF)
    mid = depth // 2
    copies = []
    top = chips.bit_length() - 2
    for js, dst, zs in (
        (with_bit(chips, 0), ps, slice(0, mid)),
        (without_bit(chips, 0), pk, slice(0, mid)),
        (with_bit(chips, top), qs, slice(mid, depth)),
        (without_bit(chips, top), qk, slice(mid, depth)),
    ):
        for i, j in enumerate(js):
            copies.append(pltpu.make_async_copy(acc.at[j, zs], dst.at[i], sem.at[len(copies)]))
    for copy in copies:
        copy.start()
    for copy in copies:
        copy.wait()


def attention_grads(meta, chips, depth, t0, t1, s0, s1):
    _, rows, width = s0.shape
    half = width // chips // 2
    cols = 4 * width // depth
    piece = struct((chips // 2, depth // 2, half, cols), BF)
    return call(
        partial(attention_grads_kernel, chips, depth),
        meta,
        (t0, t1, s0, s1),
        [whole(t0.shape), whole(t0.shape), whole(s0.shape), whole(s0.shape)],
        (piece,) * 4,
        (ANY,) * 4,
        scratch=[
            pltpu.VMEM((chips * half, 2 * rows), BF),
            pltpu.VMEM((chips * half, 2 * rows), BF),
            pltpu.VMEM((chips, depth, half, cols), BF),
            pltpu.SemaphoreType.DMA((2 * chips,)),
        ],
        flops=2 * 2 * rows * chips * half * 4 * width,
    )


def load_pieces(meta, pieces, wet, ws, sem):
    size = ws.shape[0] // len(pieces)
    copies = []
    for j, piece in enumerate(pieces):
        start = pl.multiple_of((meta[CHIP] ^ j) * size, 16)
        for m, dst in enumerate((wet, ws)):
            copies.append(
                pltpu.make_async_copy(
                    piece.at[pl.ds(m * size, size)], dst.at[pl.ds(start, size)], sem.at[2 * j + m]
                )
            )
    for copy in copies:
        copy.start()
    return copies


def feed_kernel(chips, foreign, meta, *refs):
    toks, refs = refs[:4], refs[4:]
    if foreign:
        pieces, bias_ref, refs = refs[:chips], refs[chips], refs[chips + 1 :]
    else:
        (we, ws, bias_ref), refs = refs[:3], refs[3:]
    act_ref, eg_ref, bias_out, ps, pk, qs, qk = refs[:7]
    x, bg, act_t, eg_t, gx, gs, sem_in, sem_out = refs[7:15]
    rows = toks[0].shape[0] // 2
    width = x.shape[1]
    hidden = act_t.shape[0]
    loads = []
    for r, tok in enumerate(toks):
        for m, dst in enumerate((x, bg)):
            loads.append(
                pltpu.make_async_copy(
                    tok.at[pl.ds(m * rows, rows)],
                    dst.at[pl.ds(r * rows, rows)],
                    sem_in.at[2 * r + m],
                )
            )
    for copy in loads:
        copy.start()
    if foreign:
        we, ws, sem_w = refs[15:18]
        for copy in load_pieces(meta, pieces, we, ws, sem_w):
            copy.wait()
    step = min(256, hidden)
    for r in range(4):
        loads[2 * r].wait()
        loads[2 * r + 1].wait()
        here = slice(r * rows, (r + 1) * rows)
        for h in range(0, hidden, step):
            block = slice(h, h + step)
            if foreign:
                v = nt(x[here, :], we[block, :])
            else:
                v = nn(x[here, :], we[:, block])
            v = v + bias_ref[:, block]
            square = v * v
            t = jnp.tanh(0.7978845608 * v * (1.0 + 0.044715 * square))
            low = 0.5 * (1.0 + t)
            slope = low + 0.5 * v * (1.0 - t * t) * (0.7978845608 * (1.0 + 0.134145 * square))
            act = (v * low).astype(BF)
            eg = (nt(bg[here, :], ws[block, :]) * slope).astype(BF)
            act_ref[here, block] = act
            eg_ref[here, block] = eg
            act_t[block, here] = act.T
            eg_t[block, here] = eg.T
            total = jnp.sum(eg.astype(F32), axis=0, keepdims=True)
            if r == 0:
                bias_out[:, block] = total
            else:
                bias_out[:, block] = bias_out[:, block] + total
    chunk = width // chips
    half = chunk // 2
    core = meta[CORE]
    for k in range(chips):
        span = slice(k * chunk, (k + 1) * chunk)
        for left, right, dst in ((eg_t, x, gx), (act_t, bg, gs)):
            tile = nn(left[...], right[:, span]).astype(BF)
            for a in range(2):
                dst[meta[CHIP] ^ k, core ^ a] = tile[:, a * half : (a + 1) * half]
    top = chips.bit_length() - 2
    copies = []
    for js, src, dst in (
        (with_bit(chips, 0), gx, ps),
        (without_bit(chips, 0), gx, pk),
        (with_bit(chips, top), gs, qs),
        (without_bit(chips, top), gs, qk),
    ):
        for i, j in enumerate(js):
            copies.append(pltpu.make_async_copy(src.at[j], dst.at[i], sem_out.at[len(copies)]))
    for copy in copies:
        copy.start()
    for copy in copies:
        copy.wait()


def feed(meta, chips, toks, weights, bias, foreign):
    rows, width = toks[0].shape[0] // 2, toks[0].shape[1]
    hidden = bias.shape[1] if foreign else bias.shape[1] // 2
    half = width // chips // 2
    if foreign:
        weight_specs = [ANY] * chips
        bias_spec = whole((1, hidden))
    else:
        weight_specs = [
            pl.BlockSpec((width, hidden), lambda i, meta: (0, meta[CORE])),
            pl.BlockSpec((hidden, width), lambda i, meta: (meta[CORE], 0)),
        ]
        bias_spec = pl.BlockSpec((1, hidden), lambda i, meta: (0, meta[CORE]))
    piece = struct((chips // 2, 2, hidden, half), BF)
    scratch = [
        pltpu.VMEM((4 * rows, width), BF),
        pltpu.VMEM((4 * rows, width), BF),
        pltpu.VMEM((hidden, 4 * rows), BF),
        pltpu.VMEM((hidden, 4 * rows), BF),
        pltpu.VMEM((chips, 2, hidden, half), BF),
        pltpu.VMEM((chips, 2, hidden, half), BF),
        pltpu.SemaphoreType.DMA((8,)),
        pltpu.SemaphoreType.DMA((2 * chips,)),
    ]
    if foreign:
        scratch += [
            pltpu.VMEM((hidden, width), BF),
            pltpu.VMEM((hidden, width), BF),
            pltpu.SemaphoreType.DMA((2 * chips,)),
        ]
    return call(
        partial(feed_kernel, chips, foreign),
        meta,
        (*toks, *weights, bias),
        [ANY] * 4 + weight_specs + [bias_spec],
        (struct((4 * rows, hidden), BF),) * 2 + (struct((1, hidden), F32),) + (piece,) * 4,
        (whole((4 * rows, hidden)),) * 2 + (whole((1, hidden)),) + (ANY,) * 4,
        scratch=scratch,
        flops=8 * 4 * rows * width * hidden,
    )


def feed_out_kernel(chips, shards, meta, *refs):
    we, ws, act0, eg0 = refs[:4]
    refs = refs[4:]
    others = []
    for _ in range(shards - 1):
        others.append((refs[0], refs[1], refs[2 : 2 + chips]))
        refs = refs[2 + chips :]
    keep, send = refs[:2]
    refs = refs[2:]
    rows = keep.shape[2]
    copies = []
    for n, (_, _, pieces) in enumerate(others):
        copies += load_pieces(meta, pieces, *refs[3 * n : 3 * n + 3])
    for n, copy in enumerate(copies):
        copy.wait()
    for r in (1, 3, 0, 2):
        here = slice(r * rows, (r + 1) * rows)
        dst = send if r % 2 else keep
        grad = nt(eg0[here, :], we[...])
        for n, (_, eg, _) in enumerate(others):
            grad = grad + nn(eg[here, :], refs[3 * n][...])
        dst[0, r // 2] = grad.astype(BF)
        out = nn(act0[here, :], ws[...])
        for n, (act, _, _) in enumerate(others):
            out = out + nn(act[here, :], refs[3 * n + 1][...])
        dst[1, r // 2] = out.astype(BF)


def feed_out(meta, chips, we, ws, own, others):
    hidden, (width, rows4) = own[0].shape[1], (we.shape[0], own[0].shape[0])
    args = [we, ws, *own]
    specs = [
        pl.BlockSpec((width, hidden), lambda i, meta: (0, meta[CORE])),
        pl.BlockSpec((hidden, width), lambda i, meta: (meta[CORE], 0)),
        whole(own[0].shape),
        whole(own[0].shape),
    ]
    scratch = []
    for act, eg, pieces in others:
        args += [act, eg, *pieces]
        specs += [whole(act.shape), whole(act.shape)] + [ANY] * chips
        scratch += [
            pltpu.VMEM((hidden, width), BF),
            pltpu.VMEM((hidden, width), BF),
            pltpu.SemaphoreType.DMA((2 * chips,)),
        ]
    result = struct((2, 2, rows4 // 4, width), BF)
    return call(
        partial(feed_out_kernel, chips, 1 + len(others)),
        meta,
        tuple(args),
        specs,
        (result, result),
        (whole(result.shape), whole(result.shape)),
        scratch=scratch,
        flops=4 * rows4 * width * hidden * (1 + len(others)),
    )


def norm_back_kernel(meta, x_ref, u_ref, gain_ref, g0, g1, g2, g3, out_ref, gain_out, shift_out):
    rows, width = x_ref.shape
    step = 64
    count = meta[COUNT].astype(F32)
    gain_sum = jnp.zeros((1, width), F32)
    shift_sum = jnp.zeros((1, width), F32)
    for r in range(0, rows, step):
        here = slice(r, r + step)
        xhat, inverse = normalize(x_ref[here, :].astype(F32))
        grad = g0[here, :] + g1[0, 0, here, :].astype(F32) + g2[0, 0, here, :].astype(F32)
        grad = grad + g3[0, here, :].astype(F32)
        gain_sum = gain_sum + jnp.sum(grad * xhat, axis=0, keepdims=True)
        shift_sum = shift_sum + jnp.sum(grad, axis=0, keepdims=True)
        scaled = grad * gain_ref[...]
        mean = jnp.mean(scaled, axis=-1, keepdims=True)
        dot = jnp.mean(scaled * xhat, axis=-1, keepdims=True)
        out_ref[here, :] = u_ref[here, :].astype(F32) * count + inverse * (
            scaled - mean - xhat * dot
        )
    gain_out[...] = gain_sum
    shift_out[...] = shift_sum


def norm_back(meta, x, u, gain, g0, g1, g2, g3):
    rows, width = x.shape
    first = pl.BlockSpec((1, 1, rows, width), lambda i, meta: (0, 0, 0, 0))
    return call(
        norm_back_kernel,
        meta,
        (x, u, gain, g0, g1, g2, g3),
        [
            whole(x.shape),
            whole(x.shape),
            whole((1, width)),
            whole(x.shape),
            first,
            first,
            pl.BlockSpec((1, rows, width), lambda i, meta: (0, 0, 0)),
        ],
        (struct((rows, width), F32), struct((1, width), F32), struct((1, width), F32)),
        (whole(x.shape), whole((1, width)), whole((1, width))),
        vmem=24,
        flops=30 * rows * width,
    )


def exchange(x, axis, flip):
    n = lax.axis_size(axis)
    return lax.ppermute(x, axis, [(i, i ^ flip) for i in range(n)])


def split_bit(x, ascending):
    if ascending:
        return x[0::2], x[1::2]
    middle = x.shape[0] // 2
    return x[:middle], x[middle:]


def reduce_chips(send, keep, bits):
    ascending = len(bits) < 2 or bits[0] < bits[1]
    stays = [keep.astype(F32), exchange(send, "dp", 2 << bits[0]).astype(F32)]
    for bit in bits[1:]:
        halves = [split_bit(s, ascending) for s in stays]
        send = sum(h[1] for h in halves).astype(BF)
        stays = [h[0] for h in halves] + [exchange(send, "dp", 2 << bit).astype(F32)]
    return sum(stays)[0]


def local(
    residual_in,
    upstream,
    layer_norm_gain,
    layer_norm_bias,
    attend_weight,
    output_weight,
    expand_weight,
    expand_bias,
    shrink_weight,
    shrink_bias,
    seq_lengths,
    terminal_pos,
    window_offset,
):
    rows, width = residual_in.shape
    data_ways, depth = lax.axis_size("dp"), lax.axis_size("mp")
    chips = data_ways // 2
    shards = depth // 2
    shard = expand_weight.shape[1]
    hidden = shard // 2
    share = hidden // chips
    half = width // data_ways
    up = list(range(chips.bit_length() - 1))
    down = up[::-1]

    place, zpos = lax.axis_index("dp"), lax.axis_index("mp")
    core, chip = place & 1, place >> 1
    lengths = lax.dynamic_slice_in_dim(seq_lengths[0], zpos * SEQ_DEV, SEQ_DEV)
    head = jnp.stack([core, chip, zpos, jnp.sum(lengths), jnp.sum(seq_lengths[0])])
    meta = jnp.concatenate(
        [head.astype(jnp.int32), lengths, terminal_pos[0], window_offset[0]]
    ).astype(jnp.int32)
    gain = layer_norm_gain[None, :]

    start = core * hidden + chip * share
    bias_half = lax.dynamic_slice_in_dim(expand_bias, core * hidden, hidden)
    high = lax.reduce_precision(bias_half, 8, 7)
    middle = lax.reduce_precision(bias_half - high, 8, 7)
    lowest = bias_half - high - middle
    bias_rows = jnp.pad(
        jnp.stack([high, middle, lowest]).astype(BF), ((0, 13), (0, width - hidden))
    )
    packed = jnp.concatenate(
        [
            lax.dynamic_slice_in_dim(expand_weight, start, share, axis=1).T,
            lax.dynamic_slice_in_dim(shrink_weight, start, share, axis=0),
            bias_rows,
        ]
    )
    shares = [exchange(packed, "mp", 2 * k) for k in range(1, shards)]

    tok, shrink_bias_grad = prepare(meta, residual_in, upstream, gain, layer_norm_bias[None, :])
    tok_core = exchange(tok, "dp", 1)
    tok_deep = exchange(tok, "mp", 1)
    tok_both = exchange(tok_deep, "dp", 1)
    toks = (tok, tok_core, tok_deep, tok_both)

    foreign = []
    for arrived in shares:
        pieces = [arrived] + [exchange(arrived, "dp", 2 * j) for j in range(1, chips)]
        parts = arrived[2 * share : 2 * share + 3, :hidden].astype(F32)
        foreign.append((pieces, (parts[0] + parts[1] + parts[2])[None, :]))

    sides = attention(meta, tok, attend_weight, output_weight)
    sides_core = exchange(sides, "dp", 1)
    attn = attention_grads(meta, chips, depth, tok, tok_core, sides, sides_core)
    attn_low = reduce_chips(attn[0], attn[1], up)
    attn_high = reduce_chips(attn[2], attn[3], down)
    attn_parts = [a[z] for a in (attn_low, attn_high) for z in range(depth // 2)]
    attn_own = attn_parts[0]
    for j in range(1, depth):
        attn_own = attn_own + exchange(attn_parts[j].astype(BF), "mp", j).astype(F32)
    attn_own = attn_own.astype(BF)
    attn_all = [attn_own] + [exchange(attn_own, "mp", j) for j in range(1, depth)]
    grad_attention, attention_out = attention_back(meta, sides, attend_weight, output_weight)

    own = feed(meta, chips, toks, (expand_weight, shrink_weight), expand_bias[None, :], False)
    others = [feed(meta, chips, toks, pieces, bias, True) for pieces, bias in foreign]
    keep, send = feed_out(
        meta,
        chips,
        expand_weight,
        shrink_weight,
        own[:2],
        [(o[0], o[1], pieces) for o, (pieces, _) in zip(others, foreign)],
    )
    passed = exchange(send, "dp", 1)
    crossing = (keep[:, 1].astype(F32) + passed[:, 1].astype(F32)).astype(BF)
    crossed_grad = exchange(crossing[0:1], "mp", 1)
    crossed_out = exchange(crossing[1:2], "mp", 1)

    sums = [
        (reduce_chips(f[3], f[4], up), reduce_chips(f[5], f[6], down)) for f in (*others, own)
    ]
    mlp = list(sums[-1])
    for k, pair in enumerate(sums[:-1]):
        both = exchange(jnp.stack(pair).astype(BF), "mp", 2 * (k + 1)).astype(F32)
        mlp = [mlp[0] + both[0], mlp[1] + both[1]]
    mlp = jnp.stack(mlp)
    mine = mlp[:, 0]
    sibling = exchange(mlp[:, 1].astype(BF), "dp", 1).astype(F32)

    grad_rows, gain_sum, shift_sum = norm_back(
        meta, residual_in, upstream, gain, grad_attention, keep, passed, crossed_grad
    )
    live = (jnp.arange(rows, dtype=jnp.int32) < meta[LIVE])[:, None]
    branch = attention_out + keep[1, 0].astype(F32) + passed[1, 0].astype(F32)
    branch = branch + crossed_out[0].astype(F32) + shrink_bias
    residual_out = (
        residual_in.astype(F32) + jnp.where(live, branch, 0.0)
    ).astype(BF)

    def half_row(v):
        row = jnp.concatenate([jnp.where(core == 0, v, 0.0), jnp.where(core == 1, v, 0.0)], axis=1)
        return jnp.pad(row, ((0, 0), (0, width - shard)))

    count_row = jnp.full((1, width), meta[COUNT].astype(F32))
    small = jnp.concatenate(
        [gain_sum, shift_sum, shrink_bias_grad, count_row, half_row(own[2])]
        + [half_row(o[2]) for o in others]
    )
    for bit in range(depth.bit_length() - 1):
        other = exchange(small, "mp", 1 << bit)
        rest = [small[4 + k] for k in range(shards)]
        if bit > 0:
            step = 1 << (bit - 1)
            rest = [
                r if k & step else r + other[4 + (k | step)] for k, r in enumerate(rest)
            ]
        small = jnp.concatenate([small[:4] + other[:4], jnp.stack(rest)])
    small = small[:5]
    for bit in range(data_ways.bit_length() - 1):
        small = small + exchange(small, "dp", 1 << bit)
    scale = (data_ways * depth) / small[3, 0]

    attn_stack = [a.astype(F32) for a in attn_all]
    parts = []
    for a in range(depth):
        part = attn_stack[0]
        for j in range(1, depth):
            part = jnp.where((zpos ^ a) == j, attn_stack[j], part)
        parts.append(part * scale)
    split = 3 * depth // 4
    attend_sum = jnp.concatenate(parts[:split], axis=1)
    output_sum = jnp.concatenate(parts[split:], axis=1)
    low = jnp.where(core == 0, mine, sibling)
    top = jnp.where(core == 0, sibling, mine)
    mlp_sum = jnp.concatenate([low, top], axis=1) * scale
    return (
        residual_out,
        grad_rows * scale,
        small[0] * scale,
        small[1] * scale,
        attend_sum,
        output_sum,
        mlp_sum[0].T,
        small[4, :shard] * scale,
        mlp_sum[1],
        small[2] * scale,
    )


def solution(mesh):
    in_specs = (
        P(("dp", "mp"), None),
        P(("dp", "mp"), None),
        P(),
        P(),
        P(),
        P(),
        P(None, "mp"),
        P("mp"),
        P("mp", None),
        P(),
        P("dp", None),
        P("dp", "mp"),
        P("dp", "mp"),
    )
    out_specs = (
        P(("dp", "mp"), None),
        P(("dp", "mp"), None),
        P(),
        P(),
        P("dp", None),
        P("dp", None),
        P("dp", "mp"),
        P("mp"),
        P("mp", "dp"),
        P(),
    )
    return jax.shard_map(local, mesh=mesh, in_specs=in_specs, out_specs=out_specs, check_vma=False)
```

time: 437 us -> 280 us (0.64)
  matrix products: 72.4 us -> 0 us
  waiting for transfers between devices: 192 us -> 122 us
  Pallas kernels: 0 us -> 56.3 us
  blocking collectives: 50.1 us -> 0 us
  local copies, waits for them, and re-layouts: 72.1 us -> 26.9 us
  starting transfers between devices: 1.49 us -> 41.8 us
  between operations: 16.2 us -> 2.67 us
    ppermute x0 -> x36, waiting for transfers between devices: none -> 122 us  [exchange(): return lax.ppermute(x, axis, [(i, i ^ flip) for i in range(n)])]
    reduce_scatter x5 -> x0, waiting for transfers between devices: 73.4 us -> none  [the longest x1 42.8 us: local(): lax.psum_scatter(jnp.dot(row_slice, shrink_weight, preferred_element_type...]
    dot_general x18 -> x0, matrix products: 72.4 us -> none  [the longest x4 18.3 us: contract_cols(): lax.dot_general(left, right, (((1,), (1,)), ((), ())), preferred_element_...]
    all_gather x2 -> x0, waiting for transfers between devices: 67.7 us -> none  [the longest x1 40.3 us: local(): gathered_grad = lax.all_gather(branch_grad, 'mp', axis=0, tiled=True)]
    pallas_call x0 -> x8, Pallas kernels: none -> 56.3 us  [call(): pl.pallas_call(kernel, grid_spec=pltpu.PrefetchScalarGridSpec(num_scalar_...]
    psum x1 -> x0, waiting for transfers between devices: 50.4 us -> none  [local(): lax.psum(attention_piece.astype(jnp.bfloat16), 'mp').astype(jnp.float32)]
    psum x3 -> x0, blocking collectives: 50.1 us -> none  [the longest x1 24.8 us: local(): lax.psum((small_local, expand_bias_grad), 'dp')]
    ppermute x0 -> x36, starting transfers between devices: none -> 41.8 us  [exchange(): return lax.ppermute(x, axis, [(i, i ^ flip) for i in range(n)])]
  transfers between devices with their start and end apart: 8 -> 36, of which waited for: 5 -> 16; matrix products, arithmetic and copies ran while one was open for 35% -> 11% of each run, Pallas kernels for 0% -> 13%
where the time goes in v1:
time: 280 us; the launch traced here: 278 us
  waiting for transfers between devices  122 us (44%)
  Pallas kernels  56.3 us (20%)
  starting transfers between devices  41.8 us (15%)
  other arithmetic  27.6 us (10%)
  local copies, waits for them, and re-layouts  26.9 us (10%)
    ppermute x36, waiting for transfers between devices, exchange(): return lax.ppermute(x, axis, [(i, i ^ flip) for i in range(n)])  122 us
    pallas_call x8, Pallas kernels, call(): pl.pallas_call(kernel, grid_spec=pltpu.PrefetchScalarGridSpec(num_scalar_...  56.3 us
    ppermute x36, starting transfers between devices, exchange(): return lax.ppermute(x, axis, [(i, i ^ flip) for i in range(n)])  41.8 us
    unnamed x72, local copies, waits for them, and re-layouts  19 us
    convert_element_type x12, other arithmetic, reduce_chips(): stays = [keep.astype(F32), exchange(send, 'dp', 2 << bits[0]).astype(F32)]  8.4 us
  transfers between devices with their start and end apart: 36, of which 16 were waited for; matrix products, arithmetic and copies ran while one was open for 11% of the time, Pallas kernels for 13%

profile of v1, /device:TPU:0, one launch (start us, length us, event | category | flops | bytes accessed | tf_op | source)
XLA Modules:
  0.0 277.5 jit_solution(13396583899392306179)
XLA Ops:
  1.9 1.4 fusion.43
  3.3 2.0 concatenate.30.meta
  10.0 2.8 %copy-done = bf16[1024,3072]{1,0:T(8,128)(2,1)S(1)} copy-done((bf16[1024,3072]{1,0:T(8,128)(2,1)S(1)}, bf16[1024,3072]{1,0:T(8,128)(2,1)}, u32[]{:S(2)}) %copy-start) | copy-done | bytes 6291480
  12.8 1.6 copy-done.2
  15.1 17.9 %shard_map.214.sb_ref.s0 = bf16[4,256,1024]{2,1,0:T(8,128)(2,1)} custom-call(s32[17]{0:T(128)S(1)} %concatenate.30.meta, bf16[512,1024]{1,0:T(8,128)(2,1)S(1)} %get-tuple-element.37.tok_ref.refs_0_.t0, f32[1,256]{1,0:T(1,128)S(1)} %copy-done.18, bf16[1024,3072]{1,0:T(8,128)(2,1)S(1)} %copy-done, bf16[1024,3072]{1,0:T(8,128)(2,1)S(1)} %copy-done, ...), custom_call_target="tpu_custom_call" | custom-call | flops 5905580032 | bytes 24118272 | tf_op jit(solution)/shard_map/pallas_call | solution.py:36
  33.4 2.6 collective-permute-start.1
  36.3 1.7 constant_dynamic-slice_fusion.1
  41.0 2.6 collective-permute-start.3
  43.5 28.3 %collective-permute-done.1.refs_2_ = bf16[512,1024]{1,0:T(8,128)(2,1)} collective-permute-done((bf16[512,1024]{1,0:T(8,128)(2,1)S(1)}, bf16[512,1024]{1,0:T(8,128)(2,1)}, u32[]{:S(2)}, u32[]{:S(2)}) %collective-permute-start.1) | collective-permute-done | bytes 1048608 | tf_op jit(solution)/shard_map/ppermute | solution.py:568
  73.2 2.8 %copy-done.1 = bf16[1024,3072]{1,0:T(8,128)(2,1)S(1)} copy-done((bf16[1024,3072]{1,0:T(8,128)(2,1)S(1)}, bf16[1024,3072]{1,0:T(8,128)(2,1)}, u32[]{:S(2)}) %copy-start.1) | copy-done | bytes 6291480
  76.0 5.5 %shard_map.215 = (f32[256,1024]{1,0:T(8,128)S(1)}, f32[256,1024]{1,0:T(8,128)S(1)}) custom-call(s32[17]{0:T(128)S(1)} %concatenate.30.meta, bf16[4,256,1024]{2,1,0:T(8,128)(2,1)} %shard_map.214.sb_ref.s0, bf16[1024,3072]{1,0:T(8,128)(2,1)S(1)} %copy-done.1, bf16[1024,1024]{1,0:T(8,128)(2,1)S(1)} %copy-done.3), custom_call_target="tpu_custom_call" | custom-call | flops 2147483648 | bytes 12582912 | tf_op jit(solution)/shard_map/pallas_call | solution.py:36
  82.5 2.6 collective-permute-start.6
  86.8 5.9 %shard_map.220 = (bf16[2,2,128,1024]{3,2,1,0:T(8,128)(2,1)S(1)}, bf16[2,2,128,1024]{3,2,1,0:T(8,128)(2,1)S(1)}, bf16[2,2,128,1024]{3,2,1,0:T(8,128)(2,1)S(1)}, bf16[2,2,128,1024]{3,2,1,0:T(8,128)(2,1)S(1)}) custom-call(s32[17]{0:T(128)S(1)} %concatenate.30.meta, bf16[512,1024]{1,0:T(8,128)(2,1)S(1)} %get-tuple-element.37.tok_ref.refs_0_.t0, ...), custom_call_target="tpu_custom_call" | custom-call | flops 2147483648 | bytes 10485760 | tf_op jit(solution)/shard_map/pallas_call | solution.py:36
  92.6 1.6 convert_element_type.177
  94.2 1.7 collective-permute-start.16
  95.9 3.2 %collective-permute-done.6.refs_7_.refs_9_ = bf16[272,1024]{1,0:T(8,128)(2,1)S(1)} collective-permute-done((bf16[272,1024]{1,0:T(8,128)(2,1)}, bf16[272,1024]{1,0:T(8,128)(2,1)S(1)}, u32[]{:S(2)}, u32[]{:S(2)}) %collective-permute-start.6) | collective-permute-done | bytes 557088 | tf_op jit(solution)/shard_map/ppermute | solution.py:568
  99.1 1.7 collective-permute-start.19
  100.8 9.9 %collective-permute-done.5.refs_6_.refs_8_ = bf16[272,1024]{1,0:T(8,128)(2,1)S(1)} collective-permute-done((bf16[272,1024]{1,0:T(8,128)(2,1)}, bf16[272,1024]{1,0:T(8,128)(2,1)S(1)}, u32[]{:S(2)}, u32[]{:S(2)}) %collective-permute-start.5) | collective-permute-done | bytes 557088 | tf_op jit(solution)/shard_map/ppermute | solution.py:568
  111.2 9.5 %shard_map.217 = (bf16[1024,512]{1,0:T(8,128)(2,1)S(1)}, bf16[1024,512]{1,0:T(8,128)(2,1)S(1)}, f32[1,512]{1,0:T(1,128)S(1)}, bf16[2,2,512,128]{3,2,1,0:T(8,128)...) custom-call(s32[17]{0:T(128)S(1)} %concatenate.30.meta, ...), custom_call_target="tpu_custom_call" | custom-call | flops 4294967296 | bytes 10620928 | tf_op jit(solution)/shard_map/pallas_call | solution.py:36
  122.7 1.5 collective-permute-start.28
  124.2 7.3 %shard_map.216 = (bf16[1024,512]{1,0:T(8,128)(2,1)S(1)}, bf16[1024,512]{1,0:T(8,128)(2,1)S(1)}, f32[1,512]{1,0:T(1,128)S(1)}, bf16[2,2,512,128]{3,2,1,0:T(8,128)...) custom-call(s32[17]{0:T(128)S(1)} %concatenate.30.meta, ...), custom_call_target="tpu_custom_call" | custom-call | flops 4294967296 | bytes 12589056 | tf_op jit(solution)/shard_map/pallas_call | solution.py:36
  135.5 7.4 %shard_map.218 = (bf16[2,2,256,1024]{3,2,1,0:T(8,128)(2,1)S(1)}, bf16[2,2,256,1024]{3,2,1,0:T(8,128)(2,1)S(1)}) custom-call(s32[17]{0:T(128)S(1)} %concatenate.30.meta, bf16[1024,1024]{1,0:T(8,128)(2,1)S(1)} %copy-done.13, bf16[1024,1024]{1,0:T(8,128)(2,1)} %refs_1_.1, bf16[1024,512]{1,0:T(8,128)(2,1)S(1)} %get-tuple-element.39.refs_2_, ...), custom_call_target="tpu_custom_call" | custom-call | flops 4294967296 | bytes 14811136 | tf_op jit(solution)/shard_map/pallas_call | solution.py:36
  142.9 2.1 collective-permute-done.28
  146.6 9.3 %collective-permute-done.26 = bf16[2,2,512,128]{3,2,1,0:T(8,128)(2,1)} collective-permute-done((bf16[2,2,512,128]{3,2,1,0:T(8,128)(2,1)S(1)}, bf16[2,2,512,128]{3,2,1,0:T(8,128)(2,1)}, u32[]{:S(2)}, u32[]{:S(2)}) %collective-permute-start.26) | collective-permute-done | bytes 524320 | tf_op jit(solution)/shard_map/ppermute | solution.py:568
  158.7 1.8 collective-permute-start.27
  160.6 5.6 %collective-permute-done.29 = bf16[1,2,512,128]{3,2,1,0:T(8,128)(2,1)S(1)} collective-permute-done((bf16[1,2,512,128]{3,2,1,0:T(8,128)(2,1)S(1)}, bf16[1,2,512,128]{3,2,1,0:T(8,128)(2,1)S(1)}, u32[]{:S(2)}, u32[]{:S(2)}) %collective-permute-start.29) | collective-permute-done | bytes 262176 | tf_op jit(solution)/shard_map/ppermute | solution.py:568
  166.2 1.5 collective-permute-start.31
  167.8 6.0 %collective-permute-done.31 = bf16[1,2,512,128]{3,2,1,0:T(8,128)(2,1)S(1)} collective-permute-done((bf16[1,2,512,128]{3,2,1,0:T(8,128)(2,1)S(1)}, bf16[1,2,512,128]{3,2,1,0:T(8,128)(2,1)S(1)}, u32[]{:S(2)}, u32[]{:S(2)}) %collective-permute-start.31) | collective-permute-done | bytes 262176 | tf_op jit(solution)/shard_map/ppermute | solution.py:568
  173.8 1.5 collective-permute-start.34
  175.4 1.6 collective-permute-start.32
  177.1 1.5 convert_element_type.178
  179.3 1.5 convert_element_type.184
  181.9 17.7 %collective-permute-done.32 = bf16[2,2,512,128]{3,2,1,0:T(8,128)(2,1)S(1)} collective-permute-done((bf16[2,2,512,128]{3,2,1,0:T(8,128)(2,1)S(1)}, bf16[2,2,512,128]{3,2,1,0:T(8,128)(2,1)S(1)}, u32[]{:S(2)}, u32[]{:S(2)}) %collective-permute-start.32) | collective-permute-done | bytes 524320 | tf_op jit(solution)/shard_map/ppermute | solution.py:568
  203.8 2.1 collective-permute-start.18
  205.8 11.6 %collective-permute-done.9.g3 = bf16[1,256,1024]{2,1,0:T(8,128)(2,1)S(1)} collective-permute-done((bf16[1,256,1024]{2,1,0:T(8,128)(2,1)S(1)}, bf16[1,256,1024]{2,1,0:T(8,128)(2,1)S(1)}, u32[]{:S(2)}, u32[]{:S(2)}) %collective-permute-start.9) | collective-permute-done | bytes 524320 | tf_op jit(solution)/shard_map/ppermute | solution.py:568
  217.5 1.6 shard_map.219
  220.3 2.0 fusion.2
  222.3 1.8 collective-permute-done.10
  225.4 1.9 collective-permute-start.21
  227.3 2.5 collective-permute-start.22
  229.8 9.1 %collective-permute-done.11 = f32[6,1024]{1,0:T(8,128)S(1)} collective-permute-done((f32[6,1024]{1,0:T(8,128)S(1)}, f32[6,1024]{1,0:T(8,128)S(1)}, u32[]{:S(2)}, u32[]{:S(2)}) %collective-permute-start.11) | collective-permute-done | bytes 24608 | tf_op jit(solution)/shard_map/ppermute | solution.py:568
  240.2 1.6 collective-permute-start.13
  241.8 4.5 %collective-permute-done.21 = bf16[128,1024]{1,0:T(8,128)(2,1)S(1)} collective-permute-done((bf16[128,1024]{1,0:T(8,128)(2,1)S(1)}, bf16[128,1024]{1,0:T(8,128)(2,1)S(1)}, u32[]{:S(2)}, u32[]{:S(2)}) %collective-permute-start.21) | collective-permute-done | bytes 262176 | tf_op jit(solution)/shard_map/ppermute | solution.py:568
  247.4 5.4 %collective-permute-start.25 = (bf16[128,1024]{1,0:T(8,128)(2,1)S(1)}, bf16[128,1024]{1,0:T(8,128)(2,1)S(1)}, u32[]{:S(2)}, u32[]{:S(2)}) collective-permute-start(bf16[128,1024]{1,0:T(8,128)(2,1)S(1)} %fusion.29), channel_id=1, source_target_pairs={{0,1},{1,0},{2,3},{3,2},{4,5},{5,4},{6,7},{7,6},{8,9},{9,8},{10,11... | collective-permute-start | bytes 786440 | tf_op jit(solution)/shard_map/ppermute | solution.py:568
  253.2 2.0 collective-permute-start.23
  255.8 2.4 fusion.8
  264.0 10.1 %collective-permute-done.24 = bf16[128,1024]{1,0:T(8,128)(2,1)S(1)} collective-permute-done((bf16[128,1024]{1,0:T(8,128)(2,1)S(1)}, bf16[128,1024]{1,0:T(8,128)(2,1)S(1)}, u32[]{:S(2)}, u32[]{:S(2)}) %collective-permute-start.24) | collective-permute-done | bytes 262176 | tf_op jit(solution)/shard_map/ppermute | solution.py:568
  274.2 2.1 fusion.12
  (171 shorter events, 42.9 us)
Async XLA Ops:
  15.1 21.2 %copy-start.19 = (f32[1024]{0:T(1024)S(1)}, f32[1024]{0:T(1024)}, u32[]{:S(2)}) copy-start(f32[1024]{0:T(1024)} %param.21) | copy-start | bytes 12292
  33.0 40.2 %copy-start.3 = (bf16[1024,1024]{1,0:T(8,128)(2,1)S(1)}, bf16[1024,1024]{1,0:T(8,128)(2,1)}, u32[]{:S(2)}) copy-start(bf16[1024,1024]{1,0:T(8,128)(2,1)} %wo_ref.3) | copy-start | bytes 6291460
  33.0 53.8 %collective-permute-start.15 = (bf16[4,256,1024]{2,1,0:T(8,128)(2,1)}, bf16[4,256,1024]{2,1,0:T(8,128)(2,1)}, u32[]{:S(2)}, u32[]{:S(2)}) collective-permute-start(bf16[4,256,1024]{2,1,0:T(8,128)(2,1)} %shard_map.214.sb_ref.s0), channel_id=1, source_target_pairs={{0,4},{4,0},{8,12},{12,8},{16,20},{20,16},{24,28},{28,24},{1,5},{5... | collective-permute-start | bytes 6291464 | tf_op jit(solution)/shard_map/ppermute | solution.py:568
  33.4 38.4 %collective-permute-start.1 = (bf16[512,1024]{1,0:T(8,128)(2,1)S(1)}, bf16[512,1024]{1,0:T(8,128)(2,1)}, u32[]{:S(2)}, u32[]{:S(2)}) collective-permute-start(bf16[512,1024]{1,0:T(8,128)(2,1)S(1)} %get-tuple-element.37.tok_ref.refs_0_.t0), channel_id=1, source_target_pairs={{0,1},{1,0},{2,3},{3,2},{4,5},{5,4},{6,7},{7,6},{8,9},{9,8},{10,11... | collective-permute-start | bytes 3145736 | tf_op jit(solution)/shard_map/ppermute | solution.py:568
  36.0 49.6 %collective-permute-start = (bf16[512,1024]{1,0:T(8,128)(2,1)S(1)}, bf16[512,1024]{1,0:T(8,128)(2,1)}, u32[]{:S(2)}, u32[]{:S(2)}) collective-permute-start(bf16[512,1024]{1,0:T(8,128)(2,1)S(1)} %get-tuple-element.37.tok_ref.refs_0_.t0), channel_id=1, source_target_pairs={{0,4},{4,0},{8,12},{12,8},{16,20},{20,16},{24,28},{28,24},{1,5},{5... | collective-permute-start | bytes 3145736 | tf_op jit(solution)/shard_map/ppermute | solution.py:568
  41.0 41.5 %collective-permute-start.3 = (bf16[272,1024]{1,0:T(8,128)(2,1)}, bf16[272,1024]{1,0:T(8,128)(2,1)}, u32[]{:S(2)}, u32[]{:S(2)}) collective-permute-start(bf16[272,1024]{1,0:T(8,128)(2,1)} %pad_maximum_fusion.1), channel_id=1, source_target_pairs={{0,2},{1,3},{2,0},{3,1},{4,6},{5,7},{6,4},{7,5},{8,10},{9,11},{10,... | collective-permute-start | bytes 1671176 | tf_op jit(solution)/shard_map/ppermute | solution.py:568
  71.9 39.4 %collective-permute-start.2 = (bf16[512,1024]{1,0:T(8,128)(2,1)}, bf16[512,1024]{1,0:T(8,128)(2,1)}, u32[]{:S(2)}, u32[]{:S(2)}) collective-permute-start(bf16[512,1024]{1,0:T(8,128)(2,1)} %collective-permute-done.1.refs_2_), channel_id=1, source_target_pairs={{0,4},{4,0},{8,12},{12,8},{16,20},{20,16},{24,28},{28,24},{1,5},{5... | collective-permute-start | bytes 3145736 | tf_op jit(solution)/shard_map/ppermute | solution.py:568
  82.5 16.6 %collective-permute-start.6 = (bf16[272,1024]{1,0:T(8,128)(2,1)}, bf16[272,1024]{1,0:T(8,128)(2,1)S(1)}, u32[]{:S(2)}, u32[]{:S(2)}) collective-permute-start(bf16[272,1024]{1,0:T(8,128)(2,1)} %collective-permute-done.3.refs_4_.refs_6_), channel_id=1, source_target_pairs={{0,24},{4,28},{8,16},{12,20},{16,8},{20,12},{24,0},{28,4},{1,25},{... | collective-permute-start | bytes 1671176 | tf_op jit(solution)/shard_map/ppermute | solution.py:568
  85.1 25.5 %collective-permute-start.5 = (bf16[272,1024]{1,0:T(8,128)(2,1)}, bf16[272,1024]{1,0:T(8,128)(2,1)S(1)}, u32[]{:S(2)}, u32[]{:S(2)}) collective-permute-start(bf16[272,1024]{1,0:T(8,128)(2,1)} %collective-permute-done.3.refs_4_.refs_6_), channel_id=1, source_target_pairs={{0,16},{4,20},{8,24},{12,28},{16,0},{20,4},{24,8},{28,12},{1,17},{... | collective-permute-start | bytes 1671176 | tf_op jit(solution)/shard_map/ppermute | solution.py:568
  85.6 25.6 %collective-permute-start.4 = (bf16[272,1024]{1,0:T(8,128)(2,1)}, bf16[272,1024]{1,0:T(8,128)(2,1)S(1)}, u32[]{:S(2)}, u32[]{:S(2)}) collective-permute-start(bf16[272,1024]{1,0:T(8,128)(2,1)} %collective-permute-done.3.refs_4_.refs_6_), channel_id=1, source_target_pairs={{0,8},{4,12},{8,0},{12,4},{16,24},{20,28},{24,16},{28,20},{1,9},{5... | collective-permute-start | bytes 1671176 | tf_op jit(solution)/shard_map/ppermute | solution.py:568
  94.2 81.2 %collective-permute-start.16 = (bf16[2,2,128,1024]{3,2,1,0:T(8,128)(2,1)S(1)}, bf16[2,2,128,1024]{3,2,1,0:T(8,128)(2,1)}, u32[]{:S(2)}, u32[]{:S(2)}) collective-permute-start(bf16[2,2,128,1024]{3,2,1,0:T(8,128)(2,1)S(1)} %get-tuple-element.53), channel_id=1, source_target_pairs={{0,8},{4,12},{8,0},{12,4},{16,24},{20,28},{24,16},{28,20},{1,9},{5... | collective-permute-start | bytes 3145736 | tf_op jit(solution)/shard_map/ppermute | solution.py:568
  99.1 25.1 %copy-start.13 = (bf16[1024,1024]{1,0:T(8,128)(2,1)S(1)}, bf16[1024,1024]{1,0:T(8,128)(2,1)}, u32[]{:S(2)}) copy-start(bf16[1024,1024]{1,0:T(8,128)(2,1)} %refs_0_.1) | copy-start | bytes 6291460
  99.1 25.1 %copy-start.14 = (bf16[1024,1024]{1,0:T(8,128)(2,1)S(1)}, bf16[1024,1024]{1,0:T(8,128)(2,1)}, u32[]{:S(2)}) copy-start(bf16[1024,1024]{1,0:T(8,128)(2,1)} %refs_1_.1) | copy-start | bytes 6291460
  99.1 79.6 %collective-permute-start.19 = (bf16[2,2,128,1024]{3,2,1,0:T(8,128)(2,1)S(1)}, bf16[2,2,128,1024]{3,2,1,0:T(8,128)(2,1)}, u32[]{:S(2)}, u32[]{:S(2)}) collective-permute-start(bf16[2,2,128,1024]{3,2,1,0:T(8,128)(2,1)S(1)} %get-tuple-element.55), channel_id=1, source_target_pairs={{0,16},{4,20},{8,24},{12,28},{16,0},{20,4},{24,8},{28,12},{1,17},{... | collective-permute-start | bytes 3145736 | tf_op jit(solution)/shard_map/ppermute | solution.py:568
  122.7 22.4 %collective-permute-start.28 = (bf16[2,2,512,128]{3,2,1,0:T(8,128)(2,1)S(1)}, bf16[2,2,512,128]{3,2,1,0:T(8,128)(2,1)}, u32[]{:S(2)}, u32[]{:S(2)}) collective-permute-start(bf16[2,2,512,128]{3,2,1,0:T(8,128)(2,1)S(1)} %get-tuple-element.59), channel_id=1, source_target_pairs={{0,8},{4,12},{8,0},{12,4},{16,24},{20,28},{24,16},{28,20},{1,9},{5... | collective-permute-start | bytes 1572872 | tf_op jit(solution)/shard_map/ppermute | solution.py:568
  131.8 49.0 %copy-start.25 = (f32[2,2,128,1024]{3,2,1,0:T(8,128)}, f32[2,2,128,1024]{3,2,1,0:T(8,128)S(1)}, u32[]{:S(2)}) copy-start(f32[2,2,128,1024]{3,2,1,0:T(8,128)S(1)} %convert_element_type.183) | copy-start | bytes 6291460
  131.8 24.1 %collective-permute-start.26 = (bf16[2,2,512,128]{3,2,1,0:T(8,128)(2,1)S(1)}, bf16[2,2,512,128]{3,2,1,0:T(8,128)(2,1)}, u32[]{:S(2)}, u32[]{:S(2)}) collective-permute-start(bf16[2,2,512,128]{3,2,1,0:T(8,128)(2,1)S(1)} %get-tuple-element.57), channel_id=1, source_target_pairs={{0,8},{4,12},{8,0},{12,4},{16,24},{20,28},{24,16},{28,20},{1,9},{5... | collective-permute-start | bytes 1572872 | tf_op jit(solution)/shard_map/ppermute | solution.py:568
  132.4 24.7 %collective-permute-start.33 = (bf16[2,2,512,128]{3,2,1,0:T(8,128)(2,1)S(1)}, bf16[2,2,512,128]{3,2,1,0:T(8,128)(2,1)}, u32[]{:S(2)}, u32[]{:S(2)}) collective-permute-start(bf16[2,2,512,128]{3,2,1,0:T(8,128)(2,1)S(1)} %get-tuple-element.63), channel_id=1, source_target_pairs={{0,16},{4,20},{8,24},{12,28},{16,0},{20,4},{24,8},{28,12},{1,17},{... | collective-permute-start | bytes 1572872 | tf_op jit(solution)/shard_map/ppermute | solution.py:568
  145.1 13.6 %collective-permute-start.30 = (bf16[2,2,512,128]{3,2,1,0:T(8,128)(2,1)S(1)}, bf16[2,2,512,128]{3,2,1,0:T(8,128)(2,1)S(1)}, u32[]{:S(2)}, u32[]{:S(2)}) collective-permute-start(bf16[2,2,512,128]{3,2,1,0:T(8,128)(2,1)S(1)} %get-tuple-element.61), channel_id=1, source_target_pairs={{0,16},{4,20},{8,24},{12,28},{16,0},{20,4},{24,8},{28,12},{1,17},{... | collective-permute-start | bytes 1572872 | tf_op jit(solution)/shard_map/ppermute | solution.py:568
  155.9 45.3 %collective-permute-start.7 = (bf16[2,2,256,1024]{3,2,1,0:T(8,128)(2,1)S(1)}, bf16[2,2,256,1024]{3,2,1,0:T(8,128)(2,1)S(1)}, u32[]{:S(2)}, u32[]{:S(2)}) collective-permute-start(bf16[2,2,256,1024]{3,2,1,0:T(8,128)(2,1)S(1)} %get-tuple-element.44), channel_id=1, source_target_pairs={{0,4},{4,0},{8,12},{12,8},{16,20},{20,16},{24,28},{28,24},{1,5},{5... | collective-permute-start | bytes 6291464 | tf_op jit(solution)/shard_map/ppermute | solution.py:568
  157.0 9.2 %collective-permute-start.29 = (bf16[1,2,512,128]{3,2,1,0:T(8,128)(2,1)S(1)}, bf16[1,2,512,128]{3,2,1,0:T(8,128)(2,1)S(1)}, u32[]{:S(2)}, u32[]{:S(2)}) collective-permute-start(bf16[1,2,512,128]{3,2,1,0:T(8,128)(2,1)S(1)} %fusion.21), channel_id=1, source_target_pairs={{0,16},{4,20},{8,24},{12,28},{16,0},{20,4},{24,8},{28,12},{1,17},{... | collective-permute-start | bytes 786440 | tf_op jit(solution)/shard_map/ppermute | solution.py:568
  158.7 41.5 %collective-permute-start.27 = (bf16[1,2,512,128]{3,2,1,0:T(8,128)(2,1)S(1)}, bf16[1,2,512,128]{3,2,1,0:T(8,128)(2,1)S(1)}, u32[]{:S(2)}, u32[]{:S(2)}) collective-permute-start(bf16[1,2,512,128]{3,2,1,0:T(8,128)(2,1)S(1)} %fusion.24), channel_id=1, source_target_pairs={{0,16},{4,20},{8,24},{12,28},{16,0},{20,4},{24,8},{28,12},{1,17},{... | collective-permute-start | bytes 786440 | tf_op jit(solution)/shard_map/ppermute | solution.py:568
  166.2 7.6 %collective-permute-start.31 = (bf16[1,2,512,128]{3,2,1,0:T(8,128)(2,1)S(1)}, bf16[1,2,512,128]{3,2,1,0:T(8,128)(2,1)S(1)}, u32[]{:S(2)}, u32[]{:S(2)}) collective-permute-start(bf16[1,2,512,128]{3,2,1,0:T(8,128)(2,1)S(1)} %fusion.18), channel_id=1, source_target_pairs={{0,8},{4,12},{8,0},{12,4},{16,24},{20,28},{24,16},{28,20},{1,9},{5... | collective-permute-start | bytes 786440 | tf_op jit(solution)/shard_map/ppermute | solution.py:568
  173.8 26.5 %collective-permute-start.34 = (bf16[1,2,512,128]{3,2,1,0:T(8,128)(2,1)S(1)}, bf16[1,2,512,128]{3,2,1,0:T(8,128)(2,1)S(1)}, u32[]{:S(2)}, u32[]{:S(2)}) collective-permute-start(bf16[1,2,512,128]{3,2,1,0:T(8,128)(2,1)S(1)} %fusion.16), channel_id=1, source_target_pairs={{0,8},{4,12},{8,0},{12,4},{16,24},{20,28},{24,16},{28,20},{1,9},{5... | collective-permute-start | bytes 786440 | tf_op jit(solution)/shard_map/ppermute | solution.py:568
  175.4 24.2 %collective-permute-start.32 = (bf16[2,2,512,128]{3,2,1,0:T(8,128)(2,1)S(1)}, bf16[2,2,512,128]{3,2,1,0:T(8,128)(2,1)S(1)}, u32[]{:S(2)}, u32[]{:S(2)}) collective-permute-start(bf16[2,2,512,128]{3,2,1,0:T(8,128)(2,1)S(1)} %pad_maximum_fusion.3), channel_id=1, source_target_pairs={{0,2},{1,3},{2,0},{3,1},{4,6},{5,7},{6,4},{7,5},{8,10},{9,11},{10,... | collective-permute-start | bytes 1572872 | tf_op jit(solution)/shard_map/ppermute | solution.py:568
  178.7 24.0 %collective-permute-start.17 = (bf16[1,2,128,1024]{3,2,1,0:T(8,128)(2,1)S(1)}, bf16[1,2,128,1024]{3,2,1,0:T(8,128)(2,1)S(1)}, u32[]{:S(2)}, u32[]{:S(2)}) collective-permute-start(bf16[1,2,128,1024]{3,2,1,0:T(8,128)(2,1)S(1)} %fusion.3), channel_id=1, source_target_pairs={{0,16},{4,20},{8,24},{12,28},{16,0},{20,4},{24,8},{28,12},{1,17},{... | collective-permute-start | bytes 1572872 | tf_op jit(solution)/shard_map/ppermute | solution.py:568
  180.8 19.4 %copy-start.26 = (f32[2,2,128,1024]{3,2,1,0:T(8,128)}, f32[2,2,128,1024]{3,2,1,0:T(8,128)S(1)}, u32[]{:S(2)}) copy-start(f32[2,2,128,1024]{3,2,1,0:T(8,128)S(1)} %convert_element_type.184) | copy-start | bytes 6291460
  199.6 20.7 %collective-permute-start.20 = (bf16[1,2,128,1024]{3,2,1,0:T(8,128)(2,1)}, bf16[1,2,128,1024]{3,2,1,0:T(8,128)(2,1)}, u32[]{:S(2)}, u32[]{:S(2)}) collective-permute-start(bf16[1,2,128,1024]{3,2,1,0:T(8,128)(2,1)} %fusion), channel_id=1, source_target_pairs={{0,8},{4,12},{8,0},{12,4},{16,24},{20,28},{24,16},{28,20},{1,9},{5... | collective-permute-start | bytes 1572872 | tf_op jit(solution)/shard_map/ppermute | solution.py:568
  201.2 37.7 %collective-permute-start.35 = (bf16[2,512,128]{2,1,0:T(8,128)(2,1)}, bf16[2,512,128]{2,1,0:T(8,128)(2,1)S(1)}, u32[]{:S(2)}, u32[]{:S(2)}) collective-permute-start(bf16[2,512,128]{2,1,0:T(8,128)(2,1)} %fusion.31), channel_id=1, source_target_pairs={{0,4},{4,0},{8,12},{12,8},{16,20},{20,16},{24,28},{28,24},{1,5},{5... | collective-permute-start | bytes 786440 | tf_op jit(solution)/shard_map/ppermute | solution.py:568
  201.2 16.2 %copy-start.4 = (bf16[2,2,256,1024]{3,2,1,0:T(8,128)(2,1)}, bf16[2,2,256,1024]{3,2,1,0:T(8,128)(2,1)S(1)}, u32[]{:S(2)}) copy-start(bf16[2,2,256,1024]{3,2,1,0:T(8,128)(2,1)S(1)} %collective-permute-done.7.g2) | copy-start | bytes 6291460
  202.7 14.7 %collective-permute-start.9 = (bf16[1,256,1024]{2,1,0:T(8,128)(2,1)S(1)}, bf16[1,256,1024]{2,1,0:T(8,128)(2,1)S(1)}, u32[]{:S(2)}, u32[]{:S(2)}) collective-permute-start(bf16[1,256,1024]{2,1,0:T(8,128)(2,1)S(1)} %get-tuple-element.84), channel_id=1, source_target_pairs={{0,1},{1,0},{2,3},{3,2},{4,5},{5,4},{6,7},{7,6},{8,9},{9,8},{10,11... | collective-permute-start | bytes 1572872 | tf_op jit(solution)/shard_map/ppermute | solution.py:568
  203.8 38.0 %collective-permute-start.18 = (bf16[128,1024]{1,0:T(8,128)(2,1)}, bf16[128,1024]{1,0:T(8,128)(2,1)}, u32[]{:S(2)}, u32[]{:S(2)}) collective-permute-start(bf16[128,1024]{1,0:T(8,128)(2,1)} %fusion.30), channel_id=1, source_target_pairs={{0,1},{1,0},{2,3},{3,2},{4,5},{5,4},{6,7},{7,6},{8,9},{9,8},{10,11... | collective-permute-start | bytes 786440 | tf_op jit(solution)/shard_map/ppermute | solution.py:568
  220.1 18.7 %copy-start.33 = (bf16[1,256,1024]{2,1,0:T(8,128)(2,1)S(1)}, bf16[1,256,1024]{2,1,0:T(8,128)(2,1)}, u32[]{:S(2)}) copy-start(bf16[1,256,1024]{2,1,0:T(8,128)(2,1)} %get-tuple-element.85) | copy-start | bytes 1572868
  220.1 18.9 %copy-start.28 = (f32[1,2,512,128]{3,2,1,0:T(8,128)S(1)}, f32[1,2,512,128]{3,2,1,0:T(8,128)}, u32[]{:S(2)}) copy-start(f32[1,2,512,128]{3,2,1,0:T(8,128)} %copy-done.27) | copy-start | bytes 1572868
  220.2 4.0 %collective-permute-start.10 = (f32[6,1024]{1,0:T(8,128)S(1)}, f32[6,1024]{1,0:T(8,128)S(1)}, u32[]{:S(2)}, u32[]{:S(2)}) collective-permute-start(f32[6,1024]{1,0:T(8,128)S(1)} %concatenate.35), channel_id=1, source_target_pairs={{0,1},{1,0},{2,3},{3,2},{4,5},{5,4},{6,7},{7,6},{8,9},{9,8},{10,11... | collective-permute-start | bytes 73736 | tf_op jit(solution)/shard_map/ppermute | solution.py:568
  222.3 24.0 %copy-start.32 = (f32[1,2,128,1024]{3,2,1,0:T(8,128)S(1)}, f32[1,2,128,1024]{3,2,1,0:T(8,128)}, u32[]{:S(2)}) copy-start(f32[1,2,128,1024]{3,2,1,0:T(8,128)} %copy-done.31) | copy-start | bytes 3145732
  224.2 14.6 %collective-permute-start.11 = (f32[6,1024]{1,0:T(8,128)S(1)}, f32[6,1024]{1,0:T(8,128)S(1)}, u32[]{:S(2)}, u32[]{:S(2)}) collective-permute-start(f32[6,1024]{1,0:T(8,128)S(1)} %maximum_maximum_fusion), channel_id=1, source_target_pairs={{0,2},{1,3},{2,0},{3,1},{4,6},{5,7},{6,4},{7,5},{8,10},{9,11},{10,... | collective-permute-start | bytes 73736 | tf_op jit(solution)/shard_map/ppermute | solution.py:568
  225.4 20.9 %collective-permute-start.21 = (bf16[128,1024]{1,0:T(8,128)(2,1)S(1)}, bf16[128,1024]{1,0:T(8,128)(2,1)S(1)}, u32[]{:S(2)}, u32[]{:S(2)}) collective-permute-start(bf16[128,1024]{1,0:T(8,128)(2,1)S(1)} %get-tuple-element.86), channel_id=1, source_target_pairs={{0,2},{1,3},{2,0},{3,1},{4,6},{5,7},{6,4},{7,5},{8,10},{9,11},{10,... | collective-permute-start | bytes 786440 | tf_op jit(solution)/shard_map/ppermute | solution.py:568
  227.3 19.0 %collective-permute-start.22 = (bf16[128,1024]{1,0:T(8,128)(2,1)S(1)}, bf16[128,1024]{1,0:T(8,128)(2,1)S(1)}, u32[]{:S(2)}, u32[]{:S(2)}) collective-permute-start(bf16[128,1024]{1,0:T(8,128)(2,1)S(1)} %get-tuple-element.87), channel_id=1, source_target_pairs={{0,3},{1,2},{2,1},{3,0},{4,7},{5,6},{6,5},{7,4},{8,11},{9,10},{10,... | collective-permute-start | bytes 786440 | tf_op jit(solution)/shard_map/ppermute | solution.py:568
  238.8 17.0 %collective-permute-start.8 = (bf16[1,256,1024]{2,1,0:T(8,128)(2,1)S(1)}, bf16[1,256,1024]{2,1,0:T(8,128)(2,1)S(1)}, u32[]{:S(2)}, u32[]{:S(2)}) collective-permute-start(bf16[1,256,1024]{2,1,0:T(8,128)(2,1)S(1)} %copy-done.33), channel_id=1, source_target_pairs={{0,1},{1,0},{2,3},{3,2},{4,5},{5,4},{6,7},{7,6},{8,9},{9,8},{10,11... | collective-permute-start | bytes 1572872 | tf_op jit(solution)/shard_map/ppermute | solution.py:568
  238.9 16.9 %copy-start.10 = (f32[256,1024]{1,0:T(8,128)S(1)}, f32[256,1024]{1,0:T(8,128)}, u32[]{:S(2)}) copy-start(f32[256,1024]{1,0:T(8,128)} %copy-done.9) | copy-start | bytes 3145732
  238.9 16.9 %copy-start.34 = (f32[1024]{0:T(1024)S(1)}, f32[1024]{0:T(1024)}, u32[]{:S(2)}) copy-start(f32[1024]{0:T(1024)} %param.23) | copy-start | bytes 12292
  238.9 1.3 collective-permute-start.12
  240.2 15.0 %collective-permute-start.13 = (f32[5,1024]{1,0:T(8,128)S(1)}, f32[5,1024]{1,0:T(8,128)S(1)}, u32[]{:S(2)}, u32[]{:S(2)}) collective-permute-start(f32[5,1024]{1,0:T(8,128)S(1)} %fusion.42), channel_id=1, source_target_pairs={{0,8},{4,12},{8,0},{12,4},{16,24},{20,28},{24,16},{28,20},{1,9},{5... | collective-permute-start | bytes 61448 | tf_op jit(solution)/shard_map/ppermute | solution.py:568
  247.4 16.6 %collective-permute-start.25 = (bf16[128,1024]{1,0:T(8,128)(2,1)S(1)}, bf16[128,1024]{1,0:T(8,128)(2,1)S(1)}, u32[]{:S(2)}, u32[]{:S(2)}) collective-permute-start(bf16[128,1024]{1,0:T(8,128)(2,1)S(1)} %fusion.29), channel_id=1, source_target_pairs={{0,1},{1,0},{2,3},{3,2},{4,5},{5,4},{6,7},{7,6},{8,9},{9,8},{10,11... | collective-permute-start | bytes 786440 | tf_op jit(solution)/shard_map/ppermute | solution.py:568
  252.8 21.4 %collective-permute-start.24 = (bf16[128,1024]{1,0:T(8,128)(2,1)S(1)}, bf16[128,1024]{1,0:T(8,128)(2,1)S(1)}, u32[]{:S(2)}, u32[]{:S(2)}) collective-permute-start(bf16[128,1024]{1,0:T(8,128)(2,1)S(1)} %fusion.29), channel_id=1, source_target_pairs={{0,2},{1,3},{2,0},{3,1},{4,6},{5,7},{6,4},{7,5},{8,10},{9,11},{10,... | collective-permute-start | bytes 786440 | tf_op jit(solution)/shard_map/ppermute | solution.py:568
  253.2 20.9 %collective-permute-start.23 = (bf16[128,1024]{1,0:T(8,128)(2,1)S(1)}, bf16[128,1024]{1,0:T(8,128)(2,1)}, u32[]{:S(2)}, u32[]{:S(2)}) collective-permute-start(bf16[128,1024]{1,0:T(8,128)(2,1)S(1)} %fusion.29), channel_id=1, source_target_pairs={{0,3},{1,2},{2,1},{3,0},{4,7},{5,6},{6,5},{7,4},{8,11},{9,10},{10,... | collective-permute-start | bytes 786440 | tf_op jit(solution)/shard_map/ppermute | solution.py:568
  255.2 4.0 %collective-permute-start.14 = (f32[5,1024]{1,0:T(8,128)S(1)}, f32[5,1024]{1,0:T(8,128)S(1)}, u32[]{:S(2)}, u32[]{:S(2)}) collective-permute-start(f32[5,1024]{1,0:T(8,128)S(1)} %add.154), channel_id=1, source_target_pairs={{0,16},{4,20},{8,24},{12,28},{16,0},{20,4},{24,8},{28,12},{1,17},{... | collective-permute-start | bytes 61448 | tf_op jit(solution)/shard_map/ppermute | solution.py:568
  (23 other events, 107.1 us)

commit v2 on v0

v2 whole, which is shorter than its diff:
```python
from functools import partial

import numpy as np

import jax
import jax.numpy as jnp
from jax import lax
from jax.experimental import pallas as pl
from jax.experimental.pallas import tpu as pltpu
from jax.sharding import PartitionSpec as P

HEADS = 16
HEAD_DIM = 64
ROT = 32
SEQ_DEV = 4
EPSILON = 1e-05
NEGATIVE = -1e30
LANES = 256
BF = jnp.bfloat16
F32 = jnp.float32
MIB = 1 << 20
BIAS_ROWS = 16
US = 0.1
SUMS = 4

COUNT, LIVE, ENDS, STARTS, TERMS, OFFS, TABLE = 0, 1, 2, 6, 10, 14, 24


def nn(a, b):
    return lax.dot_general(a, b, (((1,), (0,)), ((), ())), preferred_element_type=F32)


def nt(a, b):
    return lax.dot_general(a, b, (((1,), (1,)), ((), ())), preferred_element_type=F32)


def call(kernel, args, outs, scratch=(), specs=None, out_specs=None, grid=None, vmem=24, us=US, after=()):
    count = len(args)
    specs = specs or {}

    def body(*refs):
        kernel(*refs[:count], *refs[count + len(after) :])

    single = not isinstance(outs, tuple)
    options = {} if grid is None else {"grid": grid}
    return pl.pallas_call(
        body,
        in_specs=[specs.get(n, VMEM) for n in range(count)] + [ANY] * len(after),
        out_specs=out_specs or (VMEM if single else (VMEM,) * len(outs)),
        out_shape=outs,
        scratch_shapes=list(scratch),
        compiler_params=pltpu.CompilerParams(vmem_limit_bytes=vmem * MIB),
        cost_estimate=pl.CostEstimate(
            flops=int(us * 1e9), bytes_accessed=1024, transcendentals=0
        ),
        **options,
    )(*args, *after)


def places():
    place = lax.axis_index("dp")
    return lax.bitwise_and(place, 1), lax.shift_right_logical(place, 1), lax.axis_index("mp")


VMEM = pl.BlockSpec(memory_space=pltpu.VMEM)
SMEM = pl.BlockSpec(memory_space=pltpu.SMEM)
HBM = pl.BlockSpec(memory_space=pltpu.HBM)
ANY = pl.BlockSpec(memory_space=pl.ANY)


def struct(shape, dtype):
    return jax.ShapeDtypeStruct(shape, dtype)


def normalize(hidden):
    mean = jnp.mean(hidden, axis=-1, keepdims=True)
    removed = hidden - mean
    variance = jnp.mean(removed * removed, axis=-1, keepdims=True)
    inverse = lax.rsqrt(variance + EPSILON)
    return removed * inverse, inverse


def pack_kernel(chips, eb_ref, we_ref, ws_ref, pack_ref, row_ref, sem):
    width = we_ref.shape[0]
    hidden = ws_ref.shape[0] // 2
    share, strip = hidden // chips, width // chips
    core, chip, _ = places()
    half = pl.ds(pl.multiple_of(core * hidden, 128), hidden)
    start = pl.multiple_of(core * hidden + chip * share, 16)
    copies = [
        pltpu.make_async_copy(eb_ref.at[:, half], row_ref, sem.at[0]),
        pltpu.make_async_copy(
            we_ref.at[pl.ds(pl.multiple_of(chip * strip, 16), strip), half],
            pack_ref.at[pl.ds(0, strip), pl.ds(0, hidden)],
            sem.at[1],
        ),
    ]
    for b in range(width // hidden):
        copies.append(
            pltpu.make_async_copy(
                ws_ref.at[pl.ds(start, share), pl.ds(b * hidden, hidden)],
                pack_ref.at[pl.ds(b * share, share), pl.ds(hidden, hidden)],
                sem.at[2 + b],
            )
        )
    for copy in copies:
        copy.start()
    copies[0].wait()
    bias = row_ref[...]
    high = bias.astype(BF)
    middle = (bias - high.astype(F32)).astype(BF)
    lowest = (bias - high.astype(F32) - middle.astype(F32)).astype(BF)
    line = lax.broadcasted_iota(jnp.int32, (BIAS_ROWS, hidden), 0)
    table = jnp.where(line == 0, high.astype(F32), 0.0)
    table = jnp.where(line == 1, middle.astype(F32), table)
    table = jnp.where(line == 2, lowest.astype(F32), table)
    pack_ref[strip:, :hidden] = table.astype(BF)
    pack_ref[strip:, hidden:] = jnp.zeros((BIAS_ROWS, hidden), BF)
    for copy in copies[1:]:
        copy.wait()


def pack(chips, eb, we, ws):
    width, hidden = we.shape[0], ws.shape[0] // 2
    return call(
        partial(pack_kernel, chips),
        (eb, we, ws),
        struct((width // chips + BIAS_ROWS, 2 * hidden), BF),
        scratch=[
            pltpu.VMEM((1, hidden), F32),
            pltpu.SemaphoreType.DMA((2 + width // hidden,)),
        ],
        specs={0: HBM, 1: HBM, 2: HBM},
        vmem=59,
    )


def prepare_kernel(
    lens_ref,
    terms_ref,
    offs_ref,
    x_hbm,
    u_hbm,
    gain_hbm,
    bias_hbm,
    info,
    normed_ref,
    grad_ref,
    sum_ref,
    x_ref,
    u_ref,
    gain_ref,
    bias_ref,
    sem,
):
    rows, width = x_ref.shape
    zpos = places()[2]
    copies = [
        pltpu.make_async_copy(src, dst, sem.at[n])
        for n, (src, dst) in enumerate(
            ((x_hbm, x_ref), (gain_hbm, gain_ref), (bias_hbm, bias_ref), (u_hbm, u_ref))
        )
    ]
    for copy in copies:
        copy.start()

    def note(row, number):
        info[row : row + 1, :] = jnp.zeros((1, info.shape[1]), jnp.int32) + number

    live = 0
    for s in range(SEQ_DEV):
        note(STARTS + s, live)
        live = live + lens_ref[0, zpos * SEQ_DEV + s]
        note(ENDS + s, live)
        note(TERMS + s, terms_ref[0, s])
        note(OFFS + s, offs_ref[0, s])
    total = 0
    for s in range(lens_ref.shape[1]):
        total = total + lens_ref[0, s]
    note(LIVE, live)
    note(COUNT, total)
    step = 64
    count = total.astype(F32)
    sums = jnp.zeros((1, width), F32)
    for copy in copies:
        copy.wait()
    for r in range(0, rows, step):
        xhat, _ = normalize(x_ref[r : r + step, :].astype(F32))
        normed_ref[r : r + step, :] = (xhat * gain_ref[...] + bias_ref[...]).astype(BF)
        where = lax.broadcasted_iota(jnp.int32, (step, width), 0) + r
        grad = jnp.where(where < live, u_ref[r : r + step, :].astype(F32) * count, 0.0).astype(BF)
        grad_ref[r : r + step, :] = grad
        sums = sums + jnp.sum(grad.astype(F32), axis=0, keepdims=True)
    sum_ref[...] = sums


def prepare(lens, terms, offs, x, u, gain, bias, after=()):
    rows, width = x.shape
    return call(
        prepare_kernel,
        (lens, terms, offs, x, u, gain, bias),
        (
            struct((TABLE, LANES), jnp.int32),
            struct((rows, width), BF),
            struct((rows, width), BF),
            struct((1, width), F32),
        ),
        scratch=[
            pltpu.VMEM((rows, width), BF),
            pltpu.VMEM((rows, width), BF),
            pltpu.VMEM((1, width), F32),
            pltpu.VMEM((1, width), F32),
            pltpu.SemaphoreType.DMA((4,)),
        ],
        specs={0: SMEM, 1: SMEM, 2: SMEM, 3: HBM, 4: HBM, 5: HBM, 6: HBM},
        vmem=58,
        after=after,
    )


def slot_of(place, ends):
    index = jnp.zeros(place.shape, jnp.int32)
    for end in ends:
        index = index + (place >= end).astype(jnp.int32)
    return index


def attention_kernel(
    info, normed_ref, bg_ref, freq_ref, wa_hbm, wo_hbm, *refs
):
    out_ref, cos_ref, sin_ref, mask_ref, wa_ref, wo_ref, sem = refs
    rows, lanes = cos_ref.shape
    width = normed_ref.shape[1]
    blocks = width // lanes
    copies = []
    for n in range(blocks):
        here = slice(n * lanes, (n + 1) * lanes)
        for p in range(3):
            cols = slice(p * width + n * lanes, p * width + (n + 1) * lanes)
            copies.append(
                pltpu.make_async_copy(wa_hbm.at[:, cols], wa_ref.at[n, p], sem.at[4 * n + p])
            )
        copies.append(
            pltpu.make_async_copy(wo_hbm.at[here, :], wo_ref.at[here, :], sem.at[4 * n + 3])
        )
    for copy in copies:
        copy.start()

    def tables():
        ends = [info[ENDS + s : ENDS + s + 1, :] for s in range(SEQ_DEV)]
        place = lax.broadcasted_iota(jnp.int32, (rows, lanes), 0)
        index = slot_of(place, ends)
        start = jnp.zeros(place.shape, jnp.int32)
        terminal = jnp.zeros(place.shape, jnp.int32)
        offset = jnp.zeros(place.shape, jnp.int32)
        for s in range(SEQ_DEV):
            here = index == s
            start = jnp.where(here, info[STARTS + s : STARTS + s + 1, :], start)
            terminal = jnp.where(here, info[TERMS + s : TERMS + s + 1, :], terminal)
            offset = jnp.where(here, info[OFFS + s : OFFS + s + 1, :], offset)
        local = place - start
        position = jnp.where(local <= terminal, offset + local, local - terminal - 1)
        angle = position.astype(F32) * freq_ref[...]
        parity = lax.broadcasted_iota(jnp.int32, (rows, lanes), 1) % 2
        sine = jnp.sin(angle)
        cos_ref[...] = jnp.cos(angle)
        sin_ref[...] = jnp.where(parity == 0, -sine, sine)
        key = lax.broadcasted_iota(jnp.int32, (rows, rows), 0)
        query = lax.broadcasted_iota(jnp.int32, (rows, rows), 1)
        allowed = (slot_of(key, ends) == slot_of(query, ends)) & (key <= query)
        mask_ref[...] = jnp.where(allowed, 0.0, NEGATIVE)

    tables()
    even = lax.broadcasted_iota(jnp.int32, (rows, lanes), 1) % 2 == 0

    def swap(v):
        return jnp.where(even, pltpu.roll(v, lanes - 1, 1), pltpu.roll(v, 1, 1))

    def turn(v):
        return v * cos_ref[...] + swap(v) * sin_ref[...]

    def turn_back(v):
        return v * cos_ref[...] - swap(v) * sin_ref[...]

    scale = HEAD_DIM ** (-0.5)
    for n in range(blocks):
        for copy in copies[4 * n : 4 * n + 4]:
            copy.wait()
        here = slice(n * lanes, (n + 1) * lanes)
        attention_heads(
            normed_ref,
            bg_ref,
            wa_ref.at[n],
            wo_ref.at[here],
            mask_ref,
            [out_ref.at[m, :, here] for m in range(4)],
            turn,
            turn_back,
        )


def attention_heads(normed_ref, bg_ref, wa_ref, wo_ref, mask_ref, outs, turn, turn_back):
    rows, lanes = outs[0].shape
    scale = HEAD_DIM ** (-0.5)
    normed = normed_ref[...]
    queries = (turn(nn(normed, wa_ref[0])) * scale).astype(BF)
    keys = turn(nn(normed, wa_ref[1])).astype(BF)
    values = nn(normed, wa_ref[2]).astype(BF)
    grads = nt(bg_ref[...], wo_ref[...]).astype(BF)
    pair = 2 * HEAD_DIM
    lane = lax.broadcasted_iota(jnp.int32, (rows, pair), 1)
    masks = [lane < HEAD_DIM, lane >= HEAD_DIM]

    def one(v, h):
        return jnp.where(masks[h], v, jnp.zeros_like(v))

    queries_t = queries.T
    grads_t = grads.T
    keys_t = keys.T
    values_t = values.T
    attended_t, query_grad_t, key_grads, value_grads = [], [], [], []
    for p in range(lanes // pair):
        cols = slice(p * pair, (p + 1) * pair)
        q2, k2, v2, g2 = queries[:, cols], keys[:, cols], values[:, cols], grads[:, cols]
        scores2 = nn(jnp.concatenate([one(k2, 0), one(k2, 1)], axis=0), queries_t[cols, :])
        pg2 = nn(jnp.concatenate([one(v2, 0), one(v2, 1)], axis=0), grads_t[cols, :])
        key_grad = jnp.zeros((rows, pair), F32)
        value_grad = jnp.zeros((rows, pair), F32)
        for h in range(2):
            head = slice(p * pair + h * HEAD_DIM, p * pair + (h + 1) * HEAD_DIM)
            scores = scores2[h * rows : (h + 1) * rows] + mask_ref[...]
            exponent = jnp.exp(scores - jnp.max(scores, axis=0, keepdims=True))
            probs = exponent * (1.0 / jnp.sum(exponent, axis=0, keepdims=True))
            probs_low = probs.astype(BF)
            probs_grad = pg2[h * rows : (h + 1) * rows]
            row_dot = jnp.sum(probs * probs_grad, axis=0, keepdims=True)
            scores_grad = (probs * (probs_grad - row_dot)).astype(BF)
            attended_t.append(nn(values_t[head, :], probs_low))
            query_grad_t.append(nn(keys_t[head, :], scores_grad))
            key_grad = key_grad + nn(scores_grad, one(q2, h))
            value_grad = value_grad + nn(probs_low, one(g2, h))
        key_grads.append(key_grad)
        value_grads.append(value_grad)
    outs[0][...] = jnp.concatenate(attended_t, axis=0).T.astype(BF)
    outs[1][...] = turn_back(jnp.concatenate(query_grad_t, axis=0).T * scale).astype(BF)
    outs[2][...] = turn_back(jnp.concatenate(key_grads, axis=1)).astype(BF)
    outs[3][...] = jnp.concatenate(value_grads, axis=1).astype(BF)


def attention(info, normed, bg, attend_weight, output_weight, after=()):
    rows, width = normed.shape
    blocks = width // LANES
    pair = np.arange(LANES) % HEAD_DIM // 2
    freq = np.where(pair < ROT // 2, 10000.0 ** (-2.0 * pair / ROT), 0.0)[None].astype(np.float32)
    return call(
        attention_kernel,
        (info, normed, bg, jnp.asarray(freq), attend_weight, output_weight),
        struct((4, rows, width), BF),
        scratch=[
            pltpu.VMEM((rows, LANES), F32),
            pltpu.VMEM((rows, LANES), F32),
            pltpu.VMEM((rows, rows), F32),
            pltpu.VMEM((blocks, 3, width, LANES), BF),
            pltpu.VMEM((width, width), BF),
            pltpu.SemaphoreType.DMA((4 * blocks,)),
        ],
        specs={4: HBM, 5: HBM},
        vmem=52,
        after=after,
    )


def attention_back_kernel(sides, wa_ref, wo_ref, grad_ref, out_ref):
    width = sides.shape[2]
    grad = nt(sides[1], wa_ref[:, :width])
    grad = grad + nt(sides[2], wa_ref[:, width : 2 * width])
    grad_ref[...] = grad + nt(sides[3], wa_ref[:, 2 * width :])
    out_ref[...] = nn(sides[0], wo_ref[...])


def attention_back(sides, attend_weight, output_weight, after=()):
    _, rows, width = sides.shape
    block = pl.BlockSpec((rows, LANES), lambda i: (0, i))
    specs = {
        0: pl.BlockSpec(sides.shape, lambda i: (0, 0, 0)),
        1: pl.BlockSpec((LANES, 3 * width), lambda i: (i, 0)),
        2: pl.BlockSpec((width, LANES), lambda i: (0, i)),
    }
    return call(
        attention_back_kernel,
        (sides, attend_weight, output_weight),
        (struct((rows, width), F32), struct((rows, width), F32)),
        specs=specs,
        out_specs=(block, block),
        grid=(width // LANES,),
        after=after,
    )


def with_bit(n, bit):
    return [j for j in range(n) if j >> bit & 1]


def without_bit(n, bit):
    return [j for j in range(n) if not j >> bit & 1]


def attention_grads_kernel(
    chips, depth, n0, n1, g0, g1, s0, s1, ps, pk, qs, qk, ln, la, acc, sem
):
    rows, width = n0.shape
    chunk = width // chips
    half = chunk // 2
    cols = 4 * width // depth
    core, chip, zpos = places()
    for s, (tok, sb) in enumerate(((n0, s0), (n1, s1))):
        for k in range(chips):
            for ref, dst in ((tok, ln), (sb.at[0], la)):
                if half % 128 == 0:
                    start = pl.multiple_of(k * chunk + core * half, 128)
                    piece = ref[0:rows, pl.ds(start, half)]
                else:
                    both = ref[0:rows, k * chunk : (k + 1) * chunk].astype(F32)
                    piece = jnp.where(core == 0, both[:, :half], both[:, half:]).astype(BF)
                dst[k * half : (k + 1) * half, s * rows : (s + 1) * rows] = piece.T
    for a in range(depth):
        part, off = a * cols // width, a * cols % width
        span = slice(off, off + cols)
        if part < 3:
            left, right0, right1 = ln, s0[1 + part, :, span], s1[1 + part, :, span]
        else:
            left, right0, right1 = la, g0[:, span], g1[:, span]
        tile = (nn(left[:, :rows], right0) + nn(left[:, rows:], right1)).astype(BF)
        for k in range(chips):
            acc[chip ^ k, zpos ^ a] = tile[k * half : (k + 1) * half]
    mid = depth // 2
    copies = []
    top = chips.bit_length() - 2
    for js, dst, zs in (
        (with_bit(chips, 0), ps, slice(0, mid)),
        (without_bit(chips, 0), pk, slice(0, mid)),
        (with_bit(chips, top), qs, slice(mid, depth)),
        (without_bit(chips, top), qk, slice(mid, depth)),
    ):
        for i, j in enumerate(js):
            copies.append(pltpu.make_async_copy(acc.at[j, zs], dst.at[i], sem.at[len(copies)]))
    for copy in copies:
        copy.start()
    for copy in copies:
        copy.wait()


def attention_grads(chips, depth, own, core, s0, s1, after=()):
    rows, width = own[0].shape
    half = width // chips // 2
    cols = 4 * width // depth
    piece = struct((chips // 2, depth // 2, half, cols), BF)
    return call(
        partial(attention_grads_kernel, chips, depth),
        (own[0], core[0], own[1], core[1], s0, s1),
        (piece,) * 4,
        scratch=[
            pltpu.VMEM((chips * half, 2 * rows), BF),
            pltpu.VMEM((chips * half, 2 * rows), BF),
            pltpu.VMEM((chips, depth, half, cols), BF),
            pltpu.SemaphoreType.DMA((2 * chips,)),
        ],
        after=after,
    )


def load_weights(sources, we, ws, sem):
    hidden, width = ws.shape
    core, place, _ = places()
    if len(sources) == 2:
        half = pl.ds(pl.multiple_of(core * hidden, 128), hidden)
        return [
            pltpu.make_async_copy(sources[0].at[:, half], we, sem.at[0]),
            pltpu.make_async_copy(sources[1].at[half], ws, sem.at[1]),
        ]
    share, strip = hidden // len(sources), width // len(sources)
    copies = []
    for j, piece in enumerate(sources):
        chip = place ^ j
        copies.append(
            pltpu.make_async_copy(
                piece.at[pl.ds(0, strip), pl.ds(0, hidden)],
                we.at[pl.ds(pl.multiple_of(chip * strip, 16), strip)],
                sem.at[len(copies)],
            )
        )
        for b in range(width // hidden):
            copies.append(
                pltpu.make_async_copy(
                    piece.at[pl.ds(b * share, share), pl.ds(hidden, hidden)],
                    ws.at[
                        pl.ds(pl.multiple_of(chip * share, 16), share),
                        pl.ds(b * hidden, hidden),
                    ],
                    sem.at[len(copies)],
                )
            )
    return copies


def weight_scratch(chips, hidden, width):
    return [
        pltpu.VMEM((width, hidden), BF),
        pltpu.VMEM((hidden, width), BF),
        pltpu.SemaphoreType.DMA((chips * (1 + width // hidden),)),
    ]


def feed_kernel(chips, foreign, *refs):
    toks, refs = refs[:8], refs[8:]
    sources = refs[: chips if foreign else 2]
    refs = refs[len(sources) :]
    if not foreign:
        bias_ref, refs = refs[0], refs[1:]
    act_ref, eg_ref, bias_out, ps, pk, qs, qk = refs[:7]
    x, bg, act_t, eg_t, sem_in, we, ws, sem_w = refs[7:15]
    rows, width = toks[0].shape
    hidden = act_t.shape[0]
    weights = load_weights(sources, we, ws, sem_w)
    if foreign:
        bias_rows, sem_b = refs[15:17]
        strip = width // chips
        weights.append(
            pltpu.make_async_copy(sources[0].at[pl.ds(strip, BIAS_ROWS)], bias_rows, sem_b)
        )
    for copy in weights:
        copy.start()
    loads = []
    for n, tok in enumerate(toks):
        dst = (x, bg)[n % 2].at[pl.ds(n // 2 * rows, rows)]
        loads.append(pltpu.make_async_copy(tok, dst, sem_in.at[n]))
    for copy in loads:
        copy.start()
    for copy in weights:
        copy.wait()
    if foreign:
        bias = jnp.sum(bias_rows[:, :hidden].astype(F32), axis=0, keepdims=True)
    else:
        bias = bias_ref[:, pl.ds(pl.multiple_of(places()[0] * hidden, 128), hidden)]
    for copy in loads:
        copy.wait()
    step = min(256, hidden)
    for h in range(0, hidden, step):
        block = slice(h, h + step)
        v = nn(x[...], we[:, block]) + bias[:, block]
        square = v * v
        t = jnp.tanh(0.7978845608 * v * (1.0 + 0.044715 * square))
        low = 0.5 * (1.0 + t)
        slope = low + 0.5 * v * (1.0 - t * t) * (0.7978845608 * (1.0 + 0.134145 * square))
        act = (v * low).astype(BF)
        eg = (nt(bg[...], ws[block, :]) * slope).astype(BF)
        act_ref[:, block] = act
        eg_ref[:, block] = eg
        act_t[block, :] = act.T
        eg_t[block, :] = eg.T
        bias_out[:, block] = jnp.sum(eg.astype(F32), axis=0, keepdims=True)
    chunk = width // chips
    half = chunk // 2
    core, chip, _ = places()
    top = chips.bit_length() - 2
    for left, right, bit, send, keep in ((eg_t, x, 0, ps, pk), (act_t, bg, top, qs, qk)):
        for dst, js in ((send, with_bit(chips, bit)), (keep, without_bit(chips, bit))):
            for i, j in enumerate(js):
                if half % 128 == 0:
                    start = pl.multiple_of((chip ^ j) * chunk, 128)
                    tile = nn(left[...], right[:, pl.ds(start, chunk)]).astype(BF)
                    for a in range(2):
                        dst[i, core ^ a] = tile[:, a * half : (a + 1) * half]
                    continue
                for k in range(chips):

                    @pl.when(chip ^ j == k)
                    def narrow():
                        tile = nn(left[...], right[:, k * chunk : (k + 1) * chunk]).astype(BF)
                        for a in range(2):
                            dst[i, core ^ a] = tile[:, a * half : (a + 1) * half].T


def feed(chips, toks, weights, bias, hidden, after=()):
    rows, width = toks[0].shape
    half = width // chips // 2
    foreign = bias is None
    edge = (hidden, half) if half % 128 == 0 else (half, hidden)
    piece = struct((chips // 2, 2, *edge), BF)
    scratch = [
        pltpu.VMEM((4 * rows, width), BF),
        pltpu.VMEM((4 * rows, width), BF),
        pltpu.VMEM((hidden, 4 * rows), BF),
        pltpu.VMEM((hidden, 4 * rows), BF),
        pltpu.SemaphoreType.DMA((8,)),
        *weight_scratch(chips, hidden, width),
    ]
    args = (*toks, *weights)
    specs = {n: ANY for n in range(len(args))}
    if foreign:
        scratch += [pltpu.VMEM((BIAS_ROWS, 2 * hidden), BF), pltpu.SemaphoreType.DMA(())]
    else:
        args += (bias,)
    return call(
        partial(feed_kernel, chips, foreign),
        args,
        (struct((4 * rows, hidden), BF),) * 2 + (struct((1, hidden), F32),) + (piece,) * 4,
        scratch=scratch,
        specs=specs,
        us=20.0 if foreign else US,
        after=after,
    )


def feed_out_kernel(chips, shards, *refs):
    sets = []
    for n in range(shards):
        size = chips if n else 2
        sets.append((refs[0], refs[1], refs[2 : 2 + size]))
        refs = refs[2 + size :]
    keep, send = refs[:2]
    rows = keep.shape[2]
    scratch = [refs[2 + 3 * n : 5 + 3 * n] for n in range(shards)]
    copies = []
    for (_, _, sources), (we, ws, sem) in zip(sets, scratch):
        copies += load_weights(sources, we, ws, sem)
    for copy in copies:
        copy.start()
    for copy in copies:
        copy.wait()
    width = keep.shape[3]
    step = min(256, width)
    for c in range(0, width, step):
        block = slice(c, c + step)
        grad, out = 0.0, 0.0
        for (act, eg, _), (we, ws, _) in zip(sets, scratch):
            grad = grad + nt(eg[...], we[block, :])
            out = out + nn(act[...], ws[:, block])
        for m, value in enumerate((grad, out)):
            for r in range(4):
                dst = send if r % 2 else keep
                dst[m, r // 2, :, block] = value[r * rows : (r + 1) * rows].astype(BF)


def feed_out(chips, sets, after=()):
    rows4, hidden = sets[0][0].shape
    width = sets[0][2][1].shape[1]
    args, specs, scratch = (), {}, []
    for act, eg, sources in sets:
        for n in range(len(sources)):
            specs[len(args) + 2 + n] = ANY
        args += (act, eg, *sources)
        scratch += weight_scratch(chips, hidden, width)
    result = struct((2, 2, rows4 // 4, width), BF)
    return call(
        partial(feed_out_kernel, chips, len(sets)),
        args,
        (result, result),
        scratch=scratch,
        specs=specs,
        after=after,
    )


def norm_back_kernel(info, x_ref, u_ref, gain_ref, g0, g1, g2, g3, sum_ref, *refs):
    biases, (out_ref, small_ref) = refs[:-2], refs[-2:]
    rows, width = x_ref.shape
    step = 64
    count = info[COUNT : COUNT + 1, 0:1].astype(F32)
    gain_sum = jnp.zeros((1, width), F32)
    shift_sum = jnp.zeros((1, width), F32)
    for r in range(0, rows, step):
        here = slice(r, r + step)
        xhat, inverse = normalize(x_ref[here, :].astype(F32))
        grad = g0[here, :] + g1[0, 0, here, :].astype(F32) + g2[0, 0, here, :].astype(F32)
        grad = grad + g3[0, here, :].astype(F32)
        gain_sum = gain_sum + jnp.sum(grad * xhat, axis=0, keepdims=True)
        shift_sum = shift_sum + jnp.sum(grad, axis=0, keepdims=True)
        scaled = grad * gain_ref[...]
        mean = jnp.mean(scaled, axis=-1, keepdims=True)
        dot = jnp.mean(scaled * xhat, axis=-1, keepdims=True)
        out_ref[here, :] = u_ref[here, :].astype(F32) * count + inverse * (
            scaled - mean - xhat * dot
        )
    small_ref[...] = jnp.zeros(small_ref.shape, F32)
    small_ref[0:1, :] = gain_sum
    small_ref[1:2, :] = shift_sum
    small_ref[2:3, :] = sum_ref[...]
    small_ref[3:4, :] = jnp.zeros((1, width), F32) + count
    hidden = biases[0].shape[1]
    half = pl.ds(pl.multiple_of(places()[0] * hidden, 128), hidden)
    for k, bias in enumerate(biases):
        small_ref[SUMS + k : SUMS + k + 1, half] = bias[...]


def norm_back(info, x, u, gain, g0, g1, g2, g3, sums, biases, after=()):
    small = (SUMS + len(biases), x.shape[1])
    return call(
        norm_back_kernel,
        (info, x, u, gain, g0, g1, g2, g3, sums, *biases),
        (struct(x.shape, F32), struct(small, F32)),
        after=after,
    )


def small_kernel(axis, bit, mine, other, out):
    if axis == "dp":
        out[...] = mine[...] + other[...]
        return
    out[:SUMS, :] = mine[:SUMS, :] + other[:SUMS, :]
    step = (1 << bit) // 2
    for k in range(mine.shape[0] - SUMS):
        row = slice(SUMS + k, SUMS + k + 1)
        if step and not k & step:
            twin = SUMS + (k | step)
            out[row, :] = mine[row, :] + other[twin : twin + 1, :]
        else:
            out[row, :] = mine[row, :]


def small_sum(small, axis, bit):
    other = exchange(small, axis, 1 << bit)
    return call(partial(small_kernel, axis, bit), (small, other), struct(small.shape, F32))


def row_out_kernel(info, x_ref, sum_ref, g1, g2, g3, bias_ref, out_ref):
    rows, width = x_ref.shape
    step = 64
    for r in range(0, rows, step):
        here = slice(r, r + step)
        branch = sum_ref[here, :] + g1[1, 0, here, :].astype(F32) + g2[1, 0, here, :].astype(F32)
        branch = branch + g3[0, here, :].astype(F32) + bias_ref[...]
        where = lax.broadcasted_iota(jnp.int32, (step, width), 0) + r
        branch = jnp.where(where < info[LIVE : LIVE + 1, 0:1], branch, 0.0)
        out_ref[here, :] = (x_ref[here, :].astype(F32) + branch).astype(BF)


def row_out(info, x, attention_out, g1, g2, g3, bias, after=()):
    return call(
        row_out_kernel,
        (info, x, attention_out, g1, g2, g3, bias),
        struct(x.shape, BF),
        after=after,
    )


def attend_final_kernel(scale, small_ref, *refs):
    parts, (attend, output) = refs[:-2], refs[-2:]
    depth = len(parts)
    cols = parts[0].shape[2]
    edge = 3 * depth // 4
    factor = scale / small_ref[3:4, 0:1]
    for j, part in enumerate(parts):
        place = places()[2] ^ j
        value = part[0].astype(F32) * factor

        @pl.when(place < edge)
        def inner():
            attend[:, pl.ds(pl.multiple_of(place * cols, 128), cols)] = value

        @pl.when(place >= edge)
        def outer():
            output[:, pl.ds(pl.multiple_of((place - edge) * cols, 128), cols)] = value


def attend_final(scale, small, parts):
    _, half, cols = parts[0].shape
    depth = len(parts)
    attend, output = (half, 3 * depth // 4 * cols), (half, depth // 4 * cols)
    return call(
        partial(attend_final_kernel, scale),
        (small, *parts),
        (struct(attend, F32), struct(output, F32)),
    )


def row_final_kernel(scale, small_ref, grad_ref, out_ref, gain, shift, bias, expand):
    factor = scale / small_ref[3:4, 0:1]
    out_ref[...] = grad_ref[...] * factor
    gain[...] = small_ref[0:1, :] * factor
    shift[...] = small_ref[1:2, :] * factor
    bias[...] = small_ref[2:3, :] * factor
    expand[...] = small_ref[SUMS : SUMS + 1, : expand.shape[1]] * factor


def row_final(scale, small, grad, shard):
    row = struct((1, grad.shape[1]), F32)
    return call(
        partial(row_final_kernel, scale),
        (small, grad),
        (struct(grad.shape, F32), row, row, row, struct((1, shard), F32)),
    )


def feed_final_kernel(scale, narrow, small_ref, mine, sibling, expand, shrink):
    hidden = mine.shape[2 if narrow else 1]
    factor = scale / small_ref[3:4, 0:1]
    for n, part in enumerate((mine, sibling)):
        start = pl.multiple_of((places()[0] ^ n) * hidden, 128)
        first, second = part[0].astype(F32), part[1].astype(F32)
        expand[:, pl.ds(start, hidden)] = (first if narrow else first.T) * factor
        shrink[pl.ds(start, hidden), :] = (second.T if narrow else second) * factor


def feed_final(scale, small, mine, sibling, half):
    narrow = half % 128 != 0
    hidden = mine.shape[2 if narrow else 1]
    return call(
        partial(feed_final_kernel, scale, narrow),
        (small, mine, sibling),
        (struct((half, 2 * hidden), F32), struct((2 * hidden, half), F32)),
    )


def add_kernel(plan, *refs):
    ins = refs[: len(refs) - len(plan)]
    for out, (_, parts) in zip(refs[len(ins) :], plan):
        for p, part in enumerate(parts):
            out[p] = sum(ins[n][index].astype(F32) for n, index in part).astype(out.dtype)


def add(plan, after=()):
    arrays, outs, inner = [], [], []
    for dtype, parts in plan:
        entries = []
        for part in parts:
            entry = []
            for array, index in part:
                n = next((n for n, a in enumerate(arrays) if a is array), len(arrays))
                if n == len(arrays):
                    arrays.append(array)
                entry.append((n, index))
            entries.append(entry)
        inner.append((dtype, entries))
        array, index = parts[0][0]
        outs.append(struct((len(parts), *array.shape[len(index) :]), dtype))
    return call(partial(add_kernel, inner), tuple(arrays), tuple(outs), after=after)


def exchange(x, axis, flip):
    n = lax.axis_size(axis)
    return lax.ppermute(x, axis, [(i, i ^ flip) for i in range(n)])


def reduce_chips(chips, low, high, afters):
    bits = list(range(chips.bit_length() - 1))
    orders = (bits, bits[::-1])
    left = []
    for (send, keep), order in zip((low, high), orders):
        got = exchange(send, "dp", 2 << order[0])
        left.append([[(keep, (i,)), (got, (i,))] for i in range(chips // 2)])
    sends = ()
    for n in range(1, len(bits)):
        stay, go = [], []
        for entries, order in zip(left, orders):
            if order[0] == 0:
                stay.append(entries[0::2])
                go.append(entries[1::2])
            else:
                stay.append(entries[: len(entries) // 2])
                go.append(entries[len(entries) // 2 :])
        sends = add([(BF, g) for g in go], after=afters)
        left = []
        for entries, send, order in zip(stay, sends, orders):
            got = exchange(send, "dp", 2 << order[n])
            left.append([e + [(got, (i,))] for i, e in enumerate(entries)])
    return (left[0][0], left[1][0]), sends


def behind(x, *others):
    return lax.optimization_barrier((x, *others))[0]


def at(entry, *index):
    return [(array, first + index) for array, first in entry]


def local(
    residual_in,
    upstream,
    layer_norm_gain,
    layer_norm_bias,
    attend_weight,
    output_weight,
    expand_weight,
    expand_bias,
    shrink_weight,
    shrink_bias,
    seq_lengths,
    terminal_pos,
    window_offset,
):
    rows, width = residual_in.shape
    data_ways, depth = lax.axis_size("dp"), lax.axis_size("mp")
    chips = data_ways // 2
    shards = depth // 2
    shard = expand_weight.shape[1]
    hidden = shard // 2
    gain = layer_norm_gain[None, :]
    packed = pack(chips, expand_bias[None, :], expand_weight, shrink_weight)
    shares = [exchange(packed, "mp", 2 * k) for k in range(1, shards)]
    info, normed, bg, shrink_bias_grad = prepare(
        seq_lengths,
        terminal_pos,
        window_offset,
        residual_in,
        upstream,
        gain,
        layer_norm_bias[None, :],
        after=(packed,),
    )
    tok = (normed, bg)
    tok_core = [exchange(t, "dp", 1) for t in tok]

    sides = attention(info, normed, bg, attend_weight, output_weight)
    grad_attention, attention_out = attention_back(sides, attend_weight, output_weight)
    deep_normed = exchange(normed, "mp", 1)
    sides_core = exchange(
        behind(sides, grad_attention, *shares, *tok_core, deep_normed), "dp", 1
    )
    tok_deep = [deep_normed, exchange(behind(bg, sides), "mp", 1)]
    foreign = [[s] + [exchange(s, "dp", 2 * j) for j in range(1, chips)] for s in shares]
    attn = attention_grads(chips, depth, tok, tok_core, sides, sides_core, after=shares)
    tok_both = [exchange(behind(t, attn[0]), "dp", 1) for t in tok_deep]
    attn = [behind(a, *tok_both) for a in attn]
    toks = (*tok, *tok_core, *tok_deep, *tok_both)

    weights = (expand_weight, shrink_weight)
    own = feed(chips, toks, weights, expand_bias[None, :], hidden, after=attn[:1])
    others = [feed(chips, toks, pieces, None, hidden, after=own[:1]) for pieces in foreign]
    sets = [(own[0], own[1], weights)]
    sets += [(o[0], o[1], pieces) for o, pieces in zip(others, foreign)]
    attn_sums, sent = reduce_chips(chips, attn[:2], attn[2:], (others[-1][2],))
    keep, send = feed_out(chips, sets, after=sent)
    passed = exchange(send, "dp", 1)
    crossing = add([(BF, [[(keep, (m, 1)), (passed, (m, 1))]]) for m in range(2)])
    crossed_grad, crossed_out = (exchange(c, "mp", 1) for c in crossing)

    middle = depth // 2
    entries = [at(attn_sums[z // middle], z % middle) for z in range(depth)]
    parts = add([(BF, [e]) for e in entries[1:]])
    arrived = [(exchange(p, "mp", j + 1), (0,)) for j, p in enumerate(parts)]
    attn_own = add([(BF, [entries[0] + arrived])])[0]
    attn_all = [attn_own] + [exchange(attn_own, "mp", j) for j in range(1, depth)]

    mine, away = [[], []], [[], []]
    for k, f in enumerate((*others, own)):
        pair, _ = reduce_chips(chips, f[3:5], f[5:7], (keep,))
        if k < len(others):
            both = add([(BF, [at(p, a) for p in pair for a in range(2)])])[0]
            both = exchange(both, "mp", 2 * (k + 1))
            pair = [[(both, (2 * n,))] for n in range(2)], [[(both, (2 * n + 1,))] for n in range(2)]
        else:
            pair = [at(p, 0) for p in pair], [at(p, 1) for p in pair]
        for n in range(2):
            mine[n] = mine[n] + pair[0][n]
            away[n] = away[n] + pair[1][n]
    mine, away = add([(F32, mine), (BF, away)])
    sibling = exchange(away, "dp", 1)

    grad_rows, small = norm_back(
        info,
        residual_in,
        upstream,
        gain,
        grad_attention,
        keep,
        passed,
        crossed_grad,
        shrink_bias_grad,
        [f[2] for f in (own, *others)],
    )
    residual_out = row_out(
        info, residual_in, attention_out, keep, passed, crossed_out, shrink_bias[None, :]
    )
    for bit in range(depth.bit_length() - 1):
        small = small_sum(small, "mp", bit)
    for bit in range(data_ways.bit_length() - 1):
        small = small_sum(small, "dp", bit)

    factor = float(data_ways * depth)
    attend_sum, output_sum = attend_final(factor, small, attn_all)
    expand_sum, shrink_sum = feed_final(factor, small, mine, sibling, width // data_ways)
    grad_rows, gain_sum, shift_sum, bias_sum, expand_bias_sum = row_final(
        factor, small, grad_rows, shard
    )
    return (
        residual_out,
        grad_rows,
        gain_sum[0],
        shift_sum[0],
        attend_sum,
        output_sum,
        expand_sum,
        expand_bias_sum[0],
        shrink_sum,
        bias_sum[0],
    )


def solution(mesh):
    in_specs = (
        P(("dp", "mp"), None),
        P(("dp", "mp"), None),
        P(),
        P(),
        P(),
        P(),
        P(None, "mp"),
        P("mp"),
        P("mp", None),
        P(),
        P("dp", None),
        P("dp", "mp"),
        P("dp", "mp"),
    )
    out_specs = (
        P(("dp", "mp"), None),
        P(("dp", "mp"), None),
        P(),
        P(),
        P("dp", None),
        P("dp", None),
        P("dp", "mp"),
        P("mp"),
        P("mp", "dp"),
        P(),
    )
    return jax.shard_map(local, mesh=mesh, in_specs=in_specs, out_specs=out_specs, check_vma=False)
```

time: 437 us -> 208 us (0.48); the launches traced: 431 us -> 208 us
  waiting for transfers between devices: 192 us -> 111 us
  matrix products: 72.4 us -> 0 us
  local copies, waits for them, and re-layouts: 72.1 us -> 4.48 us
  blocking collectives: 50.1 us -> 0 us
  Pallas kernels: 0 us -> 48.6 us
  starting transfers between devices: 1.49 us -> 43.1 us
  other arithmetic: 26.9 us -> 0.01 us
  between operations: 16.2 us -> 0.98 us
    ppermute x0 -> x39, waiting for transfers between devices: none -> 111 us  [exchange(): return lax.ppermute(x, axis, [(i, i ^ flip) for i in range(n)])]
    reduce_scatter x5 -> x0, waiting for transfers between devices: 73.4 us -> none  [the longest x1 42.8 us: local(): lax.psum_scatter(jnp.dot(row_slice, shrink_weight, preferred_element_type...]
    dot_general x18 -> x0, matrix products: 72.4 us -> none  [the longest x4 18.3 us: contract_cols(): lax.dot_general(left, right, (((1,), (1,)), ((), ())), preferred_element_...]
    all_gather x2 -> x0, waiting for transfers between devices: 67.7 us -> none  [the longest x1 40.3 us: local(): gathered_grad = lax.all_gather(branch_grad, 'mp', axis=0, tiled=True)]
    psum x1 -> x0, waiting for transfers between devices: 50.4 us -> none  [local(): lax.psum(attention_piece.astype(jnp.bfloat16), 'mp').astype(jnp.float32)]
    psum x3 -> x0, blocking collectives: 50.1 us -> none  [the longest x1 24.8 us: local(): lax.psum((small_local, expand_bias_grad), 'dp')]
    pallas_call x0 -> x26, Pallas kernels: none -> 48.6 us  [call(): pl.pallas_call(body, in_specs=[specs.get(n, VMEM) for n in range(count)]...]
    ppermute x0 -> x39, starting transfers between devices: none -> 43.1 us  [exchange(): return lax.ppermute(x, axis, [(i, i ^ flip) for i in range(n)])]
  transfers between devices with their start and end apart: 8 -> 39, of which waited for: 5 -> 20; matrix products, arithmetic and copies ran while one was open for 35% -> 0% of each run, Pallas kernels for 0% -> 19%
where the time goes in v2:
time: 208 us
  waiting for transfers between devices  111 us (53%)
  Pallas kernels  48.6 us (23%)
  starting transfers between devices  43.1 us (21%)
  local copies, waits for them, and re-layouts  4.48 us (2%)
    ppermute x39, waiting for transfers between devices, exchange(): return lax.ppermute(x, axis, [(i, i ^ flip) for i in range(n)])  111 us
    pallas_call x26, Pallas kernels, call(): pl.pallas_call(body, in_specs=[specs.get(n, VMEM) for n in range(count)]...  48.6 us
    ppermute x39, starting transfers between devices, exchange(): return lax.ppermute(x, axis, [(i, i ^ flip) for i in range(n)])  43.1 us
    unnamed x38, local copies, waits for them, and re-layouts  4.48 us
  transfers between devices with their start and end apart: 39, of which 20 were waited for; matrix products, arithmetic and copies ran while one was open for 0% of the time, Pallas kernels for 19%

profile of v2, /device:TPU:0, one launch (start us, length us, event | category | flops | bytes accessed | tf_op | source)
XLA Modules:
  0.0 208.0 jit_solution(8909228884056240214)
XLA Ops:
  0.7 1.9 shard_map.213.refs_7_
  2.6 4.1 %collective-permute-start.4 = (bf16[272,1024]{1,0:T(8,128)(2,1)}, bf16[272,1024]{1,0:T(8,128)(2,1)S(1)}, u32[]{:S(2)}, u32[]{:S(2)}) collective-permute-start(bf16[272,1024]{1,0:T(8,128)(2,1)} %shard_map.213.refs_7_), channel_id=1, source_target_pairs={{0,2},{1,3},{2,0},{3,1},{4,6},{5,7},{6,4},{7,5},{8,10},{9,11},{10,... | collective-permute-start | bytes 1671176 | tf_op jit(solution)/shard_map/ppermute | solution.py:842
  6.7 3.4 %shard_map.214 = (s32[24,256]{1,0:T(8,128)}, bf16[256,1024]{1,0:T(8,128)(2,1)}, bf16[256,1024]{1,0:T(8,128)(2,1)}, f32[1,1024]{1,0:T(1,128)}) custom-call(s32[1,16]{1,0:T(1,128)} %refs_0_.1, s32[1,4]{1,0:T(1,128)} %refs_1_.6, s32[1,4]{1,0:T(1,128)} %refs_2_.6, bf16[256,1024]{1,0:T(8,128)(2,1)} %refs_1_.9, bf16[256,1024]{1,0:T(8,128)(2,1)} %refs_2_.9, ...), custom_call_target="tpu_custom_call" | custom-call | flops 100000000 | bytes 1024 | tf_op jit(solution)/shard_map/pallas_call | solution.py:46
  10.1 1.6 collective-permute-start.2
  15.1 11.7 %shard_map.215.refs_0_.refs_4_ = bf16[4,256,1024]{2,1,0:T(8,128)(2,1)} custom-call(s32[24,256]{1,0:T(8,128)S(1)} %copy-done.11, bf16[256,1024]{1,0:T(8,128)(2,1)S(1)} %copy-done.6, bf16[256,1024]{1,0:T(8,128)(2,1)S(1)} %copy-done.7, f32[1,256]{1,0:T(1,128)S(1)} %copy-done.16, bf16[1024,3072]{1,0:T(8,128)(2,1)} %refs_1_.7, bf16[1024,1024]{1,0:T(8,128)(2,1)} %refs_2_.7), custom_call_target="tpu_custom_call" | custom-call | flops 100000000 | bytes 1024 | tf_op jit(solution)/shard_map/pallas_call | solution.py:46
  26.8 1.6 copy-done
  28.4 3.4 %shard_map.216 = (f32[256,1024]{1,0:T(8,128)S(1)}, f32[256,1024]{1,0:T(8,128)S(1)}) custom-call(bf16[4,256,1024]{2,1,0:T(8,128)(2,1)S(1)} %copy-done, bf16[1024,3072]{1,0:T(8,128)(2,1)S(1)} %bitcast.9, bf16[1024,1024]{1,0:T(8,128)(2,1)S(1)} %copy-done.4), custom_call_target="tpu_custom_call" | custom-call | flops 100000000 | bytes 1024 | tf_op jit(solution)/shard_map/pallas_call | solution.py:46
  31.8 2.7 %collective-permute-done.2.refs_4_ = bf16[256,1024]{1,0:T(8,128)(2,1)S(1)} collective-permute-done((bf16[256,1024]{1,0:T(8,128)(2,1)}, bf16[256,1024]{1,0:T(8,128)(2,1)S(1)}, u32[]{:S(2)}, u32[]{:S(2)}) %collective-permute-start.2) | collective-permute-done | bytes 524320 | tf_op jit(solution)/shard_map/ppermute | solution.py:842
  34.8 2.6 %collective-permute-start.10 = (bf16[272,1024]{1,0:T(8,128)(2,1)S(1)}, bf16[272,1024]{1,0:T(8,128)(2,1)S(1)}, u32[]{:S(2)}, u32[]{:S(2)}) collective-permute-start(bf16[272,1024]{1,0:T(8,128)(2,1)S(1)} %collective-permute-done.4.refs_6_.refs_8_), channel_id=1, source_target_pairs={{0,24},{4,28},{8,16},{12,20},{16,8},{20,12},{24,0},{28,4},{1,25},{... | collective-permute-start | bytes 1671176 | tf_op jit(solution)/shard_map/ppermute | solution.py:842
  38.8 2.8 %shard_map.217 = (bf16[2,2,128,1024]{3,2,1,0:T(8,128)(2,1)S(1)}, bf16[2,2,128,1024]{3,2,1,0:T(8,128)(2,1)S(1)}, bf16[2,2,128,1024]{3,2,1,0:T(8,128)(2,1)S(1)}, bf16[2,2,128,1024]{3,2,1,0:T(8,128)(2,1)S(1)}) custom-call(bf16[256,1024]{1,0:T(8,128)(2,1)S(1)} %copy-done.6, bf16[256,1024]{1,0:T(8,128)(2,1)S(1)} %collective-permute-done.refs_1_.refs_2_, ...), custom_call_target="tpu_custom_call" | custom-call | flops 100000000 | bytes 1024 | tf_op jit(solution)/shard_map/pallas_call | solution.py:46
  41.6 7.4 %collective-permute-done.3.refs_5_ = bf16[256,1024]{1,0:T(8,128)(2,1)S(1)} collective-permute-done((bf16[256,1024]{1,0:T(8,128)(2,1)S(1)}, bf16[256,1024]{1,0:T(8,128)(2,1)S(1)}, u32[]{:S(2)}, u32[]{:S(2)}) %collective-permute-start.3) | collective-permute-done | bytes 524320 | tf_op jit(solution)/shard_map/ppermute | solution.py:842
  49.5 1.4 collective-permute-done.6.refs_6_
  51.7 1.5 collective-permute-start.11
  53.2 1.5 collective-permute-start.12
  54.7 6.0 %shard_map.218 = (bf16[1024,512]{1,0:T(8,128)(2,1)S(1)}, bf16[1024,512]{1,0:T(8,128)(2,1)S(1)}, f32[1,512]{1,0:T(1,128)S(1)}, bf16[2,2,512,128]{3,2,1,0:T(8,128)...) custom-call(bf16[256,1024]{1,0:T(8,128)(2,1)S(1)} %copy-done.6, ...), custom_call_target="tpu_custom_call" | custom-call | flops 100000000 | bytes 1024 | tf_op jit(solution)/shard_map/pallas_call | solution.py:46
  60.7 1.9 collective-permute-done.9.refs_10_.refs_8_
  63.2 6.1 %shard_map.219 = (bf16[1024,512]{1,0:T(8,128)(2,1)S(1)}, bf16[1024,512]{1,0:T(8,128)(2,1)S(1)}, f32[1,512]{1,0:T(1,128)S(1)}, bf16[2,2,512,128]{3,2,1,0:T(8,128)...) custom-call(bf16[256,1024]{1,0:T(8,128)(2,1)S(1)} %copy-done.6, ...), custom_call_target="tpu_custom_call" | custom-call | flops 20000000000 | bytes 1024 | tf_op jit(solution)/shard_map/pallas_call | solution.py:46
  69.3 15.8 %collective-permute-done.11.refs_1_ = bf16[2,2,128,1024]{3,2,1,0:T(8,128)(2,1)S(1)} collective-permute-done((bf16[2,2,128,1024]{3,2,1,0:T(8,128)(2,1)S(1)}, bf16[2,2,128,1024]{3,2,1,0:T(8,128)(2,1)S(1)}, u32[]{:S(2)}, u32[]{:S(2)}) %collective-permute-start.11) | collective-permute-done | bytes 1048608 | tf_op jit(solution)/shard_map/ppermute | solution.py:842
  85.4 5.4 %shard_map.221 = (bf16[2,2,256,1024]{3,2,1,0:T(8,128)(2,1)S(1)}, bf16[2,2,256,1024]{3,2,1,0:T(8,128)(2,1)S(1)}) custom-call(bf16[1024,512]{1,0:T(8,128)(2,1)S(1)} %get-tuple-element.79.refs_12_.refs_0_, bf16[1024,512]{1,0:T(8,128)(2,1)S(1)} %get-tuple-element.80.refs_1_, bf16[1024,1024]{1,0:T(8,128)(2,1)S(1)} %copy-done.2, bf16[1024,1024]{1,0:T(8,128)(2,1)S(1)} %copy-done.3, ...), custom_call_target="tpu_custom_call" | custom-call | flops 100000000 | bytes 1024 | tf_op jit(solution)/shard_map/pallas_call | solution.py:46
  90.9 1.6 collective-permute-start.29
  93.1 1.9 collective-permute-done.13.refs_1_.refs_4_.refs_6_
  95.3 1.8 collective-permute-start.15
  97.1 8.1 %collective-permute-done.29.refs_1_ = bf16[2,2,512,128]{3,2,1,0:T(8,128)(2,1)S(1)} collective-permute-done((bf16[2,2,512,128]{3,2,1,0:T(8,128)(2,1)S(1)}, bf16[2,2,512,128]{3,2,1,0:T(8,128)(2,1)S(1)}, u32[]{:S(2)}, u32[]{:S(2)}) %collective-permute-start.29) | collective-permute-done | bytes 524320 | tf_op jit(solution)/shard_map/ppermute | solution.py:842
  105.3 1.2 collective-permute-done.30.refs_3_.refs_4_
  107.4 1.3 collective-permute-start.34
  109.3 1.4 collective-permute-start.21
  110.7 5.3 %collective-permute-done.31.refs_2_ = bf16[1,2,512,128]{3,2,1,0:T(8,128)(2,1)S(1)} collective-permute-done((bf16[1,2,512,128]{3,2,1,0:T(8,128)(2,1)S(1)}, bf16[1,2,512,128]{3,2,1,0:T(8,128)(2,1)S(1)}, u32[]{:S(2)}, u32[]{:S(2)}) %collective-permute-start.31) | collective-permute-done | bytes 262176 | tf_op jit(solution)/shard_map/ppermute | solution.py:842
  116.5 1.5 collective-permute-start.22
  119.1 8.8 %collective-permute-done.32.refs_5_ = bf16[1,2,512,128]{3,2,1,0:T(8,128)(2,1)S(1)} collective-permute-done((bf16[1,2,512,128]{3,2,1,0:T(8,128)(2,1)S(1)}, bf16[1,2,512,128]{3,2,1,0:T(8,128)(2,1)S(1)}, u32[]{:S(2)}, u32[]{:S(2)}) %collective-permute-start.32) | collective-permute-done | bytes 262176 | tf_op jit(solution)/shard_map/ppermute | solution.py:842
  127.8 1.8 collective-permute-start.16
  129.8 1.3 collective-permute-start.33
  131.2 1.4 collective-permute-start.36
  133.1 5.3 %collective-permute-done.21.refs_2_ = bf16[1,2,128,1024]{3,2,1,0:T(8,128)(2,1)S(1)} collective-permute-done((bf16[1,2,128,1024]{3,2,1,0:T(8,128)(2,1)S(1)}, bf16[1,2,128,1024]{3,2,1,0:T(8,128)(2,1)S(1)}, u32[]{:S(2)}, u32[]{:S(2)}) %collective-permute-start.21) | collective-permute-done | bytes 524320 | tf_op jit(solution)/shard_map/ppermute | solution.py:842
  138.4 2.7 %collective-permute-start.17 = (f32[6,1024]{1,0:T(8,128)S(1)}, f32[6,1024]{1,0:T(8,128)S(1)}, u32[]{:S(2)}, u32[]{:S(2)}) collective-permute-start(f32[6,1024]{1,0:T(8,128)S(1)} %shard_map.225.refs_0_), channel_id=1, source_target_pairs={{0,2},{1,3},{2,0},{3,1},{4,6},{5,7},{6,4},{7,5},{8,10},{9,11},{10,... | collective-permute-start | bytes 73736 | tf_op jit(solution)/shard_map/ppermute | solution.py:842
  141.1 11.9 %collective-permute-done.17.refs_1_ = f32[6,1024]{1,0:T(8,128)S(1)} collective-permute-done((f32[6,1024]{1,0:T(8,128)S(1)}, f32[6,1024]{1,0:T(8,128)S(1)}, u32[]{:S(2)}, u32[]{:S(2)}) %collective-permute-start.17) | collective-permute-done | bytes 24608 | tf_op jit(solution)/shard_map/ppermute | solution.py:842
  153.4 2.1 %collective-permute-start.23 = (bf16[1,128,1024]{2,1,0:T(8,128)(2,1)S(1)}, bf16[1,128,1024]{2,1,0:T(8,128)(2,1)S(1)}, u32[]{:S(2)}, u32[]{:S(2)}) collective-permute-start(bf16[1,128,1024]{2,1,0:T(8,128)(2,1)S(1)} %get-tuple-element.103), channel_id=1, source_target_pairs={{0,1},{1,0},{2,3},{3,2},{4,5},{5,4},{6,7},{7,6},{8,9},{9,8},{10,11... | collective-permute-start | bytes 786440 | tf_op jit(solution)/shard_map/ppermute | solution.py:842
  156.4 1.5 collective-permute-start.25
  157.9 1.3 collective-permute-start.19
  159.5 18.7 %collective-permute-done.23.refs_3_ = bf16[1,128,1024]{2,1,0:T(8,128)(2,1)S(1)} collective-permute-done((bf16[1,128,1024]{2,1,0:T(8,128)(2,1)S(1)}, bf16[1,128,1024]{2,1,0:T(8,128)(2,1)S(1)}, u32[]{:S(2)}, u32[]{:S(2)}) %collective-permute-start.23) | collective-permute-done | bytes 262176 | tf_op jit(solution)/shard_map/ppermute | solution.py:842
  178.2 5.8 %collective-permute-done.25.refs_5_ = bf16[1,128,1024]{2,1,0:T(8,128)(2,1)S(1)} collective-permute-done((bf16[1,128,1024]{2,1,0:T(8,128)(2,1)S(1)}, bf16[1,128,1024]{2,1,0:T(8,128)(2,1)S(1)}, u32[]{:S(2)}, u32[]{:S(2)}) %collective-permute-start.25) | collective-permute-done | bytes 262176 | tf_op jit(solution)/shard_map/ppermute | solution.py:842
  184.1 1.7 collective-permute-start.28
  185.9 2.7 %collective-permute-start.26 = (bf16[1,128,1024]{2,1,0:T(8,128)(2,1)S(1)}, bf16[1,128,1024]{2,1,0:T(8,128)(2,1)S(1)}, u32[]{:S(2)}, u32[]{:S(2)}) collective-permute-start(bf16[1,128,1024]{2,1,0:T(8,128)(2,1)S(1)} %shard_map.232.refs_1_), channel_id=1, source_target_pairs={{0,1},{1,0},{2,3},{3,2},{4,5},{5,4},{6,7},{7,6},{8,9},{9,8},{10,11... | collective-permute-start | bytes 786440 | tf_op jit(solution)/shard_map/ppermute | solution.py:842
  188.6 1.4 collective-permute-start.20
  190.0 1.3 shard_map.223
  191.3 1.3 collective-permute-done.20.refs_1_
  192.6 1.1 shard_map.230
  195.4 11.0 %collective-permute-done.27.refs_3_ = bf16[1,128,1024]{2,1,0:T(8,128)(2,1)S(1)} collective-permute-done((bf16[1,128,1024]{2,1,0:T(8,128)(2,1)S(1)}, bf16[1,128,1024]{2,1,0:T(8,128)(2,1)S(1)}, u32[]{:S(2)}, u32[]{:S(2)}) %collective-permute-start.27) | collective-permute-done | bytes 262176 | tf_op jit(solution)/shard_map/ppermute | solution.py:842
  206.3 1.7 shard_map.233
  (95 shorter events, 15.5 us)
Async XLA Ops:
  0.6 11.6 %copy-start.16 = (f32[1,256]{1,0:T(1,128)S(1)}, f32[1,256]{1,0:T(1,128)}, u32[]{:S(2)}) copy-start(f32[1,256]{1,0:T(1,128)} %constant.2.clone.refs_3_) | copy-start | bytes 3076
  2.6 32.0 %collective-permute-start.4 = (bf16[272,1024]{1,0:T(8,128)(2,1)}, bf16[272,1024]{1,0:T(8,128)(2,1)S(1)}, u32[]{:S(2)}, u32[]{:S(2)}) collective-permute-start(bf16[272,1024]{1,0:T(8,128)(2,1)} %shard_map.213.refs_7_), channel_id=1, source_target_pairs={{0,2},{1,3},{2,0},{3,1},{4,6},{5,7},{6,4},{7,5},{8,10},{9,11},{10,... | collective-permute-start | bytes 1671176 | tf_op jit(solution)/shard_map/ppermute | solution.py:842
  6.7 20.1 %slice-start = ((s8[6291456]{0:T(1024)(128)(4,1)}), s8[2097152]{0:T(1024)(128)(4,1)S(1)}, s32[]{:S(2)}) async-start(s8[6291456]{0:T(1024)(128)(4,1)} %bitcast.8), calls=%async_computation | async-start | bytes 4194304
  10.1 24.4 %collective-permute-start.2 = (bf16[256,1024]{1,0:T(8,128)(2,1)}, bf16[256,1024]{1,0:T(8,128)(2,1)S(1)}, u32[]{:S(2)}, u32[]{:S(2)}) collective-permute-start(bf16[256,1024]{1,0:T(8,128)(2,1)} %get-tuple-element.69.refs_1_.refs_0_), channel_id=1, source_target_pairs={{0,1},{1,0},{2,3},{3,2},{4,5},{5,4},{6,7},{7,6},{8,9},{9,8},{10,11... | collective-permute-start | bytes 1572872 | tf_op jit(solution)/shard_map/ppermute | solution.py:842
  11.8 22.8 %collective-permute-start = (bf16[256,1024]{1,0:T(8,128)(2,1)}, bf16[256,1024]{1,0:T(8,128)(2,1)S(1)}, u32[]{:S(2)}, u32[]{:S(2)}) collective-permute-start(bf16[256,1024]{1,0:T(8,128)(2,1)} %get-tuple-element.69.refs_1_.refs_0_), channel_id=1, source_target_pairs={{0,4},{4,0},{8,12},{12,8},{16,20},{20,16},{24,28},{28,24},{1,5},{5... | collective-permute-start | bytes 1572872 | tf_op jit(solution)/shard_map/ppermute | solution.py:842
  11.8 22.8 %collective-permute-start.1 = (bf16[256,1024]{1,0:T(8,128)(2,1)}, bf16[256,1024]{1,0:T(8,128)(2,1)S(1)}, u32[]{:S(2)}, u32[]{:S(2)}) collective-permute-start(bf16[256,1024]{1,0:T(8,128)(2,1)} %get-tuple-element.72.refs_2_.refs_1_), channel_id=1, source_target_pairs={{0,4},{4,0},{8,12},{12,8},{16,20},{20,16},{24,28},{28,24},{1,5},{5... | collective-permute-start | bytes 1572872 | tf_op jit(solution)/shard_map/ppermute | solution.py:842
  15.1 11.7 %slice-start.1 = ((s8[6291456]{0:T(1024)(128)(4,1)}), s8[4194304]{0:T(1024)(128)(4,1)S(1)}, s32[]{:S(2)}) async-start(s8[6291456]{0:T(1024)(128)(4,1)} %bitcast.8), calls=%async_computation.1 | async-start | bytes 8388608
  15.1 11.7 %copy-start.4 = (bf16[1024,1024]{1,0:T(8,128)(2,1)S(1)}, bf16[1024,1024]{1,0:T(8,128)(2,1)}, u32[]{:S(2)}) copy-start(bf16[1024,1024]{1,0:T(8,128)(2,1)} %refs_2_.7) | copy-start | bytes 6291460
  34.6 20.2 %copy-start.2 = (bf16[1024,1024]{1,0:T(8,128)(2,1)S(1)}, bf16[1024,1024]{1,0:T(8,128)(2,1)}, u32[]{:S(2)}) copy-start(bf16[1024,1024]{1,0:T(8,128)(2,1)} %refs_2_.8) | copy-start | bytes 6291460
  34.6 20.2 %copy-start.3 = (bf16[1024,1024]{1,0:T(8,128)(2,1)S(1)}, bf16[1024,1024]{1,0:T(8,128)(2,1)}, u32[]{:S(2)}) copy-start(bf16[1024,1024]{1,0:T(8,128)(2,1)} %refs_3_.4) | copy-start | bytes 6291460
  34.6 20.2 %copy-start.13 = (f32[1024]{0:T(1024)S(1)}, f32[1024]{0:T(1024)}, u32[]{:S(2)}) copy-start(f32[1024]{0:T(1024)} %param.21) | copy-start | bytes 12292
  34.6 4.2 %collective-permute-start.5 = (bf16[4,256,1024]{2,1,0:T(8,128)(2,1)S(1)}, bf16[4,256,1024]{2,1,0:T(8,128)(2,1)S(1)}, u32[]{:S(2)}, u32[]{:S(2)}) collective-permute-start(bf16[4,256,1024]{2,1,0:T(8,128)(2,1)S(1)} %copy-done), channel_id=1, source_target_pairs={{0,4},{4,0},{8,12},{12,8},{16,20},{20,16},{24,28},{28,24},{1,5},{5... | collective-permute-start | bytes 6291464 | tf_op jit(solution)/shard_map/ppermute | solution.py:842
  34.7 14.3 %collective-permute-start.3 = (bf16[256,1024]{1,0:T(8,128)(2,1)S(1)}, bf16[256,1024]{1,0:T(8,128)(2,1)S(1)}, u32[]{:S(2)}, u32[]{:S(2)}) collective-permute-start(bf16[256,1024]{1,0:T(8,128)(2,1)S(1)} %copy-done.7), channel_id=1, source_target_pairs={{0,1},{1,0},{2,3},{3,2},{4,5},{5,4},{6,7},{7,6},{8,9},{9,8},{10,11... | collective-permute-start | bytes 1572872 | tf_op jit(solution)/shard_map/ppermute | solution.py:842
  34.8 26.0 %collective-permute-start.10 = (bf16[272,1024]{1,0:T(8,128)(2,1)S(1)}, bf16[272,1024]{1,0:T(8,128)(2,1)S(1)}, u32[]{:S(2)}, u32[]{:S(2)}) collective-permute-start(bf16[272,1024]{1,0:T(8,128)(2,1)S(1)} %collective-permute-done.4.refs_6_.refs_8_), channel_id=1, source_target_pairs={{0,24},{4,28},{8,16},{12,20},{16,8},{20,12},{24,0},{28,4},{1,25},{... | collective-permute-start | bytes 1671176 | tf_op jit(solution)/shard_map/ppermute | solution.py:842
  37.3 25.3 %collective-permute-start.9 = (bf16[272,1024]{1,0:T(8,128)(2,1)S(1)}, bf16[272,1024]{1,0:T(8,128)(2,1)S(1)}, u32[]{:S(2)}, u32[]{:S(2)}) collective-permute-start(bf16[272,1024]{1,0:T(8,128)(2,1)S(1)} %collective-permute-done.4.refs_6_.refs_8_), channel_id=1, source_target_pairs={{0,16},{4,20},{8,24},{12,28},{16,0},{20,4},{24,8},{28,12},{1,17},{... | collective-permute-start | bytes 1671176 | tf_op jit(solution)/shard_map/ppermute | solution.py:842
  37.8 25.4 %collective-permute-start.8 = (bf16[272,1024]{1,0:T(8,128)(2,1)S(1)}, bf16[272,1024]{1,0:T(8,128)(2,1)S(1)}, u32[]{:S(2)}, u32[]{:S(2)}) collective-permute-start(bf16[272,1024]{1,0:T(8,128)(2,1)S(1)} %collective-permute-done.4.refs_6_.refs_8_), channel_id=1, source_target_pairs={{0,8},{4,12},{8,0},{12,4},{16,24},{20,28},{24,16},{28,20},{1,9},{5... | collective-permute-start | bytes 1671176 | tf_op jit(solution)/shard_map/ppermute | solution.py:842
  49.0 1.9 collective-permute-start.6
  49.0 2.7 %collective-permute-start.7 = (bf16[256,1024]{1,0:T(8,128)(2,1)S(1)}, bf16[256,1024]{1,0:T(8,128)(2,1)S(1)}, u32[]{:S(2)}, u32[]{:S(2)}) collective-permute-start(bf16[256,1024]{1,0:T(8,128)(2,1)S(1)} %collective-permute-done.3.refs_5_), channel_id=1, source_target_pairs={{0,4},{4,0},{8,12},{12,8},{16,20},{20,16},{24,28},{28,24},{1,5},{5... | collective-permute-start | bytes 1572872 | tf_op jit(solution)/shard_map/ppermute | solution.py:842
  51.7 33.5 %collective-permute-start.11 = (bf16[2,2,128,1024]{3,2,1,0:T(8,128)(2,1)S(1)}, bf16[2,2,128,1024]{3,2,1,0:T(8,128)(2,1)S(1)}, u32[]{:S(2)}, u32[]{:S(2)}) collective-permute-start(bf16[2,2,128,1024]{3,2,1,0:T(8,128)(2,1)S(1)} %get-tuple-element.78.refs_11_), channel_id=1, source_target_pairs={{0,8},{4,12},{8,0},{12,4},{16,24},{20,28},{24,16},{28,20},{1,9},{5... | collective-permute-start | bytes 3145736 | tf_op jit(solution)/shard_map/ppermute | solution.py:842
  53.2 31.9 %collective-permute-start.12 = (bf16[2,2,128,1024]{3,2,1,0:T(8,128)(2,1)S(1)}, bf16[2,2,128,1024]{3,2,1,0:T(8,128)(2,1)S(1)}, u32[]{:S(2)}, u32[]{:S(2)}) collective-permute-start(bf16[2,2,128,1024]{3,2,1,0:T(8,128)(2,1)S(1)} %get-tuple-element.88), channel_id=1, source_target_pairs={{0,16},{4,20},{8,24},{12,28},{16,0},{20,4},{24,8},{28,12},{1,17},{... | collective-permute-start | bytes 3145736 | tf_op jit(solution)/shard_map/ppermute | solution.py:842
  90.8 4.2 %collective-permute-start.13 = (bf16[2,2,256,1024]{3,2,1,0:T(8,128)(2,1)S(1)}, bf16[2,2,256,1024]{3,2,1,0:T(8,128)(2,1)S(1)}, u32[]{:S(2)}, u32[]{:S(2)}) collective-permute-start(bf16[2,2,256,1024]{3,2,1,0:T(8,128)(2,1)S(1)} %get-tuple-element.93), channel_id=1, source_target_pairs={{0,4},{4,0},{8,12},{12,8},{16,20},{20,16},{24,28},{28,24},{1,5},{5... | collective-permute-start | bytes 6291464 | tf_op jit(solution)/shard_map/ppermute | solution.py:842
  90.9 14.3 %collective-permute-start.29 = (bf16[2,2,512,128]{3,2,1,0:T(8,128)(2,1)S(1)}, bf16[2,2,512,128]{3,2,1,0:T(8,128)(2,1)S(1)}, u32[]{:S(2)}, u32[]{:S(2)}) collective-permute-start(bf16[2,2,512,128]{3,2,1,0:T(8,128)(2,1)S(1)} %get-tuple-element.109), channel_id=1, source_target_pairs={{0,8},{4,12},{8,0},{12,4},{16,24},{20,28},{24,16},{28,20},{1,9},{5... | collective-permute-start | bytes 1572872 | tf_op jit(solution)/shard_map/ppermute | solution.py:842
  92.5 14.0 %collective-permute-start.30 = (bf16[2,2,512,128]{3,2,1,0:T(8,128)(2,1)S(1)}, bf16[2,2,512,128]{3,2,1,0:T(8,128)(2,1)S(1)}, u32[]{:S(2)}, u32[]{:S(2)}) collective-permute-start(bf16[2,2,512,128]{3,2,1,0:T(8,128)(2,1)S(1)} %get-tuple-element.111), channel_id=1, source_target_pairs={{0,16},{4,20},{8,24},{12,28},{16,0},{20,4},{24,8},{28,12},{1,17},{... | collective-permute-start | bytes 1572872 | tf_op jit(solution)/shard_map/ppermute | solution.py:842
  95.3 21.2 %collective-permute-start.15 = (bf16[1,256,1024]{2,1,0:T(8,128)(2,1)S(1)}, bf16[1,256,1024]{2,1,0:T(8,128)(2,1)S(1)}, u32[]{:S(2)}, u32[]{:S(2)}) collective-permute-start(bf16[1,256,1024]{2,1,0:T(8,128)(2,1)S(1)} %get-tuple-element.95), channel_id=1, source_target_pairs={{0,1},{1,0},{2,3},{3,2},{4,5},{5,4},{6,7},{7,6},{8,9},{9,8},{10,11... | collective-permute-start | bytes 1572872 | tf_op jit(solution)/shard_map/ppermute | solution.py:842
  106.5 11.5 %copy-start.15 = (f32[1,1024]{1,0:T(1,128)S(1)}, f32[1,1024]{1,0:T(1,128)}, u32[]{:S(2)}) copy-start(f32[1,1024]{1,0:T(1,128)} %get-tuple-element.96.refs_8_) | copy-start | bytes 12292
  106.6 9.3 %collective-permute-start.31 = (bf16[1,2,512,128]{3,2,1,0:T(8,128)(2,1)S(1)}, bf16[1,2,512,128]{3,2,1,0:T(8,128)(2,1)S(1)}, u32[]{:S(2)}, u32[]{:S(2)}) collective-permute-start(bf16[1,2,512,128]{3,2,1,0:T(8,128)(2,1)S(1)} %get-tuple-element.112), channel_id=1, source_target_pairs={{0,16},{4,20},{8,24},{12,28},{16,0},{20,4},{24,8},{28,12},{1,17},{... | collective-permute-start | bytes 786440 | tf_op jit(solution)/shard_map/ppermute | solution.py:842
  107.4 22.4 %collective-permute-start.34 = (bf16[2,2,512,128]{3,2,1,0:T(8,128)(2,1)S(1)}, bf16[2,2,512,128]{3,2,1,0:T(8,128)(2,1)S(1)}, u32[]{:S(2)}, u32[]{:S(2)}) collective-permute-start(bf16[2,2,512,128]{3,2,1,0:T(8,128)(2,1)S(1)} %get-tuple-element.115), channel_id=1, source_target_pairs={{0,8},{4,12},{8,0},{12,4},{16,24},{20,28},{24,16},{28,20},{1,9},{5... | collective-permute-start | bytes 1572872 | tf_op jit(solution)/shard_map/ppermute | solution.py:842
  108.6 22.4 %collective-permute-start.35 = (bf16[2,2,512,128]{3,2,1,0:T(8,128)(2,1)S(1)}, bf16[2,2,512,128]{3,2,1,0:T(8,128)(2,1)S(1)}, u32[]{:S(2)}, u32[]{:S(2)}) collective-permute-start(bf16[2,2,512,128]{3,2,1,0:T(8,128)(2,1)S(1)} %get-tuple-element.117), channel_id=1, source_target_pairs={{0,16},{4,20},{8,24},{12,28},{16,0},{20,4},{24,8},{28,12},{1,17},{... | collective-permute-start | bytes 1572872 | tf_op jit(solution)/shard_map/ppermute | solution.py:842
  109.3 29.2 %collective-permute-start.21 = (bf16[1,2,128,1024]{3,2,1,0:T(8,128)(2,1)S(1)}, bf16[1,2,128,1024]{3,2,1,0:T(8,128)(2,1)S(1)}, u32[]{:S(2)}, u32[]{:S(2)}) collective-permute-start(bf16[1,2,128,1024]{3,2,1,0:T(8,128)(2,1)S(1)} %get-tuple-element.90.refs_10_), channel_id=1, source_target_pairs={{0,16},{4,20},{8,24},{12,28},{16,0},{20,4},{24,8},{28,12},{1,17},{... | collective-permute-start | bytes 1572872 | tf_op jit(solution)/shard_map/ppermute | solution.py:842
  115.9 11.9 %collective-permute-start.32 = (bf16[1,2,512,128]{3,2,1,0:T(8,128)(2,1)S(1)}, bf16[1,2,512,128]{3,2,1,0:T(8,128)(2,1)S(1)}, u32[]{:S(2)}, u32[]{:S(2)}) collective-permute-start(bf16[1,2,512,128]{3,2,1,0:T(8,128)(2,1)S(1)} %get-tuple-element.113), channel_id=1, source_target_pairs={{0,8},{4,12},{8,0},{12,4},{16,24},{20,28},{24,16},{28,20},{1,9},{5... | collective-permute-start | bytes 786440 | tf_op jit(solution)/shard_map/ppermute | solution.py:842
  116.5 36.5 %collective-permute-start.22 = (bf16[1,2,128,1024]{3,2,1,0:T(8,128)(2,1)S(1)}, bf16[1,2,128,1024]{3,2,1,0:T(8,128)(2,1)S(1)}, u32[]{:S(2)}, u32[]{:S(2)}) collective-permute-start(bf16[1,2,128,1024]{3,2,1,0:T(8,128)(2,1)S(1)} %get-tuple-element.91.refs_11_), channel_id=1, source_target_pairs={{0,8},{4,12},{8,0},{12,4},{16,24},{20,28},{24,16},{28,20},{1,9},{5... | collective-permute-start | bytes 1572872 | tf_op jit(solution)/shard_map/ppermute | solution.py:842
  127.8 4.8 %collective-permute-start.16 = (f32[6,1024]{1,0:T(8,128)S(1)}, f32[6,1024]{1,0:T(8,128)S(1)}, u32[]{:S(2)}, u32[]{:S(2)}) collective-permute-start(f32[6,1024]{1,0:T(8,128)S(1)} %get-tuple-element.98.refs_0_), channel_id=1, source_target_pairs={{0,1},{1,0},{2,3},{3,2},{4,5},{5,4},{6,7},{7,6},{8,9},{9,8},{10,11... | collective-permute-start | bytes 73736 | tf_op jit(solution)/shard_map/ppermute | solution.py:842
  129.8 28.1 %collective-permute-start.33 = (bf16[4,512,128]{2,1,0:T(8,128)(2,1)S(1)}, bf16[4,512,128]{2,1,0:T(8,128)(2,1)S(1)}, u32[]{:S(2)}, u32[]{:S(2)}) collective-permute-start(bf16[4,512,128]{2,1,0:T(8,128)(2,1)S(1)} %shard_map.235), channel_id=1, source_target_pairs={{0,2},{1,3},{2,0},{3,1},{4,6},{5,7},{6,4},{7,5},{8,10},{9,11},{10,... | collective-permute-start | bytes 1572872 | tf_op jit(solution)/shard_map/ppermute | solution.py:842
  131.2 22.2 %collective-permute-start.36 = (bf16[1,2,512,128]{3,2,1,0:T(8,128)(2,1)S(1)}, bf16[1,2,512,128]{3,2,1,0:T(8,128)(2,1)S(1)}, u32[]{:S(2)}, u32[]{:S(2)}) collective-permute-start(bf16[1,2,512,128]{3,2,1,0:T(8,128)(2,1)S(1)} %get-tuple-element.118), channel_id=1, source_target_pairs={{0,16},{4,20},{8,24},{12,28},{16,0},{20,4},{24,8},{28,12},{1,17},{... | collective-permute-start | bytes 786440 | tf_op jit(solution)/shard_map/ppermute | solution.py:842
  132.6 22.9 %collective-permute-start.37 = (bf16[1,2,512,128]{3,2,1,0:T(8,128)(2,1)S(1)}, bf16[1,2,512,128]{3,2,1,0:T(8,128)(2,1)S(1)}, u32[]{:S(2)}, u32[]{:S(2)}) collective-permute-start(bf16[1,2,512,128]{3,2,1,0:T(8,128)(2,1)S(1)} %get-tuple-element.119), channel_id=1, source_target_pairs={{0,8},{4,12},{8,0},{12,4},{16,24},{20,28},{24,16},{28,20},{1,9},{5... | collective-permute-start | bytes 786440 | tf_op jit(solution)/shard_map/ppermute | solution.py:842
  138.4 14.6 %collective-permute-start.17 = (f32[6,1024]{1,0:T(8,128)S(1)}, f32[6,1024]{1,0:T(8,128)S(1)}, u32[]{:S(2)}, u32[]{:S(2)}) collective-permute-start(f32[6,1024]{1,0:T(8,128)S(1)} %shard_map.225.refs_0_), channel_id=1, source_target_pairs={{0,2},{1,3},{2,0},{3,1},{4,6},{5,7},{6,4},{7,5},{8,10},{9,11},{10,... | collective-permute-start | bytes 73736 | tf_op jit(solution)/shard_map/ppermute | solution.py:842
  153.0 35.6 %collective-permute-start.14 = (bf16[1,256,1024]{2,1,0:T(8,128)(2,1)S(1)}, bf16[1,256,1024]{2,1,0:T(8,128)(2,1)S(1)}, u32[]{:S(2)}, u32[]{:S(2)}) collective-permute-start(bf16[1,256,1024]{2,1,0:T(8,128)(2,1)S(1)} %get-tuple-element.94), channel_id=1, source_target_pairs={{0,1},{1,0},{2,3},{3,2},{4,5},{5,4},{6,7},{7,6},{8,9},{9,8},{10,11... | collective-permute-start | bytes 1572872 | tf_op jit(solution)/shard_map/ppermute | solution.py:842
  153.0 3.4 %collective-permute-start.18 = (f32[6,1024]{1,0:T(8,128)S(1)}, f32[6,1024]{1,0:T(8,128)S(1)}, u32[]{:S(2)}, u32[]{:S(2)}) collective-permute-start(f32[6,1024]{1,0:T(8,128)S(1)} %shard_map.226.refs_0_), channel_id=1, source_target_pairs={{0,4},{4,0},{8,12},{12,8},{16,20},{20,16},{24,28},{28,24},{1,5},{5... | collective-permute-start | bytes 73736 | tf_op jit(solution)/shard_map/ppermute | solution.py:842
  153.4 24.8 %collective-permute-start.23 = (bf16[1,128,1024]{2,1,0:T(8,128)(2,1)S(1)}, bf16[1,128,1024]{2,1,0:T(8,128)(2,1)S(1)}, u32[]{:S(2)}, u32[]{:S(2)}) collective-permute-start(bf16[1,128,1024]{2,1,0:T(8,128)(2,1)S(1)} %get-tuple-element.103), channel_id=1, source_target_pairs={{0,1},{1,0},{2,3},{3,2},{4,5},{5,4},{6,7},{7,6},{8,9},{9,8},{10,11... | collective-permute-start | bytes 786440 | tf_op jit(solution)/shard_map/ppermute | solution.py:842
  155.5 22.7 %collective-permute-start.24 = (bf16[1,128,1024]{2,1,0:T(8,128)(2,1)S(1)}, bf16[1,128,1024]{2,1,0:T(8,128)(2,1)S(1)}, u32[]{:S(2)}, u32[]{:S(2)}) collective-permute-start(bf16[1,128,1024]{2,1,0:T(8,128)(2,1)S(1)} %get-tuple-element.104), channel_id=1, source_target_pairs={{0,2},{1,3},{2,0},{3,1},{4,6},{5,7},{6,4},{7,5},{8,10},{9,11},{10,... | collective-permute-start | bytes 786440 | tf_op jit(solution)/shard_map/ppermute | solution.py:842
  156.4 27.6 %collective-permute-start.25 = (bf16[1,128,1024]{2,1,0:T(8,128)(2,1)S(1)}, bf16[1,128,1024]{2,1,0:T(8,128)(2,1)S(1)}, u32[]{:S(2)}, u32[]{:S(2)}) collective-permute-start(bf16[1,128,1024]{2,1,0:T(8,128)(2,1)S(1)} %get-tuple-element.105), channel_id=1, source_target_pairs={{0,3},{1,2},{2,1},{3,0},{4,7},{5,6},{6,5},{7,4},{8,11},{9,10},{10,... | collective-permute-start | bytes 786440 | tf_op jit(solution)/shard_map/ppermute | solution.py:842
  157.9 27.9 %collective-permute-start.19 = (f32[6,1024]{1,0:T(8,128)S(1)}, f32[6,1024]{1,0:T(8,128)S(1)}, u32[]{:S(2)}, u32[]{:S(2)}) collective-permute-start(f32[6,1024]{1,0:T(8,128)S(1)} %shard_map.227.refs_0_), channel_id=1, source_target_pairs={{0,8},{4,12},{8,0},{12,4},{16,24},{20,28},{24,16},{28,20},{1,9},{5... | collective-permute-start | bytes 73736 | tf_op jit(solution)/shard_map/ppermute | solution.py:842
  159.5 30.5 %copy-start.14 = (f32[1024]{0:T(1024)S(1)}, f32[1024]{0:T(1024)}, u32[]{:S(2)}) copy-start(f32[1024]{0:T(1024)} %param.23) | copy-start | bytes 12292
  178.2 15.6 %collective-permute-start.38 = (bf16[2,512,128]{2,1,0:T(8,128)(2,1)S(1)}, bf16[2,512,128]{2,1,0:T(8,128)(2,1)S(1)}, u32[]{:S(2)}, u32[]{:S(2)}) collective-permute-start(bf16[2,512,128]{2,1,0:T(8,128)(2,1)S(1)} %get-tuple-element.121), channel_id=1, source_target_pairs={{0,4},{4,0},{8,12},{12,8},{16,20},{20,16},{24,28},{28,24},{1,5},{5... | collective-permute-start | bytes 786440 | tf_op jit(solution)/shard_map/ppermute | solution.py:842
  184.1 11.2 %collective-permute-start.28 = (bf16[1,128,1024]{2,1,0:T(8,128)(2,1)S(1)}, bf16[1,128,1024]{2,1,0:T(8,128)(2,1)S(1)}, u32[]{:S(2)}, u32[]{:S(2)}) collective-permute-start(bf16[1,128,1024]{2,1,0:T(8,128)(2,1)S(1)} %shard_map.232.refs_1_), channel_id=1, source_target_pairs={{0,3},{1,2},{2,1},{3,0},{4,7},{5,6},{6,5},{7,4},{8,11},{9,10},{10,... | collective-permute-start | bytes 786440 | tf_op jit(solution)/shard_map/ppermute | solution.py:842
  185.9 20.5 %collective-permute-start.27 = (bf16[1,128,1024]{2,1,0:T(8,128)(2,1)S(1)}, bf16[1,128,1024]{2,1,0:T(8,128)(2,1)S(1)}, u32[]{:S(2)}, u32[]{:S(2)}) collective-permute-start(bf16[1,128,1024]{2,1,0:T(8,128)(2,1)S(1)} %shard_map.232.refs_1_), channel_id=1, source_target_pairs={{0,2},{1,3},{2,0},{3,1},{4,6},{5,7},{6,4},{7,5},{8,10},{9,11},{10,... | collective-permute-start | bytes 786440 | tf_op jit(solution)/shard_map/ppermute | solution.py:842
  185.9 20.4 %collective-permute-start.26 = (bf16[1,128,1024]{2,1,0:T(8,128)(2,1)S(1)}, bf16[1,128,1024]{2,1,0:T(8,128)(2,1)S(1)}, u32[]{:S(2)}, u32[]{:S(2)}) collective-permute-start(bf16[1,128,1024]{2,1,0:T(8,128)(2,1)S(1)} %shard_map.232.refs_1_), channel_id=1, source_target_pairs={{0,1},{1,0},{2,3},{3,2},{4,5},{5,4},{6,7},{7,6},{8,9},{9,8},{10,11... | collective-permute-start | bytes 786440 | tf_op jit(solution)/shard_map/ppermute | solution.py:842
  188.6 4.0 %collective-permute-start.20 = (f32[6,1024]{1,0:T(8,128)S(1)}, f32[6,1024]{1,0:T(8,128)S(1)}, u32[]{:S(2)}, u32[]{:S(2)}) collective-permute-start(f32[6,1024]{1,0:T(8,128)S(1)} %shard_map.228.refs_0_), channel_id=1, source_target_pairs={{0,16},{4,20},{8,24},{12,28},{16,0},{20,4},{24,8},{28,12},{1,17},{... | collective-permute-start | bytes 73736 | tf_op jit(solution)/shard_map/ppermute | solution.py:842
  (10 other events, 70.6 us)

commit v3 on v2

--- a/solution.py
+++ b/solution.py
@@ -20,7 +20,8 @@
 F32 = jnp.float32
 MIB = 1 << 20
 BIAS_ROWS = 16
-US = 0.1
+COST = {'pack': 3, 'prep': 1, 'A': 0.05, 'B': 1, 'A3': 25, 'M': 50, 'cross': 0.3, 'at1': 12, 'fo1': 0.05, 'both': 6, 'parts': 0.05, 'aown': 0.05, 'mine': 3, 'nb': 1, 'ro': 12, 'sm': 50, 'af': 50, 'rf': 25, 'ff': 1, 'zadd': 6, 'zjoin': 1}
+CFG = {'deep0': 1, 'deep1': 4, 'sidesB': 1, 'sidesS': 1, 'sidesC': 1, 'sidesD': 0, 'W2': 1, 'A3S': 2, 'bothA3': 1, 'attnBoth': 1, 'MA3': 1, 'cross2': 1, 'at1': 1, 'fo1': 3, 'first': 0, 'nb': 1, 'parts': 0, 'both': 1, 'send': 1}
 SUMS = 4
 
 COUNT, LIVE, ENDS, STARTS, TERMS, OFFS, TABLE = 0, 1, 2, 6, 10, 14, 24
@@ -34,7 +35,7 @@
     return lax.dot_general(a, b, (((1,), (1,)), ((), ())), preferred_element_type=F32)
 
 
-def call(kernel, args, outs, scratch=(), specs=None, out_specs=None, grid=None, vmem=24, us=US, after=()):
+def call(kernel, args, outs, scratch=(), specs=None, out_specs=None, grid=None, vmem=24, tag="", after=()):
     count = len(args)
     specs = specs or {}
 
@@ -51,7 +52,7 @@
         scratch_shapes=list(scratch),
         compiler_params=pltpu.CompilerParams(vmem_limit_bytes=vmem * MIB),
         cost_estimate=pl.CostEstimate(
-            flops=int(us * 1e9), bytes_accessed=1024, transcendentals=0
+            flops=int(COST[tag] * 1e9), bytes_accessed=1024, transcendentals=0
         ),
         **options,
     )(*args, *after)
@@ -132,6 +133,7 @@
         ],
         specs={0: HBM, 1: HBM, 2: HBM},
         vmem=59,
+        tag="pack",
     )
 
 
@@ -215,6 +217,7 @@
         specs={0: SMEM, 1: SMEM, 2: SMEM, 3: HBM, 4: HBM, 5: HBM, 6: HBM},
         vmem=58,
         after=after,
+        tag="prep",
     )
 
 
@@ -367,6 +370,7 @@
         specs={4: HBM, 5: HBM},
         vmem=52,
         after=after,
+        tag="A",
     )
 
 
@@ -394,6 +398,7 @@
         out_specs=(block, block),
         grid=(width // LANES,),
         after=after,
+        tag="B",
     )
 
 
@@ -466,6 +471,7 @@
             pltpu.SemaphoreType.DMA((2 * chips,)),
         ],
         after=after,
+        tag="A3",
     )
 
 
@@ -511,159 +517,135 @@
     ]
 
 
-def feed_kernel(chips, foreign, *refs):
+def feed_kernel(chips, shards, pieces, *refs):
     toks, refs = refs[:8], refs[8:]
-    sources = refs[: chips if foreign else 2]
-    refs = refs[len(sources) :]
-    if not foreign:
-        bias_ref, refs = refs[0], refs[1:]
-    act_ref, eg_ref, bias_out, ps, pk, qs, qk = refs[:7]
-    x, bg, act_t, eg_t, sem_in, we, ws, sem_w = refs[7:15]
+    sources = []
+    for n in range(shards):
+        size = chips if n else 2
+        sources.append(refs[:size])
+        refs = refs[size:]
+    bias_ref, refs = refs[0], refs[1:]
+    sums, keep, ps, pk, qs, qk = refs[:6]
+    sends, refs = refs[6 : 6 + pieces], refs[6 + pieces :]
+    x, bg, act_n, eg_n, act_t, eg_t, sem_in = refs[:7]
+    refs = refs[7:]
+    scratch = [refs[5 * n : 5 * n + 5] for n in range(shards)]
     rows, width = toks[0].shape
-    hidden = act_t.shape[0]
-    weights = load_weights(sources, we, ws, sem_w)
-    if foreign:
-        bias_rows, sem_b = refs[15:17]
-        strip = width // chips
-        weights.append(
-            pltpu.make_async_copy(sources[0].at[pl.ds(strip, BIAS_ROWS)], bias_rows, sem_b)
-        )
-    for copy in weights:
-        copy.start()
+    hidden = act_t.shape[0] // shards
     loads = []
     for n, tok in enumerate(toks):
         dst = (x, bg)[n % 2].at[pl.ds(n // 2 * rows, rows)]
         loads.append(pltpu.make_async_copy(tok, dst, sem_in.at[n]))
-    for copy in loads:
+    weights = []
+    for n, (we, ws, sem, bias_rows, sem_b) in enumerate(scratch):
+        copies = load_weights(sources[n], we, ws, sem)
+        if n:
+            strip = width // chips
+            copies.append(
+                pltpu.make_async_copy(sources[n][0].at[pl.ds(strip, BIAS_ROWS)], bias_rows, sem_b)
+            )
+        weights.append(copies)
+    for copy in loads + [c for copies in weights for c in copies]:
         copy.start()
-    for copy in weights:
-        copy.wait()
-    if foreign:
-        bias = jnp.sum(bias_rows[:, :hidden].astype(F32), axis=0, keepdims=True)
-    else:
-        bias = bias_ref[:, pl.ds(pl.multiple_of(places()[0] * hidden, 128), hidden)]
     for copy in loads:
         copy.wait()
     step = min(256, hidden)
-    for h in range(0, hidden, step):
-        block = slice(h, h + step)
-        v = nn(x[...], we[:, block]) + bias[:, block]
-        square = v * v
-        t = jnp.tanh(0.7978845608 * v * (1.0 + 0.044715 * square))
-        low = 0.5 * (1.0 + t)
-        slope = low + 0.5 * v * (1.0 - t * t) * (0.7978845608 * (1.0 + 0.134145 * square))
-        act = (v * low).astype(BF)
-        eg = (nt(bg[...], ws[block, :]) * slope).astype(BF)
-        act_ref[:, block] = act
-        eg_ref[:, block] = eg
-        act_t[block, :] = act.T
-        eg_t[block, :] = eg.T
-        bias_out[:, block] = jnp.sum(eg.astype(F32), axis=0, keepdims=True)
+    for n, (we, ws, _, bias_rows, _) in enumerate(scratch):
+        for copy in weights[n]:
+            copy.wait()
+        if n:
+            bias = jnp.sum(bias_rows[:, :hidden].astype(F32), axis=0, keepdims=True)
+        else:
+            bias = bias_ref[:, pl.ds(pl.multiple_of(places()[0] * hidden, 128), hidden)]
+        for h in range(0, hidden, step):
+            block = slice(h, h + step)
+            there = slice(n * hidden + h, n * hidden + h + step)
+            v = nn(x[...], we[:, block]) + bias[:, block]
+            square = v * v
+            t = jnp.tanh(0.7978845608 * v * (1.0 + 0.044715 * square))
+            low = 0.5 * (1.0 + t)
+            slope = low + 0.5 * v * (1.0 - t * t) * (0.7978845608 * (1.0 + 0.134145 * square))
+            act = (v * low).astype(BF)
+            eg = (nt(bg[...], ws[block, :]) * slope).astype(BF)
+            act_n[:, there] = act
+            eg_n[:, there] = eg
+            act_t[there, :] = act.T
+            eg_t[there, :] = eg.T
+            sums[n : n + 1, block] = jnp.sum(eg.astype(F32), axis=0, keepdims=True)
+    step = min(256, width)
+    for c in range(0, width, step):
+        block = slice(c, c + step)
+        grad, out = 0.0, 0.0
+        for n, (we, ws, _, _, _) in enumerate(scratch):
+            part = slice(n * hidden, (n + 1) * hidden)
+            grad = grad + nt(eg_n[:, part], we[block, :])
+            out = out + nn(act_n[:, part], ws[:, block])
+        for m, value in enumerate((grad, out)):
+            for r in range(4):
+                place, dst = (m, r // 2), keep
+                if r % 2:
+                    flat = 2 * m + r // 2
+                    dst = sends[flat * pieces // 4]
+                    place = {1: place, 2: place[1:], 4: ()}[pieces]
+                dst[(*place, slice(None), block)] = value[r * rows : (r + 1) * rows].astype(BF)
     chunk = width // chips
     half = chunk // 2
     core, chip, _ = places()
     top = chips.bit_length() - 2
-    for left, right, bit, send, keep in ((eg_t, x, 0, ps, pk), (act_t, bg, top, qs, qk)):
-        for dst, js in ((send, with_bit(chips, bit)), (keep, without_bit(chips, bit))):
+
+    def store(dst, i, tile, turned):
+        for n in range(shards):
+            for a in range(2):
+                part = tile[n * hidden : (n + 1) * hidden, a * half : (a + 1) * half]
+                dst[i, n, core ^ a] = part.T if turned else part
+
+    for left, right, bit, go, stay in ((eg_t, x, 0, ps, pk), (act_t, bg, top, qs, qk)):
+        for dst, js in ((go, with_bit(chips, bit)), (stay, without_bit(chips, bit))):
             for i, j in enumerate(js):
                 if half % 128 == 0:
                     start = pl.multiple_of((chip ^ j) * chunk, 128)
-                    tile = nn(left[...], right[:, pl.ds(start, chunk)]).astype(BF)
-                    for a in range(2):
-                        dst[i, core ^ a] = tile[:, a * half : (a + 1) * half]
+                    store(dst, i, nn(left[...], right[:, pl.ds(start, chunk)]).astype(BF), False)
                     continue
                 for k in range(chips):
 
                     @pl.when(chip ^ j == k)
                     def narrow():
-                        tile = nn(left[...], right[:, k * chunk : (k + 1) * chunk]).astype(BF)
-                        for a in range(2):
-                            dst[i, core ^ a] = tile[:, a * half : (a + 1) * half].T
-
-
-def feed(chips, toks, weights, bias, hidden, after=()):
+                        span = slice(k * chunk, (k + 1) * chunk)
+                        store(dst, i, nn(left[...], right[:, span]).astype(BF), True)
+
+
+def feed(chips, toks, sources, bias, hidden, after=()):
     rows, width = toks[0].shape
+    shards = len(sources)
     half = width // chips // 2
-    foreign = bias is None
     edge = (hidden, half) if half % 128 == 0 else (half, hidden)
-    piece = struct((chips // 2, 2, *edge), BF)
-    scratch = [
-        pltpu.VMEM((4 * rows, width), BF),
-        pltpu.VMEM((4 * rows, width), BF),
-        pltpu.VMEM((hidden, 4 * rows), BF),
-        pltpu.VMEM((hidden, 4 * rows), BF),
-        pltpu.SemaphoreType.DMA((8,)),
-        *weight_scratch(chips, hidden, width),
-    ]
-    args = (*toks, *weights)
+    piece = struct((chips // 2, shards, 2, *edge), BF)
+    scratch = [pltpu.VMEM((4 * rows, width), BF)] * 2
+    scratch += [pltpu.VMEM((4 * rows, shards * hidden), BF)] * 2
+    scratch += [pltpu.VMEM((shards * hidden, 4 * rows), BF)] * 2
+    scratch += [pltpu.SemaphoreType.DMA((8,))]
+    for _ in range(shards):
+        scratch += weight_scratch(chips, hidden, width)
+        scratch += [pltpu.VMEM((BIAS_ROWS, 2 * hidden), BF), pltpu.SemaphoreType.DMA(())]
+    args = (*toks, *[a for source in sources for a in source])
     specs = {n: ANY for n in range(len(args))}
-    if foreign:
-        scratch += [pltpu.VMEM((BIAS_ROWS, 2 * hidden), BF), pltpu.SemaphoreType.DMA(())]
-    else:
-        args += (bias,)
+    result = struct((2, 2, rows, width), BF)
     return call(
-        partial(feed_kernel, chips, foreign),
-        args,
-        (struct((4 * rows, hidden), BF),) * 2 + (struct((1, hidden), F32),) + (piece,) * 4,
+        partial(feed_kernel, chips, shards, CFG["send"]),
+        (*args, bias),
+        (struct((shards, hidden), F32), result)
+        + (piece,) * 4
+        + (struct({1: (2, 2, rows, width), 2: (2, rows, width), 4: (rows, width)}[CFG["send"]], BF),)
+        * CFG["send"],
         scratch=scratch,
         specs=specs,
-        us=20.0 if foreign else US,
+        vmem=36,
+        tag="M",
         after=after,
     )
 
 
-def feed_out_kernel(chips, shards, *refs):
-    sets = []
-    for n in range(shards):
-        size = chips if n else 2
-        sets.append((refs[0], refs[1], refs[2 : 2 + size]))
-        refs = refs[2 + size :]
-    keep, send = refs[:2]
-    rows = keep.shape[2]
-    scratch = [refs[2 + 3 * n : 5 + 3 * n] for n in range(shards)]
-    copies = []
-    for (_, _, sources), (we, ws, sem) in zip(sets, scratch):
-        copies += load_weights(sources, we, ws, sem)
-    for copy in copies:
-        copy.start()
-    for copy in copies:
-        copy.wait()
-    width = keep.shape[3]
-    step = min(256, width)
-    for c in range(0, width, step):
-        block = slice(c, c + step)
-        grad, out = 0.0, 0.0
-        for (act, eg, _), (we, ws, _) in zip(sets, scratch):
-            grad = grad + nt(eg[...], we[block, :])
-            out = out + nn(act[...], ws[:, block])
-        for m, value in enumerate((grad, out)):
-            for r in range(4):
-                dst = send if r % 2 else keep
-                dst[m, r // 2, :, block] = value[r * rows : (r + 1) * rows].astype(BF)
-
-
-def feed_out(chips, sets, after=()):
-    rows4, hidden = sets[0][0].shape
-    width = sets[0][2][1].shape[1]
-    args, specs, scratch = (), {}, []
-    for act, eg, sources in sets:
-        for n in range(len(sources)):
-            specs[len(args) + 2 + n] = ANY
-        args += (act, eg, *sources)
-        scratch += weight_scratch(chips, hidden, width)
-    result = struct((2, 2, rows4 // 4, width), BF)
-    return call(
-        partial(feed_out_kernel, chips, len(sets)),
-        args,
-        (result, result),
-        scratch=scratch,
-        specs=specs,
-        after=after,
-    )
-
-
-def norm_back_kernel(info, x_ref, u_ref, gain_ref, g0, g1, g2, g3, sum_ref, *refs):
-    biases, (out_ref, small_ref) = refs[:-2], refs[-2:]
+def norm_back_kernel(spot, info, x_ref, u_ref, gain_ref, g0, g1, g2, g3, sum_ref, biases, out_ref, small_ref):
     rows, width = x_ref.shape
     step = 64
     count = info[COUNT : COUNT + 1, 0:1].astype(F32)
@@ -672,7 +654,7 @@
     for r in range(0, rows, step):
         here = slice(r, r + step)
         xhat, inverse = normalize(x_ref[here, :].astype(F32))
-        grad = g0[here, :] + g1[0, 0, here, :].astype(F32) + g2[0, 0, here, :].astype(F32)
+        grad = g0[here, :] + g1[0, 0, here, :].astype(F32) + g2[(*spot, here)].astype(F32)
         grad = grad + g3[0, here, :].astype(F32)
         gain_sum = gain_sum + jnp.sum(grad * xhat, axis=0, keepdims=True)
         shift_sum = shift_sum + jnp.sum(grad, axis=0, keepdims=True)
@@ -687,19 +669,19 @@
     small_ref[1:2, :] = shift_sum
     small_ref[2:3, :] = sum_ref[...]
     small_ref[3:4, :] = jnp.zeros((1, width), F32) + count
-    hidden = biases[0].shape[1]
+    shards, hidden = biases.shape
     half = pl.ds(pl.multiple_of(places()[0] * hidden, 128), hidden)
-    for k, bias in enumerate(biases):
-        small_ref[SUMS + k : SUMS + k + 1, half] = bias[...]
+    small_ref[SUMS : SUMS + shards, half] = biases[...]
 
 
 def norm_back(info, x, u, gain, g0, g1, g2, g3, sums, biases, after=()):
-    small = (SUMS + len(biases), x.shape[1])
+    small = (SUMS + biases.shape[0], x.shape[1])
     return call(
-        norm_back_kernel,
-        (info, x, u, gain, g0, g1, g2, g3, sums, *biases),
+        partial(norm_back_kernel, g2[1]),
+        (info, x, u, gain, g0, g1, g2[0], g3, sums, biases),
         (struct(x.shape, F32), struct(small, F32)),
         after=after,
+        tag="nb",
     )
 
 
@@ -720,16 +702,16 @@
 
 def small_sum(small, axis, bit):
     other = exchange(small, axis, 1 << bit)
-    return call(partial(small_kernel, axis, bit), (small, other), struct(small.shape, F32))
-
-
-def row_out_kernel(info, x_ref, sum_ref, g1, g2, g3, bias_ref, out_ref):
+    return call(partial(small_kernel, axis, bit), (small, other), struct(small.shape, F32), tag="sm")
+
+
+def row_out_kernel(spot, info, x_ref, sum_ref, g1, g2, g3, bias_ref, out_ref):
     rows, width = x_ref.shape
     step = 64
     for r in range(0, rows, step):
         here = slice(r, r + step)
-        branch = sum_ref[here, :] + g1[1, 0, here, :].astype(F32) + g2[1, 0, here, :].astype(F32)
-        branch = branch + g3[0, here, :].astype(F32) + bias_ref[...]
+        branch = sum_ref[here, :] + g1[1, 0, here, :].astype(F32) + g2[(*spot, here)].astype(F32)
+        branch = branch + g3[g3.shape[0] - 1, here, :].astype(F32) + bias_ref[...]
         where = lax.broadcasted_iota(jnp.int32, (step, width), 0) + r
         branch = jnp.where(where < info[LIVE : LIVE + 1, 0:1], branch, 0.0)
         out_ref[here, :] = (x_ref[here, :].astype(F32) + branch).astype(BF)
@@ -737,22 +719,23 @@
 
 def row_out(info, x, attention_out, g1, g2, g3, bias, after=()):
     return call(
-        row_out_kernel,
-        (info, x, attention_out, g1, g2, g3, bias),
+        partial(row_out_kernel, g2[1]),
+        (info, x, attention_out, g1, g2[0], g3, bias),
         struct(x.shape, BF),
         after=after,
-    )
-
-
-def attend_final_kernel(scale, small_ref, *refs):
+        tag="ro",
+    )
+
+
+def attend_final_kernel(scale, picks, small_ref, *refs):
     parts, (attend, output) = refs[:-2], refs[-2:]
-    depth = len(parts)
+    depth = len(picks)
     cols = parts[0].shape[2]
     edge = 3 * depth // 4
     factor = scale / small_ref[3:4, 0:1]
-    for j, part in enumerate(parts):
+    for j, (n, index) in picks.items():
         place = places()[2] ^ j
-        value = part[0].astype(F32) * factor
+        value = parts[n][index].astype(F32) * factor
 
         @pl.when(place < edge)
         def inner():
@@ -763,14 +746,21 @@
             output[:, pl.ds(pl.multiple_of((place - edge) * cols, 128), cols)] = value
 
 
-def attend_final(scale, small, parts):
-    _, half, cols = parts[0].shape
-    depth = len(parts)
+def attend_final(scale, small, have):
+    arrays, picks = [], {}
+    for j, (array, index) in have.items():
+        n = next((n for n, a in enumerate(arrays) if a is array), len(arrays))
+        if n == len(arrays):
+            arrays.append(array)
+        picks[j] = (n, index)
+    _, half, cols = arrays[0].shape
+    depth = len(picks)
     attend, output = (half, 3 * depth // 4 * cols), (half, depth // 4 * cols)
     return call(
-        partial(attend_final_kernel, scale),
-        (small, *parts),
+        partial(attend_final_kernel, scale, picks),
+        (small, *arrays),
         (struct(attend, F32), struct(output, F32)),
+        tag="af",
     )
 
 
@@ -789,6 +779,7 @@
         partial(row_final_kernel, scale),
         (small, grad),
         (struct(grad.shape, F32), row, row, row, struct((1, shard), F32)),
+        tag="rf",
     )
 
 
@@ -809,6 +800,7 @@
         partial(feed_final_kernel, scale, narrow),
         (small, mine, sibling),
         (struct((half, 2 * hidden), F32), struct((2 * hidden, half), F32)),
+        tag="ff",
     )
 
 
@@ -819,7 +811,7 @@
             out[p] = sum(ins[n][index].astype(F32) for n, index in part).astype(out.dtype)
 
 
-def add(plan, after=()):
+def add(plan, tag, after=()):
     arrays, outs, inner = [], [], []
     for dtype, parts in plan:
         entries = []
@@ -834,7 +826,7 @@
         inner.append((dtype, entries))
         array, index = parts[0][0]
         outs.append(struct((len(parts), *array.shape[len(index) :]), dtype))
-    return call(partial(add_kernel, inner), tuple(arrays), tuple(outs), after=after)
+    return call(partial(add_kernel, inner), tuple(arrays), tuple(outs), tag=tag, after=after)
 
 
 def exchange(x, axis, flip):
@@ -842,7 +834,7 @@
     return lax.ppermute(x, axis, [(i, i ^ flip) for i in range(n)])
 
 
-def reduce_chips(chips, low, high, afters):
+def reduce_chips(chips, low, high, tag, afters=()):
     bits = list(range(chips.bit_length() - 1))
     orders = (bits, bits[::-1])
     left = []
@@ -859,7 +851,7 @@
             else:
                 stay.append(entries[: len(entries) // 2])
                 go.append(entries[len(entries) // 2 :])
-        sends = add([(BF, g) for g in go], after=afters)
+        sends = add([(BF, g) for g in go], tag, after=afters)
         left = []
         for entries, send, order in zip(stay, sends, orders):
             got = exchange(send, "dp", 2 << order[n])
@@ -869,6 +861,32 @@
 
 def behind(x, *others):
     return lax.optimization_barrier((x, *others))[0]
+
+
+def reduce_depth(parts, entries, depth):
+    left = {j: e for j, e in enumerate(entries)}
+    for bit in range(depth.bit_length() - 1):
+        go = [j for j in left if j >> bit & 1]
+        if bit:
+            parts = add([(BF, [left[j] for j in go])], "zadd")[0]
+        got = exchange(parts, "mp", 1 << bit)
+        for n, j in enumerate(go):
+            left[j ^ (1 << bit)] = left[j ^ (1 << bit)] + [(got, (n,))]
+            del left[j]
+    return left[0]
+
+
+def gather_depth(own, depth):
+    have = {0: (own, (0,))}
+    packed = own
+    for bit in reversed(range(depth.bit_length() - 1)):
+        order = list(have)
+        if len(order) > 1:
+            packed = add([(BF, [[have[j]] for j in order])], "zjoin")[0]
+        got = exchange(packed, "mp", 1 << bit)
+        for n, j in enumerate(order):
+            have[j ^ (1 << bit)] = (got, (n,))
+    return have
 
 
 def at(entry, *index):
@@ -914,64 +932,110 @@
 
     sides = attention(info, normed, bg, attend_weight, output_weight)
     grad_attention, attention_out = attention_back(sides, attend_weight, output_weight)
-    deep_normed = exchange(normed, "mp", 1)
-    sides_core = exchange(
-        behind(sides, grad_attention, *shares, *tok_core, deep_normed), "dp", 1
-    )
-    tok_deep = [deep_normed, exchange(behind(bg, sides), "mp", 1)]
-    foreign = [[s] + [exchange(s, "dp", 2 * j) for j in range(1, chips)] for s in shares]
-    attn = attention_grads(chips, depth, tok, tok_core, sides, sides_core, after=shares)
-    tok_both = [exchange(behind(t, attn[0]), "dp", 1) for t in tok_deep]
-    attn = [behind(a, *tok_both) for a in attn]
+    deep_normed = exchange(behind(normed, sides) if CFG["deep0"] else normed, "mp", 1)
+    wait = []
+    if CFG["sidesB"]:
+        wait.append(grad_attention)
+    if CFG["sidesS"]:
+        wait += shares
+    if CFG["sidesC"]:
+        wait += tok_core
+    if CFG["sidesD"]:
+        wait.append(deep_normed)
+    sides_core = exchange(behind(sides, *wait) if wait else sides, "dp", 1)
+    hold = {0: (), 1: (sides,), 2: (deep_normed,), 3: (grad_attention,), 4: tuple(shares)}[CFG["deep1"]]
+    tok_deep = [deep_normed, exchange(behind(bg, *hold) if hold else bg, "mp", 1)]
+    hold = {0: (), 1: (sides,), 2: (grad_attention,), 3: (sides_core,)}[CFG["W2"]]
+    held = [behind(s, *hold) if hold else s for s in shares]
+    foreign = [[s] + [exchange(s, "dp", 2 * j) for j in range(1, chips)] for s in held]
+    attn = attention_grads(
+        chips, depth, tok, tok_core, sides, sides_core, after={0: (), 1: shares, 2: (*shares, grad_attention)}[CFG["A3S"]]
+    )
+    hold = {0: (), 1: (attn[0],), 2: (sides,), 3: (sides_core,)}[CFG["bothA3"]]
+    tok_both = [exchange(behind(t, *hold) if hold else t, "dp", 1) for t in tok_deep]
+    if CFG["attnBoth"]:
+        attn = [behind(a, *tok_both) for a in attn]
     toks = (*tok, *tok_core, *tok_deep, *tok_both)
 
-    weights = (expand_weight, shrink_weight)
-    own = feed(chips, toks, weights, expand_bias[None, :], hidden, after=attn[:1])
-    others = [feed(chips, toks, pieces, None, hidden, after=own[:1]) for pieces in foreign]
-    sets = [(own[0], own[1], weights)]
-    sets += [(o[0], o[1], pieces) for o, pieces in zip(others, foreign)]
-    attn_sums, sent = reduce_chips(chips, attn[:2], attn[2:], (others[-1][2],))
-    keep, send = feed_out(chips, sets, after=sent)
-    passed = exchange(send, "dp", 1)
-    crossing = add([(BF, [[(keep, (m, 1)), (passed, (m, 1))]]) for m in range(2)])
-    crossed_grad, crossed_out = (exchange(c, "mp", 1) for c in crossing)
-
+    fed = feed(
+        chips,
+        toks,
+        [(expand_weight, shrink_weight), *foreign],
+        expand_bias[None, :],
+        hidden,
+        after=attn[:1] if CFG["MA3"] else (),
+    )
+    sums, keep = fed[:2]
+    got = [exchange(f, "dp", 1) for f in fed[6:]]
+
+    def passed(m, r):
+        return {1: (got[0], (m, r)), 2: (got[m % len(got)], (r,)), 4: (got[-1 if len(got) < 4 else 2 * m + r], ())}[len(got)]
+
+    entries = [[(keep, (m, 1)), passed(m, 1)] for m in range(2)]
+    if CFG["cross2"]:
+        crossing = add([(BF, [e]) for e in entries], "cross")
+        crossed = [exchange(c, "mp", 1) for c in crossing]
+    else:
+        crossing = add([(BF, entries)], "cross")
+        crossed = [exchange(crossing[0], "mp", 1)]
+
+    hold = {0: (), 1: (keep,), 2: (crossing[0],)}[CFG["at1"]]
+    tracks, attn_sent = reduce_chips(chips, attn[:2], attn[2:], "at1", hold)
     middle = depth // 2
-    entries = [at(attn_sums[z // middle], z % middle) for z in range(depth)]
-    parts = add([(BF, [e]) for e in entries[1:]])
-    arrived = [(exchange(p, "mp", j + 1), (0,)) for j, p in enumerate(parts)]
-    attn_own = add([(BF, [entries[0] + arrived])])[0]
-    attn_all = [attn_own] + [exchange(attn_own, "mp", j) for j in range(1, depth)]
+    entries = [at(tracks[z // middle], z % middle) for z in range(depth)]
+
+    def feed_sums():
+        hold = {0: (), 1: (attn_sent[0],), 2: (crossing[0],), 3: (attn_sent[0], crossing[0])}[CFG["fo1"]]
+        return reduce_chips(chips, fed[2:4], fed[4:6], "fo1", hold)
+
+    def rows_back(after):
+        return norm_back(
+            info,
+            residual_in,
+            upstream,
+            gain,
+            grad_attention,
+            keep,
+            passed(0, 0),
+            crossed[0],
+            shrink_bias_grad,
+            sums,
+            after=after,
+        )
+
+    def attention_parts(after):
+        return add([(BF, [e for j, e in enumerate(entries) if j & 1])], "parts", after=after)
 
     mine, away = [[], []], [[], []]
-    for k, f in enumerate((*others, own)):
-        pair, _ = reduce_chips(chips, f[3:5], f[5:7], (keep,))
-        if k < len(others):
-            both = add([(BF, [at(p, a) for p in pair for a in range(2)])])[0]
-            both = exchange(both, "mp", 2 * (k + 1))
-            pair = [[(both, (2 * n,))] for n in range(2)], [[(both, (2 * n + 1,))] for n in range(2)]
-        else:
-            pair = [at(p, 0) for p in pair], [at(p, 1) for p in pair]
+    if CFG["nb"] == 1:
+        grad_rows, small = rows_back(())
+    if CFG["first"]:
+        parts = attention_parts((small,) if CFG["nb"] == 1 and CFG["parts"] else ())
+        pair, sent = feed_sums()
+    else:
+        pair, sent = feed_sums()
+        parts = attention_parts({0: (), 1: (sent[0],), 2: (small,) if CFG["nb"] == 1 else ()}[CFG["parts"]])
+    if CFG["nb"] != 1:
+        grad_rows, small = rows_back((parts[0],) if CFG["nb"] else ())
+    hold = {0: (), 1: (parts[0],), 2: (small,)}[CFG["both"]]
+    for k in range(1, shards):
+        both = add([(BF, [at(p, k, a) for p in pair for a in range(2)])], "both", after=hold)[0]
+        both = exchange(both, "mp", 2 * k)
         for n in range(2):
-            mine[n] = mine[n] + pair[0][n]
-            away[n] = away[n] + pair[1][n]
-    mine, away = add([(F32, mine), (BF, away)])
+            mine[n].append((both, (2 * n,)))
+            away[n].append((both, (2 * n + 1,)))
+    if CFG["nb"] == 3:
+        pass
+    attn_own = add([(BF, [reduce_depth(parts[0], entries, depth)])], "aown")[0]
+    attn_all = gather_depth(attn_own, depth)
+    for n in range(2):
+        mine[n] += at(pair[n], 0, 0)
+        away[n] += at(pair[n], 0, 1)
+    mine, away = add([(F32, mine), (BF, away)], "mine")
     sibling = exchange(away, "dp", 1)
 
-    grad_rows, small = norm_back(
-        info,
-        residual_in,
-        upstream,
-        gain,
-        grad_attention,
-        keep,
-        passed,
-        crossed_grad,
-        shrink_bias_grad,
-        [f[2] for f in (own, *others)],
-    )
     residual_out = row_out(
-        info, residual_in, attention_out, keep, passed, crossed_out, shrink_bias[None, :]
+        info, residual_in, attention_out, keep, passed(1, 0), crossed[-1], shrink_bias[None, :]
     )
     for bit in range(depth.bit_length() - 1):
         small = small_sum(small, "mp", bit)

time: 208 us -> 171 us (0.82)
  waiting for transfers between devices: 111 us -> 70.8 us
  starting transfers between devices: 43.1 us -> 37.8 us
  Pallas kernels: 48.6 us -> 53.8 us
  local copies, waits for them, and re-layouts: 4.48 us -> 7.31 us
    ppermute x39 -> x33, waiting for transfers between devices: 111 us -> 70.8 us  [exchange(): return lax.ppermute(x, axis, [(i, i ^ flip) for i in range(n)])]
    ppermute x39 -> x33, starting transfers between devices: 43.1 us -> 37.8 us  [exchange(): return lax.ppermute(x, axis, [(i, i ^ flip) for i in range(n)])]
    pallas_call x26 -> x25, Pallas kernels: 48.6 us -> 53.8 us  [call(): pl.pallas_call(body, in_specs=[specs.get(n, VMEM) for n in range(count)]...]
    unnamed x38 -> x60, local copies, waits for them, and re-layouts: 4.48 us -> 7.31 us
  transfers between devices with their start and end apart: 39 -> 33, of which waited for: 20 -> 16; matrix products, arithmetic and copies ran while one was open for 0% -> 0% of each run, Pallas kernels for 19% -> 30%
where the time goes in v3:
time: 171 us
  waiting for transfers between devices  70.8 us (41%)
  Pallas kernels  53.8 us (31%)
  starting transfers between devices  37.8 us (22%)
  local copies, waits for them, and re-layouts  7.31 us (4%)
    ppermute x33, waiting for transfers between devices, exchange(): return lax.ppermute(x, axis, [(i, i ^ flip) for i in range(n)])  70.8 us
    pallas_call x25, Pallas kernels, call(): pl.pallas_call(body, in_specs=[specs.get(n, VMEM) for n in range(count)]...  53.8 us
    ppermute x33, starting transfers between devices, exchange(): return lax.ppermute(x, axis, [(i, i ^ flip) for i in range(n)])  37.8 us
    unnamed x60, local copies, waits for them, and re-layouts  7.31 us
  transfers between devices with their start and end apart: 33, of which 16 were waited for; matrix products, arithmetic and copies ran while one was open for 0% of the time, Pallas kernels for 30%

profile of v3, /device:TPU:0, one launch (start us, length us, event | category | flops | bytes accessed | tf_op | source)
XLA Modules:
  0.0 170.7 jit_solution(10547246074477828637)
XLA Ops:
  0.6 1.9 %shard_map.213.refs_7_ = bf16[272,1024]{1,0:T(8,128)(2,1)} custom-call(f32[1,1024]{1,0:T(1,128)} %bitcast.12, bf16[1024,1024]{1,0:T(8,128)(2,1)} %refs_8_.1, bf16[1024,1024]{1,0:T(8,128)(2,1)} %refs_9_.1), custom_call_target="tpu_custom_call" | custom-call | flops 3000000000 | bytes 1024 | tf_op jit(solution)/shard_map/pallas_call | solution.py:47
  2.6 4.1 %collective-permute-start.3 = (bf16[272,1024]{1,0:T(8,128)(2,1)}, bf16[272,1024]{1,0:T(8,128)(2,1)S(1)}, u32[]{:S(2)}, u32[]{:S(2)}) collective-permute-start(bf16[272,1024]{1,0:T(8,128)(2,1)} %shard_map.213.refs_7_), channel_id=1, source_target_pairs={{0,2},{1,3},{2,0},{3,1},{4,6},{5,7},{6,4},{7,5},{8,10},{9,11},{10,... | collective-permute-start | bytes 1671176 | tf_op jit(solution)/shard_map/ppermute | solution.py:834
  6.7 3.4 %shard_map.214 = (s32[24,256]{1,0:T(8,128)}, bf16[256,1024]{1,0:T(8,128)(2,1)}, bf16[256,1024]{1,0:T(8,128)(2,1)}, f32[1,1024]{1,0:T(1,128)}) custom-call(s32[1,16]{1,0:T(1,128)} %refs_0_.1, s32[1,4]{1,0:T(1,128)} %refs_1_.6, s32[1,4]{1,0:T(1,128)} %refs_2_.5, bf16[256,1024]{1,0:T(8,128)(2,1)} %refs_1_.9, bf16[256,1024]{1,0:T(8,128)(2,1)} %refs_2_.7, ...), custom_call_target="tpu_custom_call" | custom-call | flops 1000000000 | bytes 1024 | tf_op jit(solution)/shard_map/pallas_call | solution.py:47
  10.7 1.0 copy-done.6
  11.7 1.0 copy-done.8
  13.5 11.7 %shard_map.215.refs_0_.refs_4_ = bf16[4,256,1024]{2,1,0:T(8,128)(2,1)} custom-call(s32[24,256]{1,0:T(8,128)S(1)} %copy-done.10, bf16[256,1024]{1,0:T(8,128)(2,1)S(1)} %copy-done.6, bf16[256,1024]{1,0:T(8,128)(2,1)S(1)} %copy-done.8, f32[1,256]{1,0:T(1,128)S(1)} %copy-done.15, bf16[1024,3072]{1,0:T(8,128)(2,1)} %refs_1_.7, bf16[1024,1024]{1,0:T(8,128)(2,1)} %refs_2_.6), custom_call_target="tpu_custom_call" | custom-call | flops 50000000 | bytes 1024 | tf_op jit(solution)/shard_map/pallas_call | solution.py:47
  25.2 1.6 copy-done.1
  26.8 3.4 %shard_map.216 = (f32[256,1024]{1,0:T(8,128)S(1)}, f32[256,1024]{1,0:T(8,128)S(1)}) custom-call(bf16[4,256,1024]{2,1,0:T(8,128)(2,1)S(1)} %copy-done.1, bf16[1024,3072]{1,0:T(8,128)(2,1)S(1)} %bitcast.9, bf16[1024,1024]{1,0:T(8,128)(2,1)S(1)} %copy-done), custom_call_target="tpu_custom_call" | custom-call | flops 1000000000 | bytes 1024 | tf_op jit(solution)/shard_map/pallas_call | solution.py:47
  30.3 1.0 copy-done.17
  32.2 1.6 collective-permute-start.2
  33.8 2.4 %collective-permute-start.10 = (bf16[272,1024]{1,0:T(8,128)(2,1)S(1)}, bf16[272,1024]{1,0:T(8,128)(2,1)S(1)}, u32[]{:S(2)}, u32[]{:S(2)}) collective-permute-start(bf16[272,1024]{1,0:T(8,128)(2,1)S(1)} %collective-permute-done.3.refs_6_.refs_10_), channel_id=1, source_target_pairs={{0,24},{4,28},{8,16},{12,20},{16,8},{20,12},{24,0},{28,4},{1,25},{... | collective-permute-start | bytes 1671176 | tf_op jit(solution)/shard_map/ppermute | solution.py:834
  37.9 1.0 copy-done.24
  38.9 3.9 %shard_map.217 = (bf16[2,2,128,1024]{3,2,1,0:T(8,128)(2,1)S(1)}, bf16[2,2,128,1024]{3,2,1,0:T(8,128)(2,1)S(1)}, bf16[2,2,128,1024]{3,2,1,0:T(8,128)(2,1)S(1)}, bf16[2,2,128,1024]{3,2,1,0:T(8,128)(2,1)S(1)}) custom-call(bf16[256,1024]{1,0:T(8,128)(2,1)S(1)} %copy-done.6, bf16[256,1024]{1,0:T(8,128)(2,1)S(1)} %copy-done.24, bf16[256,1024]{1,0:T(8,128)(2,1)S(1)} %copy-done.8, ...), custom_call_target="tpu_custom_call" | custom-call | flops 24999999488 | bytes 1024 | tf_op jit(solution)/shard_map/pallas_call | solution.py:47
  42.8 14.9 %collective-permute-done.4.refs_5_ = bf16[256,1024]{1,0:T(8,128)(2,1)S(1)} collective-permute-done((bf16[256,1024]{1,0:T(8,128)(2,1)S(1)}, bf16[256,1024]{1,0:T(8,128)(2,1)S(1)}, u32[]{:S(2)}, u32[]{:S(2)}) %collective-permute-start.4) | collective-permute-done | bytes 524320 | tf_op jit(solution)/shard_map/ppermute | solution.py:834
  58.2 1.4 collective-permute-done.7.refs_7_
  60.4 1.5 collective-permute-start.20
  61.9 1.5 collective-permute-start.19
  63.5 17.9 %shard_map.218 = (f32[2,512]{1,0:T(2,128)S(1)}, bf16[2,2,256,1024]{3,2,1,0:T(8,128)(2,1)S(1)}, bf16[2,2,2,512,128]{4,3,2,1,0:T(8,128)(2,1)S(1)}, bf16[2,2,2,512,...) custom-call(bf16[256,1024]{1,0:T(8,128)(2,1)S(1)} %copy-done.7, ...), custom_call_target="tpu_custom_call" | custom-call | flops 49999998976 | bytes 1024 | tf_op jit(solution)/shard_map/pallas_call | solution.py:47
  81.4 4.2 %collective-permute-done.20.refs_3_.refs_4_.refs_1_ = bf16[2,2,128,1024]{3,2,1,0:T(8,128)(2,1)S(1)} collective-permute-done((bf16[2,2,128,1024]{3,2,1,0:T(8,128)(2,1)S(1)}, bf16[2,2,128,1024]{3,2,1,0:T(8,128)(2,1)S(1)}, u32[]{:S(2)}, u32[]{:S(2)}) %collective-permute-start.20) | collective-permute-done | bytes 1048608 | tf_op jit(solution)/shard_map/ppermute | solution.py:834
  85.6 1.2 collective-permute-done.19.refs_1_
  87.6 1.5 collective-permute-start.22
  89.1 1.0 shard_map.219
  90.1 1.6 collective-permute-start.13
  91.8 8.2 %collective-permute-done.21.refs_2_ = bf16[1,2,128,1024]{3,2,1,0:T(8,128)(2,1)S(1)} collective-permute-done((bf16[1,2,128,1024]{3,2,1,0:T(8,128)(2,1)S(1)}, bf16[1,2,128,1024]{3,2,1,0:T(8,128)(2,1)S(1)}, u32[]{:S(2)}, u32[]{:S(2)}) %collective-permute-start.21) | collective-permute-done | bytes 524320 | tf_op jit(solution)/shard_map/ppermute | solution.py:834
  100.5 1.7 collective-permute-start.23
  102.1 1.5 collective-permute-start.27
  103.6 1.4 collective-permute-start.28
  105.1 1.1 shard_map.221
  106.8 7.4 %collective-permute-done.23.refs_3_ = bf16[2,128,1024]{2,1,0:T(8,128)(2,1)S(1)} collective-permute-done((bf16[2,128,1024]{2,1,0:T(8,128)(2,1)S(1)}, bf16[2,128,1024]{2,1,0:T(8,128)(2,1)S(1)}, u32[]{:S(2)}, u32[]{:S(2)}) %collective-permute-start.23) | collective-permute-done | bytes 524320 | tf_op jit(solution)/shard_map/ppermute | solution.py:834
  114.3 1.7 %collective-permute-start.24 = (bf16[1,128,1024]{2,1,0:T(8,128)(2,1)S(1)}, bf16[1,128,1024]{2,1,0:T(8,128)(2,1)S(1)}, u32[]{:S(2)}, u32[]{:S(2)}) collective-permute-start(bf16[1,128,1024]{2,1,0:T(8,128)(2,1)S(1)} %shard_map.230), channel_id=1, source_target_pairs={{0,2},{1,3},{2,0},{3,1},{4,6},{5,7},{6,4},{7,5},{8,10},{9,11},{10,... | collective-permute-start | bytes 786440 | tf_op jit(solution)/shard_map/ppermute | solution.py:834
  116.0 1.3 collective-permute-start.15
  117.3 7.4 %collective-permute-done.27.refs_1_.refs_2_ = bf16[2,2,2,512,128]{4,3,2,1,0:T(8,128)(2,1)S(1)} collective-permute-done((bf16[2,2,2,512,128]{4,3,2,1,0:T(8,128)(2,1)S(1)}, bf16[2,2,2,512,128]{4,3,2,1,0:T(8,128)(2,1)S(1)}, u32[]{:S(2)}, u32[]{:S(2)}) %collective-permute-start.27) | collective-permute-done | bytes 1048608 | tf_op jit(solution)/shard_map/ppermute | solution.py:834
  124.8 1.8 %collective-permute-done.28.refs_3_.refs_4_.refs_5_ = bf16[2,2,2,512,128]{4,3,2,1,0:T(8,128)(2,1)S(1)} collective-permute-done((bf16[2,2,2,512,128]{4,3,2,1,0:T(8,128)(2,1)S(1)}, bf16[2,2,2,512,128]{4,3,2,1,0:T(8,128)(2,1)S(1)}, u32[]{:S(2)}, u32[]{:S(2)}) %collective-permute-start.28) | collective-permute-done | bytes 1048608 | tf_op jit(solution)/shard_map/ppermute | solution.py:834
  126.9 1.5 collective-permute-start.29
  129.5 1.8 %collective-permute-start.25 = (bf16[1,128,1024]{2,1,0:T(8,128)(2,1)S(1)}, bf16[1,128,1024]{2,1,0:T(8,128)(2,1)S(1)}, u32[]{:S(2)}, u32[]{:S(2)}) collective-permute-start(bf16[1,128,1024]{2,1,0:T(8,128)(2,1)S(1)} %shard_map.231.refs_0_.refs_1_), channel_id=1, source_target_pairs={{0,2},{1,3},{2,0},{3,1},{4,6},{5,7},{6,4},{7,5},{8,10},{9,11},{10,... | collective-permute-start | bytes 786440 | tf_op jit(solution)/shard_map/ppermute | solution.py:834
  131.3 5.9 %collective-permute-done.29.refs_2_.refs_3_ = bf16[1,2,2,512,128]{4,3,2,1,0:T(8,128)(2,1)S(1)} collective-permute-done((bf16[1,2,2,512,128]{4,3,2,1,0:T(8,128)(2,1)S(1)}, bf16[1,2,2,512,128]{4,3,2,1,0:T(8,128)(2,1)S(1)}, u32[]{:S(2)}, u32[]{:S(2)}) %collective-permute-start.29) | collective-permute-done | bytes 524320 | tf_op jit(solution)/shard_map/ppermute | solution.py:834
  137.5 1.0 shard_map.235
  138.6 1.9 %collective-permute-start.31 = (bf16[4,512,128]{2,1,0:T(8,128)(2,1)}, bf16[4,512,128]{2,1,0:T(8,128)(2,1)}, u32[]{:S(2)}, u32[]{:S(2)}) collective-permute-start(bf16[4,512,128]{2,1,0:T(8,128)(2,1)} %shard_map.235), channel_id=1, source_target_pairs={{0,2},{1,3},{2,0},{3,1},{4,6},{5,7},{6,4},{7,5},{8,10},{9,11},{10,... | collective-permute-start | bytes 1572872 | tf_op jit(solution)/shard_map/ppermute | solution.py:834
  141.0 6.0 %collective-permute-done.25.refs_1_.refs_2_ = bf16[1,128,1024]{2,1,0:T(8,128)(2,1)S(1)} collective-permute-done((bf16[1,128,1024]{2,1,0:T(8,128)(2,1)S(1)}, bf16[1,128,1024]{2,1,0:T(8,128)(2,1)S(1)}, u32[]{:S(2)}, u32[]{:S(2)}) %collective-permute-start.25) | collective-permute-done | bytes 262176 | tf_op jit(solution)/shard_map/ppermute | solution.py:834
  147.1 4.5 %collective-permute-start.26 = (bf16[2,128,1024]{2,1,0:T(8,128)(2,1)S(1)}, bf16[2,128,1024]{2,1,0:T(8,128)(2,1)S(1)}, u32[]{:S(2)}, u32[]{:S(2)}) collective-permute-start(bf16[2,128,1024]{2,1,0:T(8,128)(2,1)S(1)} %shard_map.232), channel_id=1, source_target_pairs={{0,1},{1,0},{2,3},{3,2},{4,5},{5,4},{6,7},{7,6},{8,9},{9,8},{10,11... | collective-permute-start | bytes 1572872 | tf_op jit(solution)/shard_map/ppermute | solution.py:834
  152.2 2.3 %shard_map.220 = bf16[256,1024]{1,0:T(8,128)(2,1)} custom-call(s32[24,256]{1,0:T(8,128)S(1)} %copy-done.12, bf16[256,1024]{1,0:T(8,128)(2,1)S(1)} %copy-done.5, f32[256,1024]{1,0:T(8,128)S(1)} %copy-done.18, bf16[2,2,256,1024]{3,2,1,0:T(8,128)(2,1)S(1)} %get-tuple-element.69.refs_0_.refs_3_.refs_5_.refs_4_, ...), custom_call_target="tpu_custom_call" | custom-call | flops 12000000000 | bytes 1024 | tf_op jit(solution)/shard_map/pallas_call | solution.py:47
  154.6 1.0 collective-permute-done.18.refs_1_
  155.6 1.1 shard_map.227
  156.7 8.0 %collective-permute-done.31.refs_0_ = bf16[4,512,128]{2,1,0:T(8,128)(2,1)} collective-permute-done((bf16[4,512,128]{2,1,0:T(8,128)(2,1)}, bf16[4,512,128]{2,1,0:T(8,128)(2,1)}, u32[]{:S(2)}, u32[]{:S(2)}) %collective-permute-start.31) | collective-permute-done | bytes 524320 | tf_op jit(solution)/shard_map/ppermute | solution.py:834
  164.8 1.3 shard_map.236
  166.1 1.8 %collective-permute-done.26.refs_3_ = bf16[2,128,1024]{2,1,0:T(8,128)(2,1)S(1)} collective-permute-done((bf16[2,128,1024]{2,1,0:T(8,128)(2,1)S(1)}, bf16[2,128,1024]{2,1,0:T(8,128)(2,1)S(1)}, u32[]{:S(2)}, u32[]{:S(2)}) %collective-permute-start.26) | collective-permute-done | bytes 524320 | tf_op jit(solution)/shard_map/ppermute | solution.py:834
  167.9 1.7 shard_map.233
  169.6 1.1 shard_map.237
  (104 shorter events, 10.4 us)
Async XLA Ops:
  2.6 29.5 %collective-permute-start.3 = (bf16[272,1024]{1,0:T(8,128)(2,1)}, bf16[272,1024]{1,0:T(8,128)(2,1)S(1)}, u32[]{:S(2)}, u32[]{:S(2)}) collective-permute-start(bf16[272,1024]{1,0:T(8,128)(2,1)} %shard_map.213.refs_7_), channel_id=1, source_target_pairs={{0,2},{1,3},{2,0},{3,1},{4,6},{5,7},{6,4},{7,5},{8,10},{9,11},{10,... | collective-permute-start | bytes 1671176 | tf_op jit(solution)/shard_map/ppermute | solution.py:834
  6.7 18.5 %slice-start = ((s8[6291456]{0:T(1024)(128)(4,1)}), s8[2097152]{0:T(1024)(128)(4,1)S(1)}, s32[]{:S(2)}) async-start(s8[6291456]{0:T(1024)(128)(4,1)} %bitcast.8), calls=%async_computation | async-start | bytes 4194304
  10.1 21.1 %collective-permute-start = (bf16[256,1024]{1,0:T(8,128)(2,1)}, bf16[256,1024]{1,0:T(8,128)(2,1)S(1)}, u32[]{:S(2)}, u32[]{:S(2)}) collective-permute-start(bf16[256,1024]{1,0:T(8,128)(2,1)} %get-tuple-element.60.refs_1_.refs_0_), channel_id=1, source_target_pairs={{0,4},{4,0},{8,12},{12,8},{16,20},{20,16},{24,28},{28,24},{1,5},{5... | collective-permute-start | bytes 1572872 | tf_op jit(solution)/shard_map/ppermute | solution.py:834
  10.2 21.8 %collective-permute-start.1 = (bf16[256,1024]{1,0:T(8,128)(2,1)}, bf16[256,1024]{1,0:T(8,128)(2,1)}, u32[]{:S(2)}, u32[]{:S(2)}) collective-permute-start(bf16[256,1024]{1,0:T(8,128)(2,1)} %get-tuple-element.61.refs_2_.refs_1_), channel_id=1, source_target_pairs={{0,4},{4,0},{8,12},{12,8},{16,20},{20,16},{24,28},{28,24},{1,5},{5... | collective-permute-start | bytes 1572872 | tf_op jit(solution)/shard_map/ppermute | solution.py:834
  13.5 11.7 %slice-start.1 = ((s8[6291456]{0:T(1024)(128)(4,1)}), s8[4194304]{0:T(1024)(128)(4,1)S(1)}, s32[]{:S(2)}) async-start(s8[6291456]{0:T(1024)(128)(4,1)} %bitcast.8), calls=%async_computation.1 | async-start | bytes 8388608
  13.5 11.7 %copy-start = (bf16[1024,1024]{1,0:T(8,128)(2,1)S(1)}, bf16[1024,1024]{1,0:T(8,128)(2,1)}, u32[]{:S(2)}) copy-start(bf16[1024,1024]{1,0:T(8,128)(2,1)} %refs_2_.6) | copy-start | bytes 6291460
  26.8 11.1 %copy-start.2 = (bf16[4,256,1024]{2,1,0:T(8,128)(2,1)S(1)}, bf16[4,256,1024]{2,1,0:T(8,128)(2,1)}, u32[]{:S(2)}) copy-start(bf16[4,256,1024]{2,1,0:T(8,128)(2,1)} %shard_map.215.refs_0_.refs_4_) | copy-start | bytes 6291460
  26.8 36.6 %copy-start.26 = (f32[1024]{0:T(1024)S(1)}, f32[1024]{0:T(1024)}, u32[]{:S(2)}) copy-start(f32[1024]{0:T(1024)} %param.21) | copy-start | bytes 12292
  32.0 31.4 %copy-start.7 = (bf16[256,1024]{1,0:T(8,128)(2,1)S(1)}, bf16[256,1024]{1,0:T(8,128)(2,1)}, u32[]{:S(2)}) copy-start(bf16[256,1024]{1,0:T(8,128)(2,1)} %get-tuple-element.60.refs_1_.refs_0_) | copy-start | bytes 1572868
  32.0 31.4 %copy-start.9 = (bf16[256,1024]{1,0:T(8,128)(2,1)S(1)}, bf16[256,1024]{1,0:T(8,128)(2,1)}, u32[]{:S(2)}) copy-start(bf16[256,1024]{1,0:T(8,128)(2,1)} %get-tuple-element.61.refs_2_.refs_1_) | copy-start | bytes 1572868
  32.1 31.4 %copy-start.16 = (bf16[1024,1024]{1,0:T(8,128)(2,1)S(1)}, bf16[1024,1024]{1,0:T(8,128)(2,1)}, u32[]{:S(2)}) copy-start(bf16[1024,1024]{1,0:T(8,128)(2,1)} %refs_8_.1) | copy-start | bytes 6291460
  32.1 5.2 %collective-permute-start.5 = (bf16[4,256,1024]{2,1,0:T(8,128)(2,1)S(1)}, bf16[4,256,1024]{2,1,0:T(8,128)(2,1)S(1)}, u32[]{:S(2)}, u32[]{:S(2)}) collective-permute-start(bf16[4,256,1024]{2,1,0:T(8,128)(2,1)S(1)} %copy-done.1), channel_id=1, source_target_pairs={{0,4},{4,0},{8,12},{12,8},{16,20},{20,16},{24,28},{28,24},{1,5},{5... | collective-permute-start | bytes 6291464 | tf_op jit(solution)/shard_map/ppermute | solution.py:834
  32.2 25.5 %collective-permute-start.2 = (bf16[256,1024]{1,0:T(8,128)(2,1)S(1)}, bf16[256,1024]{1,0:T(8,128)(2,1)S(1)}, u32[]{:S(2)}, u32[]{:S(2)}) collective-permute-start(bf16[256,1024]{1,0:T(8,128)(2,1)S(1)} %copy-done.6), channel_id=1, source_target_pairs={{0,1},{1,0},{2,3},{3,2},{4,5},{5,4},{6,7},{7,6},{8,9},{9,8},{10,11... | collective-permute-start | bytes 1572872 | tf_op jit(solution)/shard_map/ppermute | solution.py:834
  33.8 29.6 %collective-permute-start.10 = (bf16[272,1024]{1,0:T(8,128)(2,1)S(1)}, bf16[272,1024]{1,0:T(8,128)(2,1)S(1)}, u32[]{:S(2)}, u32[]{:S(2)}) collective-permute-start(bf16[272,1024]{1,0:T(8,128)(2,1)S(1)} %collective-permute-done.3.refs_6_.refs_10_), channel_id=1, source_target_pairs={{0,24},{4,28},{8,16},{12,20},{16,8},{20,12},{24,0},{28,4},{1,25},{... | collective-permute-start | bytes 1671176 | tf_op jit(solution)/shard_map/ppermute | solution.py:834
  36.2 27.2 %collective-permute-start.8 = (bf16[272,1024]{1,0:T(8,128)(2,1)S(1)}, bf16[272,1024]{1,0:T(8,128)(2,1)S(1)}, u32[]{:S(2)}, u32[]{:S(2)}) collective-permute-start(bf16[272,1024]{1,0:T(8,128)(2,1)S(1)} %collective-permute-done.3.refs_6_.refs_10_), channel_id=1, source_target_pairs={{0,8},{4,12},{8,0},{12,4},{16,24},{20,28},{24,16},{28,20},{1,9},{5... | collective-permute-start | bytes 1671176 | tf_op jit(solution)/shard_map/ppermute | solution.py:834
  36.8 26.6 %collective-permute-start.9 = (bf16[272,1024]{1,0:T(8,128)(2,1)S(1)}, bf16[272,1024]{1,0:T(8,128)(2,1)S(1)}, u32[]{:S(2)}, u32[]{:S(2)}) collective-permute-start(bf16[272,1024]{1,0:T(8,128)(2,1)S(1)} %collective-permute-done.3.refs_6_.refs_10_), channel_id=1, source_target_pairs={{0,16},{4,20},{8,24},{12,28},{16,0},{20,4},{24,8},{28,12},{1,17},{... | collective-permute-start | bytes 1671176 | tf_op jit(solution)/shard_map/ppermute | solution.py:834
  37.3 20.4 %collective-permute-start.4 = (bf16[256,1024]{1,0:T(8,128)(2,1)S(1)}, bf16[256,1024]{1,0:T(8,128)(2,1)S(1)}, u32[]{:S(2)}, u32[]{:S(2)}) collective-permute-start(bf16[256,1024]{1,0:T(8,128)(2,1)S(1)} %copy-done.8), channel_id=1, source_target_pairs={{0,1},{1,0},{2,3},{3,2},{4,5},{5,4},{6,7},{7,6},{8,9},{9,8},{10,11... | collective-permute-start | bytes 1572872 | tf_op jit(solution)/shard_map/ppermute | solution.py:834
  38.9 24.5 %copy-start.25 = (bf16[256,1024]{1,0:T(8,128)(2,1)S(1)}, bf16[256,1024]{1,0:T(8,128)(2,1)}, u32[]{:S(2)}) copy-start(bf16[256,1024]{1,0:T(8,128)(2,1)} %copy-done.23) | copy-start | bytes 1572868
  57.7 1.9 %collective-permute-start.7 = (bf16[256,1024]{1,0:T(8,128)(2,1)S(1)}, bf16[256,1024]{1,0:T(8,128)(2,1)S(1)}, u32[]{:S(2)}, u32[]{:S(2)}) collective-permute-start(bf16[256,1024]{1,0:T(8,128)(2,1)S(1)} %collective-permute-done.4.refs_5_), channel_id=1, source_target_pairs={{0,4},{4,0},{8,12},{12,8},{16,20},{20,16},{24,28},{28,24},{1,5},{5... | collective-permute-start | bytes 1572872 | tf_op jit(solution)/shard_map/ppermute | solution.py:834
  57.7 2.7 %collective-permute-start.6 = (bf16[256,1024]{1,0:T(8,128)(2,1)S(1)}, bf16[256,1024]{1,0:T(8,128)(2,1)S(1)}, u32[]{:S(2)}, u32[]{:S(2)}) collective-permute-start(bf16[256,1024]{1,0:T(8,128)(2,1)S(1)} %collective-permute-done.2.refs_4_), channel_id=1, source_target_pairs={{0,4},{4,0},{8,12},{12,8},{16,20},{20,16},{24,28},{28,24},{1,5},{5... | collective-permute-start | bytes 1572872 | tf_op jit(solution)/shard_map/ppermute | solution.py:834
  60.4 25.2 %collective-permute-start.20 = (bf16[2,2,128,1024]{3,2,1,0:T(8,128)(2,1)S(1)}, bf16[2,2,128,1024]{3,2,1,0:T(8,128)(2,1)S(1)}, u32[]{:S(2)}, u32[]{:S(2)}) collective-permute-start(bf16[2,2,128,1024]{3,2,1,0:T(8,128)(2,1)S(1)} %get-tuple-element.85), channel_id=1, source_target_pairs={{0,16},{4,20},{8,24},{12,28},{16,0},{20,4},{24,8},{28,12},{1,17},{... | collective-permute-start | bytes 3145736 | tf_op jit(solution)/shard_map/ppermute | solution.py:834
  61.9 24.9 %collective-permute-start.19 = (bf16[2,2,128,1024]{3,2,1,0:T(8,128)(2,1)S(1)}, bf16[2,2,128,1024]{3,2,1,0:T(8,128)(2,1)S(1)}, u32[]{:S(2)}, u32[]{:S(2)}) collective-permute-start(bf16[2,2,128,1024]{3,2,1,0:T(8,128)(2,1)S(1)} %get-tuple-element.68.refs_15_), channel_id=1, source_target_pairs={{0,8},{4,12},{8,0},{12,4},{16,24},{20,28},{24,16},{28,20},{1,9},{5... | collective-permute-start | bytes 3145736 | tf_op jit(solution)/shard_map/ppermute | solution.py:834
  81.3 7.8 %collective-permute-start.11 = (bf16[2,2,256,1024]{3,2,1,0:T(8,128)(2,1)S(1)}, bf16[2,2,256,1024]{3,2,1,0:T(8,128)(2,1)S(1)}, u32[]{:S(2)}, u32[]{:S(2)}) collective-permute-start(bf16[2,2,256,1024]{3,2,1,0:T(8,128)(2,1)S(1)} %get-tuple-element.70), channel_id=1, source_target_pairs={{0,4},{4,0},{8,12},{12,8},{16,20},{20,16},{24,28},{28,24},{1,5},{5... | collective-permute-start | bytes 6291464 | tf_op jit(solution)/shard_map/ppermute | solution.py:834
  87.1 12.9 %collective-permute-start.21 = (bf16[1,2,128,1024]{3,2,1,0:T(8,128)(2,1)S(1)}, bf16[1,2,128,1024]{3,2,1,0:T(8,128)(2,1)S(1)}, u32[]{:S(2)}, u32[]{:S(2)}) collective-permute-start(bf16[1,2,128,1024]{3,2,1,0:T(8,128)(2,1)S(1)} %get-tuple-element.86.refs_4_), channel_id=1, source_target_pairs={{0,16},{4,20},{8,24},{12,28},{16,0},{20,4},{24,8},{28,12},{1,17},{... | collective-permute-start | bytes 1572872 | tf_op jit(solution)/shard_map/ppermute | solution.py:834
  87.6 12.6 %collective-permute-start.22 = (bf16[1,2,128,1024]{3,2,1,0:T(8,128)(2,1)S(1)}, bf16[1,2,128,1024]{3,2,1,0:T(8,128)(2,1)S(1)}, u32[]{:S(2)}, u32[]{:S(2)}) collective-permute-start(bf16[1,2,128,1024]{3,2,1,0:T(8,128)(2,1)S(1)} %get-tuple-element.87), channel_id=1, source_target_pairs={{0,8},{4,12},{8,0},{12,4},{16,24},{20,28},{24,16},{28,20},{1,9},{5... | collective-permute-start | bytes 1572872 | tf_op jit(solution)/shard_map/ppermute | solution.py:834
  90.1 14.9 %copy-start.3 = (bf16[256,1024]{1,0:T(8,128)(2,1)S(1)}, bf16[256,1024]{1,0:T(8,128)(2,1)}, u32[]{:S(2)}) copy-start(bf16[256,1024]{1,0:T(8,128)(2,1)} %refs_2_.7) | copy-start | bytes 1572868
  90.1 14.9 %copy-start.4 = (bf16[256,1024]{1,0:T(8,128)(2,1)S(1)}, bf16[256,1024]{1,0:T(8,128)(2,1)}, u32[]{:S(2)}) copy-start(bf16[256,1024]{1,0:T(8,128)(2,1)} %refs_1_.9) | copy-start | bytes 1572868
  90.1 14.9 %copy-start.11 = (s32[24,256]{1,0:T(8,128)S(1)}, s32[24,256]{1,0:T(8,128)}, u32[]{:S(2)}) copy-start(s32[24,256]{1,0:T(8,128)} %get-tuple-element.56.refs_0_) | copy-start | bytes 73732
  90.1 14.9 %copy-start.13 = (f32[1024]{0:T(1024)S(1)}, f32[1024]{0:T(1024)}, u32[]{:S(2)}) copy-start(f32[1024]{0:T(1024)} %param.16) | copy-start | bytes 12292
  90.1 15.0 %copy-start.14 = (f32[1,1024]{1,0:T(1,128)S(1)}, f32[1,1024]{1,0:T(1,128)}, u32[]{:S(2)}) copy-start(f32[1,1024]{1,0:T(1,128)} %get-tuple-element.73.refs_8_) | copy-start | bytes 12292
  90.1 14.9 %collective-permute-start.13 = (bf16[1,256,1024]{2,1,0:T(8,128)(2,1)S(1)}, bf16[1,256,1024]{2,1,0:T(8,128)(2,1)S(1)}, u32[]{:S(2)}, u32[]{:S(2)}) collective-permute-start(bf16[1,256,1024]{2,1,0:T(8,128)(2,1)S(1)} %get-tuple-element.72.refs_5_), channel_id=1, source_target_pairs={{0,1},{1,0},{2,3},{3,2},{4,5},{5,4},{6,7},{7,6},{8,9},{9,8},{10,11... | collective-permute-start | bytes 1572872 | tf_op jit(solution)/shard_map/ppermute | solution.py:834
  100.5 13.7 %collective-permute-start.23 = (bf16[2,128,1024]{2,1,0:T(8,128)(2,1)S(1)}, bf16[2,128,1024]{2,1,0:T(8,128)(2,1)S(1)}, u32[]{:S(2)}, u32[]{:S(2)}) collective-permute-start(bf16[2,128,1024]{2,1,0:T(8,128)(2,1)S(1)} %shard_map.229.refs_6_), channel_id=1, source_target_pairs={{0,1},{1,0},{2,3},{3,2},{4,5},{5,4},{6,7},{7,6},{8,9},{9,8},{10,11... | collective-permute-start | bytes 1572872 | tf_op jit(solution)/shard_map/ppermute | solution.py:834
  102.1 22.7 %collective-permute-start.27 = (bf16[2,2,2,512,128]{4,3,2,1,0:T(8,128)(2,1)S(1)}, bf16[2,2,2,512,128]{4,3,2,1,0:T(8,128)(2,1)S(1)}, u32[]{:S(2)}, u32[]{:S(2)}) collective-permute-start(bf16[2,2,2,512,128]{4,3,2,1,0:T(8,128)(2,1)S(1)} %get-tuple-element.91), channel_id=1, source_target_pairs={{0,8},{4,12},{8,0},{12,4},{16,24},{20,28},{24,16},{28,20},{1,9},{5... | collective-permute-start | bytes 3145736 | tf_op jit(solution)/shard_map/ppermute | solution.py:834
  103.6 23.0 %collective-permute-start.28 = (bf16[2,2,2,512,128]{4,3,2,1,0:T(8,128)(2,1)S(1)}, bf16[2,2,2,512,128]{4,3,2,1,0:T(8,128)(2,1)S(1)}, u32[]{:S(2)}, u32[]{:S(2)}) collective-permute-start(bf16[2,2,2,512,128]{4,3,2,1,0:T(8,128)(2,1)S(1)} %get-tuple-element.93), channel_id=1, source_target_pairs={{0,16},{4,20},{8,24},{12,28},{16,0},{20,4},{24,8},{28,12},{1,17},{... | collective-permute-start | bytes 3145736 | tf_op jit(solution)/shard_map/ppermute | solution.py:834
  106.2 9.8 %collective-permute-start.14 = (f32[6,1024]{1,0:T(8,128)S(1)}, f32[6,1024]{1,0:T(8,128)S(1)}, u32[]{:S(2)}, u32[]{:S(2)}) collective-permute-start(f32[6,1024]{1,0:T(8,128)S(1)} %get-tuple-element.75.refs_0_), channel_id=1, source_target_pairs={{0,1},{1,0},{2,3},{3,2},{4,5},{5,4},{6,7},{7,6},{8,9},{9,8},{10,11... | collective-permute-start | bytes 73736 | tf_op jit(solution)/shard_map/ppermute | solution.py:834
  114.3 15.0 %collective-permute-start.24 = (bf16[1,128,1024]{2,1,0:T(8,128)(2,1)S(1)}, bf16[1,128,1024]{2,1,0:T(8,128)(2,1)S(1)}, u32[]{:S(2)}, u32[]{:S(2)}) collective-permute-start(bf16[1,128,1024]{2,1,0:T(8,128)(2,1)S(1)} %shard_map.230), channel_id=1, source_target_pairs={{0,2},{1,3},{2,0},{3,1},{4,6},{5,7},{6,4},{7,5},{8,10},{9,11},{10,... | collective-permute-start | bytes 786440 | tf_op jit(solution)/shard_map/ppermute | solution.py:834
  116.0 15.2 %collective-permute-start.15 = (f32[6,1024]{1,0:T(8,128)S(1)}, f32[6,1024]{1,0:T(8,128)S(1)}, u32[]{:S(2)}, u32[]{:S(2)}) collective-permute-start(f32[6,1024]{1,0:T(8,128)S(1)} %shard_map.222.refs_0_), channel_id=1, source_target_pairs={{0,2},{1,3},{2,0},{3,1},{4,6},{5,7},{6,4},{7,5},{8,10},{9,11},{10,... | collective-permute-start | bytes 73736 | tf_op jit(solution)/shard_map/ppermute | solution.py:834
  126.9 10.4 %collective-permute-start.29 = (bf16[1,2,2,512,128]{4,3,2,1,0:T(8,128)(2,1)S(1)}, bf16[1,2,2,512,128]{4,3,2,1,0:T(8,128)(2,1)S(1)}, u32[]{:S(2)}, u32[]{:S(2)}) collective-permute-start(bf16[1,2,2,512,128]{4,3,2,1,0:T(8,128)(2,1)S(1)} %get-tuple-element.94), channel_id=1, source_target_pairs={{0,16},{4,20},{8,24},{12,28},{16,0},{20,4},{24,8},{28,12},{1,17},{... | collective-permute-start | bytes 1572872 | tf_op jit(solution)/shard_map/ppermute | solution.py:834
  128.3 9.2 %collective-permute-start.30 = (bf16[1,2,2,512,128]{4,3,2,1,0:T(8,128)(2,1)S(1)}, bf16[1,2,2,512,128]{4,3,2,1,0:T(8,128)(2,1)S(1)}, u32[]{:S(2)}, u32[]{:S(2)}) collective-permute-start(bf16[1,2,2,512,128]{4,3,2,1,0:T(8,128)(2,1)S(1)} %get-tuple-element.95), channel_id=1, source_target_pairs={{0,8},{4,12},{8,0},{12,4},{16,24},{20,28},{24,16},{28,20},{1,9},{5... | collective-permute-start | bytes 1572872 | tf_op jit(solution)/shard_map/ppermute | solution.py:834
  128.9 23.4 %collective-permute-start.12 = (bf16[1,256,1024]{2,1,0:T(8,128)(2,1)}, bf16[1,256,1024]{2,1,0:T(8,128)(2,1)}, u32[]{:S(2)}, u32[]{:S(2)}) collective-permute-start(bf16[1,256,1024]{2,1,0:T(8,128)(2,1)} %get-tuple-element.71), channel_id=1, source_target_pairs={{0,1},{1,0},{2,3},{3,2},{4,5},{5,4},{6,7},{7,6},{8,9},{9,8},{10,11... | collective-permute-start | bytes 1572872 | tf_op jit(solution)/shard_map/ppermute | solution.py:834
  129.5 17.6 %collective-permute-start.25 = (bf16[1,128,1024]{2,1,0:T(8,128)(2,1)S(1)}, bf16[1,128,1024]{2,1,0:T(8,128)(2,1)S(1)}, u32[]{:S(2)}, u32[]{:S(2)}) collective-permute-start(bf16[1,128,1024]{2,1,0:T(8,128)(2,1)S(1)} %shard_map.231.refs_0_.refs_1_), channel_id=1, source_target_pairs={{0,2},{1,3},{2,0},{3,1},{4,6},{5,7},{6,4},{7,5},{8,10},{9,11},{10,... | collective-permute-start | bytes 786440 | tf_op jit(solution)/shard_map/ppermute | solution.py:834
  131.2 9.2 %collective-permute-start.16 = (f32[6,1024]{1,0:T(8,128)S(1)}, f32[6,1024]{1,0:T(8,128)S(1)}, u32[]{:S(2)}, u32[]{:S(2)}) collective-permute-start(f32[6,1024]{1,0:T(8,128)S(1)} %shard_map.223.refs_0_), channel_id=1, source_target_pairs={{0,4},{4,0},{8,12},{12,8},{16,20},{20,16},{24,28},{28,24},{1,5},{5... | collective-permute-start | bytes 73736 | tf_op jit(solution)/shard_map/ppermute | solution.py:834
  138.6 26.2 %collective-permute-start.31 = (bf16[4,512,128]{2,1,0:T(8,128)(2,1)}, bf16[4,512,128]{2,1,0:T(8,128)(2,1)}, u32[]{:S(2)}, u32[]{:S(2)}) collective-permute-start(bf16[4,512,128]{2,1,0:T(8,128)(2,1)} %shard_map.235), channel_id=1, source_target_pairs={{0,2},{1,3},{2,0},{3,1},{4,6},{5,7},{6,4},{7,5},{8,10},{9,11},{10,... | collective-permute-start | bytes 1572872 | tf_op jit(solution)/shard_map/ppermute | solution.py:834
  140.5 11.1 %collective-permute-start.17 = (f32[6,1024]{1,0:T(8,128)S(1)}, f32[6,1024]{1,0:T(8,128)S(1)}, u32[]{:S(2)}, u32[]{:S(2)}) collective-permute-start(f32[6,1024]{1,0:T(8,128)S(1)} %shard_map.224.refs_0_), channel_id=1, source_target_pairs={{0,8},{4,12},{8,0},{12,4},{16,24},{20,28},{24,16},{28,20},{1,9},{5... | collective-permute-start | bytes 73736 | tf_op jit(solution)/shard_map/ppermute | solution.py:834
  147.1 20.8 %collective-permute-start.26 = (bf16[2,128,1024]{2,1,0:T(8,128)(2,1)S(1)}, bf16[2,128,1024]{2,1,0:T(8,128)(2,1)S(1)}, u32[]{:S(2)}, u32[]{:S(2)}) collective-permute-start(bf16[2,128,1024]{2,1,0:T(8,128)(2,1)S(1)} %shard_map.232), channel_id=1, source_target_pairs={{0,1},{1,0},{2,3},{3,2},{4,5},{5,4},{6,7},{7,6},{8,9},{9,8},{10,11... | collective-permute-start | bytes 1572872 | tf_op jit(solution)/shard_map/ppermute | solution.py:834
  151.6 4.0 %collective-permute-start.18 = (f32[6,1024]{1,0:T(8,128)S(1)}, f32[6,1024]{1,0:T(8,128)S(1)}, u32[]{:S(2)}, u32[]{:S(2)}) collective-permute-start(f32[6,1024]{1,0:T(8,128)S(1)} %shard_map.225.refs_0_), channel_id=1, source_target_pairs={{0,16},{4,20},{8,24},{12,28},{16,0},{20,4},{24,8},{28,12},{1,17},{... | collective-permute-start | bytes 73736 | tf_op jit(solution)/shard_map/ppermute | solution.py:834
  155.6 9.2 %copy-start.20 = (bf16[1,2,2,512,128]{4,3,2,1,0:T(8,128)(2,1)S(1)}, bf16[1,2,2,512,128]{4,3,2,1,0:T(8,128)(2,1)}, u32[]{:S(2)}) copy-start(bf16[1,2,2,512,128]{4,3,2,1,0:T(8,128)(2,1)} %copy-done.19) | copy-start | bytes 1572868
  166.1 3.6 %collective-permute-start.32 = (bf16[2,512,128]{2,1,0:T(8,128)(2,1)S(1)}, bf16[2,512,128]{2,1,0:T(8,128)(2,1)S(1)}, u32[]{:S(2)}, u32[]{:S(2)}) collective-permute-start(bf16[2,512,128]{2,1,0:T(8,128)(2,1)S(1)} %get-tuple-element.97), channel_id=1, source_target_pairs={{0,4},{4,0},{8,12},{12,8},{16,20},{20,16},{24,28},{28,24},{1,5},{5... | collective-permute-start | bytes 786440 | tf_op jit(solution)/shard_map/ppermute | solution.py:834
  (15 other events, 47.4 us)

commit v4 on v3

--- a/solution.py
+++ b/solution.py
@@ -20,7 +20,7 @@
 F32 = jnp.float32
 MIB = 1 << 20
 BIAS_ROWS = 16
-COST = {'pack': 3, 'prep': 1, 'A': 0.05, 'B': 1, 'A3': 25, 'M': 50, 'cross': 0.3, 'at1': 12, 'fo1': 0.05, 'both': 6, 'parts': 0.05, 'aown': 0.05, 'mine': 3, 'nb': 1, 'ro': 12, 'sm': 50, 'af': 50, 'rf': 25, 'ff': 1, 'zadd': 6, 'zjoin': 1}
+COST = {'pack': 3, 'prep': 1, 'A': 0.05, 'B': 1, 'A3': 25, 'M': 50, 'cross': 0.3, 'at1': 12, 'fo1': 0.05, 'both': 6, 'parts': 0.05, 'aown': 0.05, 'mine': 3, 'nb': 1, 'ro': 12, 'sm': 6, 'af': 50, 'rf': 25, 'ff': 1, 'zadd': 6, 'zjoin': 1}
 CFG = {'deep0': 1, 'deep1': 4, 'sidesB': 1, 'sidesS': 1, 'sidesC': 1, 'sidesD': 0, 'W2': 1, 'A3S': 2, 'bothA3': 1, 'attnBoth': 1, 'MA3': 1, 'cross2': 1, 'at1': 1, 'fo1': 3, 'first': 0, 'nb': 1, 'parts': 0, 'both': 1, 'send': 1}
 SUMS = 4
 
@@ -215,7 +215,7 @@
             pltpu.SemaphoreType.DMA((4,)),
         ],
         specs={0: SMEM, 1: SMEM, 2: SMEM, 3: HBM, 4: HBM, 5: HBM, 6: HBM},
-        vmem=58,
+        vmem=57,
         after=after,
         tag="prep",
     )
@@ -368,7 +368,7 @@
             pltpu.SemaphoreType.DMA((4 * blocks,)),
         ],
         specs={4: HBM, 5: HBM},
-        vmem=52,
+        vmem=56,
         after=after,
         tag="A",
     )

time: 171 us -> 169 us (0.988)
  local copies, waits for them, and re-layouts: 7.31 us -> 3.24 us
  starting transfers between devices: 37.8 us -> 40.6 us
  Pallas kernels: 53.8 us -> 51.8 us
    unnamed x60 -> x30, local copies, waits for them, and re-layouts: 7.31 us -> 3.24 us
    ppermute x33, starting transfers between devices: 37.8 us -> 40.6 us  [exchange(): return lax.ppermute(x, axis, [(i, i ^ flip) for i in range(n)])]
    pallas_call x25, Pallas kernels: 53.8 us -> 51.8 us  [call(): pl.pallas_call(body, in_specs=[specs.get(n, VMEM) for n in range(count)]...]
  transfers between devices with their start and end apart: 33 -> 33, of which waited for: 16 -> 17; matrix products, arithmetic and copies ran while one was open for 0% -> 0% of each run, Pallas kernels for 30% -> 29%
where the time goes in v4:
time: 169 us
  waiting for transfers between devices  72.2 us (43%)
  Pallas kernels  51.8 us (31%)
  starting transfers between devices  40.6 us (24%)
  local copies, waits for them, and re-layouts  3.24 us (2%)
    ppermute x33, waiting for transfers between devices, exchange(): return lax.ppermute(x, axis, [(i, i ^ flip) for i in range(n)])  72.2 us
    pallas_call x25, Pallas kernels, call(): pl.pallas_call(body, in_specs=[specs.get(n, VMEM) for n in range(count)]...  51.8 us
    ppermute x33, starting transfers between devices, exchange(): return lax.ppermute(x, axis, [(i, i ^ flip) for i in range(n)])  40.6 us
  transfers between devices with their start and end apart: 33, of which 17 were waited for; matrix products, arithmetic and copies ran while one was open for 0% of the time, Pallas kernels for 29%

profile of v4, /device:TPU:0, one launch (start us, length us, event | category | flops | bytes accessed | tf_op | source)
XLA Modules:
  0.0 168.8 jit_solution(4756035972188497924)
XLA Ops:
  0.6 1.9 %shard_map.213.refs_7_ = bf16[272,1024]{1,0:T(8,128)(2,1)} custom-call(f32[1,1024]{1,0:T(1,128)} %bitcast.12, bf16[1024,1024]{1,0:T(8,128)(2,1)} %refs_8_.1, bf16[1024,1024]{1,0:T(8,128)(2,1)} %refs_9_.1), custom_call_target="tpu_custom_call" | custom-call | flops 3000000000 | bytes 1024 | tf_op jit(solution)/shard_map/pallas_call | solution.py:47
  2.6 4.1 %collective-permute-start.3 = (bf16[272,1024]{1,0:T(8,128)(2,1)}, bf16[272,1024]{1,0:T(8,128)(2,1)}, u32[]{:S(2)}, u32[]{:S(2)}) collective-permute-start(bf16[272,1024]{1,0:T(8,128)(2,1)} %shard_map.213.refs_7_), channel_id=1, source_target_pairs={{0,2},{1,3},{2,0},{3,1},{4,6},{5,7},{6,4},{7,5},{8,10},{9,11},{10,... | collective-permute-start | bytes 1671176 | tf_op jit(solution)/shard_map/ppermute | solution.py:834
  6.7 3.4 %shard_map.214 = (s32[24,256]{1,0:T(8,128)}, bf16[256,1024]{1,0:T(8,128)(2,1)}, bf16[256,1024]{1,0:T(8,128)(2,1)}, f32[1,1024]{1,0:T(1,128)}) custom-call(s32[1,16]{1,0:T(1,128)} %refs_0_.1, s32[1,4]{1,0:T(1,128)} %refs_1_.6, s32[1,4]{1,0:T(1,128)} %refs_2_.5, bf16[256,1024]{1,0:T(8,128)(2,1)} %refs_1_.9, bf16[256,1024]{1,0:T(8,128)(2,1)} %refs_2_.7, ...), custom_call_target="tpu_custom_call" | custom-call | flops 1000000000 | bytes 1024 | tf_op jit(solution)/shard_map/pallas_call | solution.py:47
  10.7 13.1 %shard_map.215.refs_0_.refs_4_ = bf16[4,256,1024]{2,1,0:T(8,128)(2,1)} custom-call(s32[24,256]{1,0:T(8,128)} %get-tuple-element.56.refs_0_, bf16[256,1024]{1,0:T(8,128)(2,1)} %get-tuple-element.60.refs_1_.refs_0_, bf16[256,1024]{1,0:T(8,128)(2,1)} %get-tuple-element.61.refs_2_.refs_1_, f32[1,256]{1,0:T(1,128)} %constant.2.clone.refs_3_, ...), custom_call_target="tpu_custom_call" | custom-call | flops 50000000 | bytes 1024 | tf_op jit(solution)/shard_map/pallas_call | solution.py:47
  23.8 1.6 copy-done
  25.4 1.6 copy-done.1
  27.0 3.4 %shard_map.216 = (f32[256,1024]{1,0:T(8,128)S(1)}, f32[256,1024]{1,0:T(8,128)S(1)}) custom-call(bf16[4,256,1024]{2,1,0:T(8,128)(2,1)S(1)} %copy-done.1, bf16[1024,3072]{1,0:T(8,128)(2,1)S(1)} %bitcast.9, bf16[1024,1024]{1,0:T(8,128)(2,1)S(1)} %copy-done), custom_call_target="tpu_custom_call" | custom-call | flops 1000000000 | bytes 1024 | tf_op jit(solution)/shard_map/pallas_call | solution.py:47
  30.5 1.1 collective-permute-done.3.refs_6_.refs_10_
  31.6 0.8 collective-permute-start.2
  32.3 2.4 %collective-permute-start.10 = (bf16[272,1024]{1,0:T(8,128)(2,1)}, bf16[272,1024]{1,0:T(8,128)(2,1)S(1)}, u32[]{:S(2)}, u32[]{:S(2)}) collective-permute-start(bf16[272,1024]{1,0:T(8,128)(2,1)} %collective-permute-done.3.refs_6_.refs_10_), channel_id=1, source_target_pairs={{0,24},{4,28},{8,16},{12,20},{16,8},{20,12},{24,0},{28,4},{1,25},{... | collective-permute-start | bytes 1671176 | tf_op jit(solution)/shard_map/ppermute | solution.py:834
  35.8 1.3 collective-permute-start.4
  37.1 4.0 %shard_map.217 = (bf16[2,2,128,1024]{3,2,1,0:T(8,128)(2,1)S(1)}, bf16[2,2,128,1024]{3,2,1,0:T(8,128)(2,1)S(1)}, bf16[2,2,128,1024]{3,2,1,0:T(8,128)(2,1)S(1)}, bf16[2,2,128,1024]{3,2,1,0:T(8,128)(2,1)S(1)}) custom-call(bf16[256,1024]{1,0:T(8,128)(2,1)S(1)} %copy-done.5, bf16[256,1024]{1,0:T(8,128)(2,1)} %collective-permute-done.refs_1_.refs_2_, ...), custom_call_target="tpu_custom_call" | custom-call | flops 24999999488 | bytes 1024 | tf_op jit(solution)/shard_map/pallas_call | solution.py:47
  41.2 16.0 %collective-permute-done.4.refs_5_ = bf16[256,1024]{1,0:T(8,128)(2,1)S(1)} collective-permute-done((bf16[256,1024]{1,0:T(8,128)(2,1)S(1)}, bf16[256,1024]{1,0:T(8,128)(2,1)S(1)}, u32[]{:S(2)}, u32[]{:S(2)}) %collective-permute-start.4) | collective-permute-done | bytes 524320 | tf_op jit(solution)/shard_map/ppermute | solution.py:834
  57.6 1.4 collective-permute-done.7.refs_7_
  59.0 0.7 collective-permute-done.6.refs_6_
  59.8 1.6 collective-permute-start.20
  61.4 1.5 collective-permute-start.19
  62.9 18.0 %shard_map.218 = (f32[2,512]{1,0:T(2,128)S(1)}, bf16[2,2,256,1024]{3,2,1,0:T(8,128)(2,1)S(1)}, bf16[2,2,2,512,128]{4,3,2,1,0:T(8,128)(2,1)S(1)}, bf16[2,2,2,512,...) custom-call(bf16[256,1024]{1,0:T(8,128)(2,1)S(1)} %copy-done.5, ...), custom_call_target="tpu_custom_call" | custom-call | flops 49999998976 | bytes 1024 | tf_op jit(solution)/shard_map/pallas_call | solution.py:47
  81.0 4.0 %collective-permute-done.20.refs_3_.refs_4_.refs_1_ = bf16[2,2,128,1024]{3,2,1,0:T(8,128)(2,1)S(1)} collective-permute-done((bf16[2,2,128,1024]{3,2,1,0:T(8,128)(2,1)S(1)}, bf16[2,2,128,1024]{3,2,1,0:T(8,128)(2,1)S(1)}, u32[]{:S(2)}, u32[]{:S(2)}) %collective-permute-start.20) | collective-permute-done | bytes 1048608 | tf_op jit(solution)/shard_map/ppermute | solution.py:834
  85.0 1.3 collective-permute-done.19.refs_1_
  87.0 1.5 collective-permute-start.22
  88.9 0.7 collective-permute-start.13
  89.6 9.8 %collective-permute-done.21.refs_2_ = bf16[1,2,128,1024]{3,2,1,0:T(8,128)(2,1)S(1)} collective-permute-done((bf16[1,2,128,1024]{3,2,1,0:T(8,128)(2,1)S(1)}, bf16[1,2,128,1024]{3,2,1,0:T(8,128)(2,1)S(1)}, u32[]{:S(2)}, u32[]{:S(2)}) %collective-permute-start.21) | collective-permute-done | bytes 524320 | tf_op jit(solution)/shard_map/ppermute | solution.py:834
  99.9 0.7 collective-permute-start.23
  100.7 1.5 collective-permute-start.27
  102.2 1.4 collective-permute-start.28
  103.6 1.1 shard_map.221
  104.7 1.4 collective-permute-start.14
  106.1 6.8 %collective-permute-done.23.refs_3_ = bf16[2,128,1024]{2,1,0:T(8,128)(2,1)S(1)} collective-permute-done((bf16[2,128,1024]{2,1,0:T(8,128)(2,1)S(1)}, bf16[2,128,1024]{2,1,0:T(8,128)(2,1)S(1)}, u32[]{:S(2)}, u32[]{:S(2)}) %collective-permute-start.23) | collective-permute-done | bytes 524320 | tf_op jit(solution)/shard_map/ppermute | solution.py:834
  113.0 2.4 %collective-permute-start.24 = (bf16[1,128,1024]{2,1,0:T(8,128)(2,1)S(1)}, bf16[1,128,1024]{2,1,0:T(8,128)(2,1)S(1)}, u32[]{:S(2)}, u32[]{:S(2)}) collective-permute-start(bf16[1,128,1024]{2,1,0:T(8,128)(2,1)S(1)} %shard_map.230), channel_id=1, source_target_pairs={{0,2},{1,3},{2,0},{3,1},{4,6},{5,7},{6,4},{7,5},{8,10},{9,11},{10,... | collective-permute-start | bytes 786440 | tf_op jit(solution)/shard_map/ppermute | solution.py:834
  115.4 0.7 collective-permute-start.15
  116.1 7.2 %collective-permute-done.27.refs_1_.refs_2_ = bf16[2,2,2,512,128]{4,3,2,1,0:T(8,128)(2,1)S(1)} collective-permute-done((bf16[2,2,2,512,128]{4,3,2,1,0:T(8,128)(2,1)S(1)}, bf16[2,2,2,512,128]{4,3,2,1,0:T(8,128)(2,1)S(1)}, u32[]{:S(2)}, u32[]{:S(2)}) %collective-permute-start.27) | collective-permute-done | bytes 1048608 | tf_op jit(solution)/shard_map/ppermute | solution.py:834
  123.3 1.8 %collective-permute-done.28.refs_3_.refs_4_.refs_5_ = bf16[2,2,2,512,128]{4,3,2,1,0:T(8,128)(2,1)S(1)} collective-permute-done((bf16[2,2,2,512,128]{4,3,2,1,0:T(8,128)(2,1)S(1)}, bf16[2,2,2,512,128]{4,3,2,1,0:T(8,128)(2,1)S(1)}, u32[]{:S(2)}, u32[]{:S(2)}) %collective-permute-start.28) | collective-permute-done | bytes 1048608 | tf_op jit(solution)/shard_map/ppermute | solution.py:834
  125.4 1.5 collective-permute-start.29
  127.4 1.4 collective-permute-start.12
  128.9 2.4 %collective-permute-start.25 = (bf16[1,128,1024]{2,1,0:T(8,128)(2,1)S(1)}, bf16[1,128,1024]{2,1,0:T(8,128)(2,1)S(1)}, u32[]{:S(2)}, u32[]{:S(2)}) collective-permute-start(bf16[1,128,1024]{2,1,0:T(8,128)(2,1)S(1)} %shard_map.231.refs_0_.refs_1_), channel_id=1, source_target_pairs={{0,2},{1,3},{2,0},{3,1},{4,6},{5,7},{6,4},{7,5},{8,10},{9,11},{10,... | collective-permute-start | bytes 786440 | tf_op jit(solution)/shard_map/ppermute | solution.py:834
  131.4 4.4 %collective-permute-done.29.refs_2_.refs_3_ = bf16[1,2,2,512,128]{4,3,2,1,0:T(8,128)(2,1)S(1)} collective-permute-done((bf16[1,2,2,512,128]{4,3,2,1,0:T(8,128)(2,1)S(1)}, bf16[1,2,2,512,128]{4,3,2,1,0:T(8,128)(2,1)S(1)}, u32[]{:S(2)}, u32[]{:S(2)}) %collective-permute-start.29) | collective-permute-done | bytes 524320 | tf_op jit(solution)/shard_map/ppermute | solution.py:834
  136.3 3.8 %collective-permute-start.31 = (bf16[4,512,128]{2,1,0:T(8,128)(2,1)S(1)}, bf16[4,512,128]{2,1,0:T(8,128)(2,1)S(1)}, u32[]{:S(2)}, u32[]{:S(2)}) collective-permute-start(bf16[4,512,128]{2,1,0:T(8,128)(2,1)S(1)} %shard_map.235), channel_id=1, source_target_pairs={{0,2},{1,3},{2,0},{3,1},{4,6},{5,7},{6,4},{7,5},{8,10},{9,11},{10,... | collective-permute-start | bytes 1572872 | tf_op jit(solution)/shard_map/ppermute | solution.py:834
  140.7 5.8 %collective-permute-done.25.refs_1_.refs_2_ = bf16[1,128,1024]{2,1,0:T(8,128)(2,1)S(1)} collective-permute-done((bf16[1,128,1024]{2,1,0:T(8,128)(2,1)S(1)}, bf16[1,128,1024]{2,1,0:T(8,128)(2,1)S(1)}, u32[]{:S(2)}, u32[]{:S(2)}) %collective-permute-start.25) | collective-permute-done | bytes 262176 | tf_op jit(solution)/shard_map/ppermute | solution.py:834
  146.5 4.9 %collective-permute-start.26 = (bf16[2,128,1024]{2,1,0:T(8,128)(2,1)S(1)}, bf16[2,128,1024]{2,1,0:T(8,128)(2,1)S(1)}, u32[]{:S(2)}, u32[]{:S(2)}) collective-permute-start(bf16[2,128,1024]{2,1,0:T(8,128)(2,1)S(1)} %shard_map.232), channel_id=1, source_target_pairs={{0,1},{1,0},{2,3},{3,2},{4,5},{5,4},{6,7},{7,6},{8,9},{9,8},{10,11... | collective-permute-start | bytes 1572872 | tf_op jit(solution)/shard_map/ppermute | solution.py:834
  151.4 0.7 collective-permute-start.18
  152.1 1.3 shard_map.220
  153.3 2.0 %collective-permute-done.18.refs_1_ = f32[6,1024]{1,0:T(8,128)S(1)} collective-permute-done((f32[6,1024]{1,0:T(8,128)S(1)}, f32[6,1024]{1,0:T(8,128)S(1)}, u32[]{:S(2)}, u32[]{:S(2)}) %collective-permute-start.18) | collective-permute-done | bytes 24608 | tf_op jit(solution)/shard_map/ppermute | solution.py:834
  155.4 1.1 shard_map.227
  156.5 8.0 %collective-permute-done.31.refs_0_ = bf16[4,512,128]{2,1,0:T(8,128)(2,1)S(1)} collective-permute-done((bf16[4,512,128]{2,1,0:T(8,128)(2,1)S(1)}, bf16[4,512,128]{2,1,0:T(8,128)(2,1)S(1)}, u32[]{:S(2)}, u32[]{:S(2)}) %collective-permute-start.31) | collective-permute-done | bytes 524320 | tf_op jit(solution)/shard_map/ppermute | solution.py:834
  164.8 1.2 collective-permute-done.26.refs_3_
  166.0 1.7 shard_map.233
  167.7 1.1 shard_map.237
  (74 shorter events, 6.4 us)
Async XLA Ops:
  2.6 29.0 %collective-permute-start.3 = (bf16[272,1024]{1,0:T(8,128)(2,1)}, bf16[272,1024]{1,0:T(8,128)(2,1)}, u32[]{:S(2)}, u32[]{:S(2)}) collective-permute-start(bf16[272,1024]{1,0:T(8,128)(2,1)} %shard_map.213.refs_7_), channel_id=1, source_target_pairs={{0,2},{1,3},{2,0},{3,1},{4,6},{5,7},{6,4},{7,5},{8,10},{9,11},{10,... | collective-permute-start | bytes 1671176 | tf_op jit(solution)/shard_map/ppermute | solution.py:834
  6.7 17.1 %slice-start = ((s8[6291456]{0:T(1024)(128)(4,1)}), s8[2097152]{0:T(1024)(128)(4,1)S(1)}, s32[]{:S(2)}) async-start(s8[6291456]{0:T(1024)(128)(4,1)} %bitcast.8), calls=%async_computation | async-start | bytes 4194304
  10.1 20.4 %collective-permute-start = (bf16[256,1024]{1,0:T(8,128)(2,1)}, bf16[256,1024]{1,0:T(8,128)(2,1)}, u32[]{:S(2)}, u32[]{:S(2)}) collective-permute-start(bf16[256,1024]{1,0:T(8,128)(2,1)} %get-tuple-element.60.refs_1_.refs_0_), channel_id=1, source_target_pairs={{0,4},{4,0},{8,12},{12,8},{16,20},{20,16},{24,28},{28,24},{1,5},{5... | collective-permute-start | bytes 1572872 | tf_op jit(solution)/shard_map/ppermute | solution.py:834
  10.2 20.3 %collective-permute-start.1 = (bf16[256,1024]{1,0:T(8,128)(2,1)}, bf16[256,1024]{1,0:T(8,128)(2,1)}, u32[]{:S(2)}, u32[]{:S(2)}) collective-permute-start(bf16[256,1024]{1,0:T(8,128)(2,1)} %get-tuple-element.61.refs_2_.refs_1_), channel_id=1, source_target_pairs={{0,4},{4,0},{8,12},{12,8},{16,20},{20,16},{24,28},{28,24},{1,5},{5... | collective-permute-start | bytes 1572872 | tf_op jit(solution)/shard_map/ppermute | solution.py:834
  10.7 13.1 %slice-start.1 = ((s8[6291456]{0:T(1024)(128)(4,1)}), s8[4194304]{0:T(1024)(128)(4,1)S(1)}, s32[]{:S(2)}) async-start(s8[6291456]{0:T(1024)(128)(4,1)} %bitcast.8), calls=%async_computation.1 | async-start | bytes 8388608
  23.8 1.6 copy-start
  25.4 1.6 copy-start.1
  27.0 4.5 %copy-start.5 = (bf16[256,1024]{1,0:T(8,128)(2,1)S(1)}, bf16[256,1024]{1,0:T(8,128)(2,1)}, u32[]{:S(2)}) copy-start(bf16[256,1024]{1,0:T(8,128)(2,1)} %get-tuple-element.60.refs_1_.refs_0_) | copy-start | bytes 1572868
  27.0 8.8 %copy-start.6 = (bf16[256,1024]{1,0:T(8,128)(2,1)S(1)}, bf16[256,1024]{1,0:T(8,128)(2,1)}, u32[]{:S(2)}) copy-start(bf16[256,1024]{1,0:T(8,128)(2,1)} %get-tuple-element.61.refs_2_.refs_1_) | copy-start | bytes 1572868
  27.0 10.1 %copy-start.2 = (bf16[4,256,1024]{2,1,0:T(8,128)(2,1)S(1)}, bf16[4,256,1024]{2,1,0:T(8,128)(2,1)}, u32[]{:S(2)}) copy-start(bf16[4,256,1024]{2,1,0:T(8,128)(2,1)} %shard_map.215.refs_0_.refs_4_) | copy-start | bytes 6291460
  31.5 31.3 %copy-start.10 = (bf16[1024,1024]{1,0:T(8,128)(2,1)S(1)}, bf16[1024,1024]{1,0:T(8,128)(2,1)}, u32[]{:S(2)}) copy-start(bf16[1024,1024]{1,0:T(8,128)(2,1)} %refs_8_.1) | copy-start | bytes 6291460
  31.5 31.3 %copy-start.11 = (f32[1024]{0:T(1024)S(1)}, f32[1024]{0:T(1024)}, u32[]{:S(2)}) copy-start(f32[1024]{0:T(1024)} %param.21) | copy-start | bytes 12292
  31.5 4.3 %collective-permute-start.5 = (bf16[4,256,1024]{2,1,0:T(8,128)(2,1)S(1)}, bf16[4,256,1024]{2,1,0:T(8,128)(2,1)S(1)}, u32[]{:S(2)}, u32[]{:S(2)}) collective-permute-start(bf16[4,256,1024]{2,1,0:T(8,128)(2,1)S(1)} %copy-done.1), channel_id=1, source_target_pairs={{0,4},{4,0},{8,12},{12,8},{16,20},{20,16},{24,28},{28,24},{1,5},{5... | collective-permute-start | bytes 6291464 | tf_op jit(solution)/shard_map/ppermute | solution.py:834
  31.6 25.6 %collective-permute-start.2 = (bf16[256,1024]{1,0:T(8,128)(2,1)S(1)}, bf16[256,1024]{1,0:T(8,128)(2,1)S(1)}, u32[]{:S(2)}, u32[]{:S(2)}) collective-permute-start(bf16[256,1024]{1,0:T(8,128)(2,1)S(1)} %copy-done.5), channel_id=1, source_target_pairs={{0,1},{1,0},{2,3},{3,2},{4,5},{5,4},{6,7},{7,6},{8,9},{9,8},{10,11... | collective-permute-start | bytes 1572872 | tf_op jit(solution)/shard_map/ppermute | solution.py:834
  32.3 30.5 %collective-permute-start.10 = (bf16[272,1024]{1,0:T(8,128)(2,1)}, bf16[272,1024]{1,0:T(8,128)(2,1)S(1)}, u32[]{:S(2)}, u32[]{:S(2)}) collective-permute-start(bf16[272,1024]{1,0:T(8,128)(2,1)} %collective-permute-done.3.refs_6_.refs_10_), channel_id=1, source_target_pairs={{0,24},{4,28},{8,16},{12,20},{16,8},{20,12},{24,0},{28,4},{1,25},{... | collective-permute-start | bytes 1671176 | tf_op jit(solution)/shard_map/ppermute | solution.py:834
  34.8 28.1 %collective-permute-start.8 = (bf16[272,1024]{1,0:T(8,128)(2,1)}, bf16[272,1024]{1,0:T(8,128)(2,1)S(1)}, u32[]{:S(2)}, u32[]{:S(2)}) collective-permute-start(bf16[272,1024]{1,0:T(8,128)(2,1)} %collective-permute-done.3.refs_6_.refs_10_), channel_id=1, source_target_pairs={{0,8},{4,12},{8,0},{12,4},{16,24},{20,28},{24,16},{28,20},{1,9},{5... | collective-permute-start | bytes 1671176 | tf_op jit(solution)/shard_map/ppermute | solution.py:834
  35.3 27.5 %collective-permute-start.9 = (bf16[272,1024]{1,0:T(8,128)(2,1)}, bf16[272,1024]{1,0:T(8,128)(2,1)S(1)}, u32[]{:S(2)}, u32[]{:S(2)}) collective-permute-start(bf16[272,1024]{1,0:T(8,128)(2,1)} %collective-permute-done.3.refs_6_.refs_10_), channel_id=1, source_target_pairs={{0,16},{4,20},{8,24},{12,28},{16,0},{20,4},{24,8},{28,12},{1,17},{... | collective-permute-start | bytes 1671176 | tf_op jit(solution)/shard_map/ppermute | solution.py:834
  35.8 21.3 %collective-permute-start.4 = (bf16[256,1024]{1,0:T(8,128)(2,1)S(1)}, bf16[256,1024]{1,0:T(8,128)(2,1)S(1)}, u32[]{:S(2)}, u32[]{:S(2)}) collective-permute-start(bf16[256,1024]{1,0:T(8,128)(2,1)S(1)} %copy-done.6), channel_id=1, source_target_pairs={{0,1},{1,0},{2,3},{3,2},{4,5},{5,4},{6,7},{7,6},{8,9},{9,8},{10,11... | collective-permute-start | bytes 1572872 | tf_op jit(solution)/shard_map/ppermute | solution.py:834
  57.1 1.9 %collective-permute-start.7 = (bf16[256,1024]{1,0:T(8,128)(2,1)S(1)}, bf16[256,1024]{1,0:T(8,128)(2,1)S(1)}, u32[]{:S(2)}, u32[]{:S(2)}) collective-permute-start(bf16[256,1024]{1,0:T(8,128)(2,1)S(1)} %collective-permute-done.4.refs_5_), channel_id=1, source_target_pairs={{0,4},{4,0},{8,12},{12,8},{16,20},{20,16},{24,28},{28,24},{1,5},{5... | collective-permute-start | bytes 1572872 | tf_op jit(solution)/shard_map/ppermute | solution.py:834
  57.1 2.7 %collective-permute-start.6 = (bf16[256,1024]{1,0:T(8,128)(2,1)S(1)}, bf16[256,1024]{1,0:T(8,128)(2,1)S(1)}, u32[]{:S(2)}, u32[]{:S(2)}) collective-permute-start(bf16[256,1024]{1,0:T(8,128)(2,1)S(1)} %collective-permute-done.2.refs_4_), channel_id=1, source_target_pairs={{0,4},{4,0},{8,12},{12,8},{16,20},{20,16},{24,28},{28,24},{1,5},{5... | collective-permute-start | bytes 1572872 | tf_op jit(solution)/shard_map/ppermute | solution.py:834
  59.8 25.2 %collective-permute-start.20 = (bf16[2,2,128,1024]{3,2,1,0:T(8,128)(2,1)S(1)}, bf16[2,2,128,1024]{3,2,1,0:T(8,128)(2,1)S(1)}, u32[]{:S(2)}, u32[]{:S(2)}) collective-permute-start(bf16[2,2,128,1024]{3,2,1,0:T(8,128)(2,1)S(1)} %get-tuple-element.85), channel_id=1, source_target_pairs={{0,16},{4,20},{8,24},{12,28},{16,0},{20,4},{24,8},{28,12},{1,17},{... | collective-permute-start | bytes 3145736 | tf_op jit(solution)/shard_map/ppermute | solution.py:834
  61.4 24.9 %collective-permute-start.19 = (bf16[2,2,128,1024]{3,2,1,0:T(8,128)(2,1)S(1)}, bf16[2,2,128,1024]{3,2,1,0:T(8,128)(2,1)S(1)}, u32[]{:S(2)}, u32[]{:S(2)}) collective-permute-start(bf16[2,2,128,1024]{3,2,1,0:T(8,128)(2,1)S(1)} %get-tuple-element.68.refs_15_), channel_id=1, source_target_pairs={{0,8},{4,12},{8,0},{12,4},{16,24},{20,28},{24,16},{28,20},{1,9},{5... | collective-permute-start | bytes 3145736 | tf_op jit(solution)/shard_map/ppermute | solution.py:834
  80.9 7.7 %collective-permute-start.11 = (bf16[2,2,256,1024]{3,2,1,0:T(8,128)(2,1)S(1)}, bf16[2,2,256,1024]{3,2,1,0:T(8,128)(2,1)S(1)}, u32[]{:S(2)}, u32[]{:S(2)}) collective-permute-start(bf16[2,2,256,1024]{3,2,1,0:T(8,128)(2,1)S(1)} %get-tuple-element.70), channel_id=1, source_target_pairs={{0,4},{4,0},{8,12},{12,8},{16,20},{20,16},{24,28},{28,24},{1,5},{5... | collective-permute-start | bytes 6291464 | tf_op jit(solution)/shard_map/ppermute | solution.py:834
  86.5 12.9 %collective-permute-start.21 = (bf16[1,2,128,1024]{3,2,1,0:T(8,128)(2,1)S(1)}, bf16[1,2,128,1024]{3,2,1,0:T(8,128)(2,1)S(1)}, u32[]{:S(2)}, u32[]{:S(2)}) collective-permute-start(bf16[1,2,128,1024]{3,2,1,0:T(8,128)(2,1)S(1)} %get-tuple-element.86.refs_4_), channel_id=1, source_target_pairs={{0,16},{4,20},{8,24},{12,28},{16,0},{20,4},{24,8},{28,12},{1,17},{... | collective-permute-start | bytes 1572872 | tf_op jit(solution)/shard_map/ppermute | solution.py:834
  87.0 12.7 %collective-permute-start.22 = (bf16[1,2,128,1024]{3,2,1,0:T(8,128)(2,1)S(1)}, bf16[1,2,128,1024]{3,2,1,0:T(8,128)(2,1)S(1)}, u32[]{:S(2)}, u32[]{:S(2)}) collective-permute-start(bf16[1,2,128,1024]{3,2,1,0:T(8,128)(2,1)S(1)} %get-tuple-element.87), channel_id=1, source_target_pairs={{0,8},{4,12},{8,0},{12,4},{16,24},{20,28},{24,16},{28,20},{1,9},{5... | collective-permute-start | bytes 1572872 | tf_op jit(solution)/shard_map/ppermute | solution.py:834
  88.8 14.8 %copy-start.3 = (bf16[256,1024]{1,0:T(8,128)(2,1)S(1)}, bf16[256,1024]{1,0:T(8,128)(2,1)}, u32[]{:S(2)}) copy-start(bf16[256,1024]{1,0:T(8,128)(2,1)} %refs_2_.7) | copy-start | bytes 1572868
  88.8 14.7 %copy-start.4 = (bf16[256,1024]{1,0:T(8,128)(2,1)S(1)}, bf16[256,1024]{1,0:T(8,128)(2,1)}, u32[]{:S(2)}) copy-start(bf16[256,1024]{1,0:T(8,128)(2,1)} %refs_1_.9) | copy-start | bytes 1572868
  88.9 14.7 %copy-start.7 = (s32[24,256]{1,0:T(8,128)S(1)}, s32[24,256]{1,0:T(8,128)}, u32[]{:S(2)}) copy-start(s32[24,256]{1,0:T(8,128)} %get-tuple-element.56.refs_0_) | copy-start | bytes 73732
  88.9 14.7 %copy-start.8 = (f32[1024]{0:T(1024)S(1)}, f32[1024]{0:T(1024)}, u32[]{:S(2)}) copy-start(f32[1024]{0:T(1024)} %param.16) | copy-start | bytes 12292
  88.9 14.7 %copy-start.9 = (f32[1,1024]{1,0:T(1,128)S(1)}, f32[1,1024]{1,0:T(1,128)}, u32[]{:S(2)}) copy-start(f32[1,1024]{1,0:T(1,128)} %get-tuple-element.73.refs_8_) | copy-start | bytes 12292
  88.9 14.7 %collective-permute-start.13 = (bf16[1,256,1024]{2,1,0:T(8,128)(2,1)S(1)}, bf16[1,256,1024]{2,1,0:T(8,128)(2,1)S(1)}, u32[]{:S(2)}, u32[]{:S(2)}) collective-permute-start(bf16[1,256,1024]{2,1,0:T(8,128)(2,1)S(1)} %get-tuple-element.72.refs_5_), channel_id=1, source_target_pairs={{0,1},{1,0},{2,3},{3,2},{4,5},{5,4},{6,7},{7,6},{8,9},{9,8},{10,11... | collective-permute-start | bytes 1572872 | tf_op jit(solution)/shard_map/ppermute | solution.py:834
  99.9 13.0 %collective-permute-start.23 = (bf16[2,128,1024]{2,1,0:T(8,128)(2,1)S(1)}, bf16[2,128,1024]{2,1,0:T(8,128)(2,1)S(1)}, u32[]{:S(2)}, u32[]{:S(2)}) collective-permute-start(bf16[2,128,1024]{2,1,0:T(8,128)(2,1)S(1)} %shard_map.229.refs_6_), channel_id=1, source_target_pairs={{0,1},{1,0},{2,3},{3,2},{4,5},{5,4},{6,7},{7,6},{8,9},{9,8},{10,11... | collective-permute-start | bytes 1572872 | tf_op jit(solution)/shard_map/ppermute | solution.py:834
  100.7 22.7 %collective-permute-start.27 = (bf16[2,2,2,512,128]{4,3,2,1,0:T(8,128)(2,1)S(1)}, bf16[2,2,2,512,128]{4,3,2,1,0:T(8,128)(2,1)S(1)}, u32[]{:S(2)}, u32[]{:S(2)}) collective-permute-start(bf16[2,2,2,512,128]{4,3,2,1,0:T(8,128)(2,1)S(1)} %get-tuple-element.91), channel_id=1, source_target_pairs={{0,8},{4,12},{8,0},{12,4},{16,24},{20,28},{24,16},{28,20},{1,9},{5... | collective-permute-start | bytes 3145736 | tf_op jit(solution)/shard_map/ppermute | solution.py:834
  102.2 23.0 %collective-permute-start.28 = (bf16[2,2,2,512,128]{4,3,2,1,0:T(8,128)(2,1)S(1)}, bf16[2,2,2,512,128]{4,3,2,1,0:T(8,128)(2,1)S(1)}, u32[]{:S(2)}, u32[]{:S(2)}) collective-permute-start(bf16[2,2,2,512,128]{4,3,2,1,0:T(8,128)(2,1)S(1)} %get-tuple-element.93), channel_id=1, source_target_pairs={{0,16},{4,20},{8,24},{12,28},{16,0},{20,4},{24,8},{28,12},{1,17},{... | collective-permute-start | bytes 3145736 | tf_op jit(solution)/shard_map/ppermute | solution.py:834
  104.7 10.7 %collective-permute-start.14 = (f32[6,1024]{1,0:T(8,128)S(1)}, f32[6,1024]{1,0:T(8,128)S(1)}, u32[]{:S(2)}, u32[]{:S(2)}) collective-permute-start(f32[6,1024]{1,0:T(8,128)S(1)} %get-tuple-element.75.refs_0_), channel_id=1, source_target_pairs={{0,1},{1,0},{2,3},{3,2},{4,5},{5,4},{6,7},{7,6},{8,9},{9,8},{10,11... | collective-permute-start | bytes 73736 | tf_op jit(solution)/shard_map/ppermute | solution.py:834
  113.0 15.7 %collective-permute-start.24 = (bf16[1,128,1024]{2,1,0:T(8,128)(2,1)S(1)}, bf16[1,128,1024]{2,1,0:T(8,128)(2,1)S(1)}, u32[]{:S(2)}, u32[]{:S(2)}) collective-permute-start(bf16[1,128,1024]{2,1,0:T(8,128)(2,1)S(1)} %shard_map.230), channel_id=1, source_target_pairs={{0,2},{1,3},{2,0},{3,1},{4,6},{5,7},{6,4},{7,5},{8,10},{9,11},{10,... | collective-permute-start | bytes 786440 | tf_op jit(solution)/shard_map/ppermute | solution.py:834
  115.4 15.9 %collective-permute-start.15 = (f32[6,1024]{1,0:T(8,128)S(1)}, f32[6,1024]{1,0:T(8,128)S(1)}, u32[]{:S(2)}, u32[]{:S(2)}) collective-permute-start(f32[6,1024]{1,0:T(8,128)S(1)} %shard_map.222.refs_0_), channel_id=1, source_target_pairs={{0,2},{1,3},{2,0},{3,1},{4,6},{5,7},{6,4},{7,5},{8,10},{9,11},{10,... | collective-permute-start | bytes 73736 | tf_op jit(solution)/shard_map/ppermute | solution.py:834
  125.4 10.4 %collective-permute-start.29 = (bf16[1,2,2,512,128]{4,3,2,1,0:T(8,128)(2,1)S(1)}, bf16[1,2,2,512,128]{4,3,2,1,0:T(8,128)(2,1)S(1)}, u32[]{:S(2)}, u32[]{:S(2)}) collective-permute-start(bf16[1,2,2,512,128]{4,3,2,1,0:T(8,128)(2,1)S(1)} %get-tuple-element.94), channel_id=1, source_target_pairs={{0,16},{4,20},{8,24},{12,28},{16,0},{20,4},{24,8},{28,12},{1,17},{... | collective-permute-start | bytes 1572872 | tf_op jit(solution)/shard_map/ppermute | solution.py:834
  126.9 9.2 %collective-permute-start.30 = (bf16[1,2,2,512,128]{4,3,2,1,0:T(8,128)(2,1)S(1)}, bf16[1,2,2,512,128]{4,3,2,1,0:T(8,128)(2,1)S(1)}, u32[]{:S(2)}, u32[]{:S(2)}) collective-permute-start(bf16[1,2,2,512,128]{4,3,2,1,0:T(8,128)(2,1)S(1)} %get-tuple-element.95), channel_id=1, source_target_pairs={{0,8},{4,12},{8,0},{12,4},{16,24},{20,28},{24,16},{28,20},{1,9},{5... | collective-permute-start | bytes 1572872 | tf_op jit(solution)/shard_map/ppermute | solution.py:834
  127.4 24.7 %collective-permute-start.12 = (bf16[1,256,1024]{2,1,0:T(8,128)(2,1)S(1)}, bf16[1,256,1024]{2,1,0:T(8,128)(2,1)S(1)}, u32[]{:S(2)}, u32[]{:S(2)}) collective-permute-start(bf16[1,256,1024]{2,1,0:T(8,128)(2,1)S(1)} %get-tuple-element.71), channel_id=1, source_target_pairs={{0,1},{1,0},{2,3},{3,2},{4,5},{5,4},{6,7},{7,6},{8,9},{9,8},{10,11... | collective-permute-start | bytes 1572872 | tf_op jit(solution)/shard_map/ppermute | solution.py:834
  128.9 17.5 %collective-permute-start.25 = (bf16[1,128,1024]{2,1,0:T(8,128)(2,1)S(1)}, bf16[1,128,1024]{2,1,0:T(8,128)(2,1)S(1)}, u32[]{:S(2)}, u32[]{:S(2)}) collective-permute-start(bf16[1,128,1024]{2,1,0:T(8,128)(2,1)S(1)} %shard_map.231.refs_0_.refs_1_), channel_id=1, source_target_pairs={{0,2},{1,3},{2,0},{3,1},{4,6},{5,7},{6,4},{7,5},{8,10},{9,11},{10,... | collective-permute-start | bytes 786440 | tf_op jit(solution)/shard_map/ppermute | solution.py:834
  131.3 8.8 %collective-permute-start.16 = (f32[6,1024]{1,0:T(8,128)S(1)}, f32[6,1024]{1,0:T(8,128)S(1)}, u32[]{:S(2)}, u32[]{:S(2)}) collective-permute-start(f32[6,1024]{1,0:T(8,128)S(1)} %shard_map.223.refs_0_), channel_id=1, source_target_pairs={{0,4},{4,0},{8,12},{12,8},{16,20},{20,16},{24,28},{28,24},{1,5},{5... | collective-permute-start | bytes 73736 | tf_op jit(solution)/shard_map/ppermute | solution.py:834
  136.3 28.2 %collective-permute-start.31 = (bf16[4,512,128]{2,1,0:T(8,128)(2,1)S(1)}, bf16[4,512,128]{2,1,0:T(8,128)(2,1)S(1)}, u32[]{:S(2)}, u32[]{:S(2)}) collective-permute-start(bf16[4,512,128]{2,1,0:T(8,128)(2,1)S(1)} %shard_map.235), channel_id=1, source_target_pairs={{0,2},{1,3},{2,0},{3,1},{4,6},{5,7},{6,4},{7,5},{8,10},{9,11},{10,... | collective-permute-start | bytes 1572872 | tf_op jit(solution)/shard_map/ppermute | solution.py:834
  140.1 11.3 %collective-permute-start.17 = (f32[6,1024]{1,0:T(8,128)S(1)}, f32[6,1024]{1,0:T(8,128)S(1)}, u32[]{:S(2)}, u32[]{:S(2)}) collective-permute-start(f32[6,1024]{1,0:T(8,128)S(1)} %shard_map.224.refs_0_), channel_id=1, source_target_pairs={{0,8},{4,12},{8,0},{12,4},{16,24},{20,28},{24,16},{28,20},{1,9},{5... | collective-permute-start | bytes 73736 | tf_op jit(solution)/shard_map/ppermute | solution.py:834
  146.5 5.6 %copy-start.12 = (f32[1024]{0:T(1024)S(1)}, f32[1024]{0:T(1024)}, u32[]{:S(2)}) copy-start(f32[1024]{0:T(1024)} %param.23) | copy-start | bytes 12292
  146.5 19.5 %collective-permute-start.26 = (bf16[2,128,1024]{2,1,0:T(8,128)(2,1)S(1)}, bf16[2,128,1024]{2,1,0:T(8,128)(2,1)S(1)}, u32[]{:S(2)}, u32[]{:S(2)}) collective-permute-start(bf16[2,128,1024]{2,1,0:T(8,128)(2,1)S(1)} %shard_map.232), channel_id=1, source_target_pairs={{0,1},{1,0},{2,3},{3,2},{4,5},{5,4},{6,7},{7,6},{8,9},{9,8},{10,11... | collective-permute-start | bytes 1572872 | tf_op jit(solution)/shard_map/ppermute | solution.py:834
  151.4 4.0 %collective-permute-start.18 = (f32[6,1024]{1,0:T(8,128)S(1)}, f32[6,1024]{1,0:T(8,128)S(1)}, u32[]{:S(2)}, u32[]{:S(2)}) collective-permute-start(f32[6,1024]{1,0:T(8,128)S(1)} %shard_map.225.refs_0_), channel_id=1, source_target_pairs={{0,16},{4,20},{8,24},{12,28},{16,0},{20,4},{24,8},{28,12},{1,17},{... | collective-permute-start | bytes 73736 | tf_op jit(solution)/shard_map/ppermute | solution.py:834
  164.7 3.0 %collective-permute-start.32 = (bf16[2,512,128]{2,1,0:T(8,128)(2,1)S(1)}, bf16[2,512,128]{2,1,0:T(8,128)(2,1)S(1)}, u32[]{:S(2)}, u32[]{:S(2)}) collective-permute-start(bf16[2,512,128]{2,1,0:T(8,128)(2,1)S(1)} %get-tuple-element.97), channel_id=1, source_target_pairs={{0,4},{4,0},{8,12},{12,8},{16,20},{20,16},{24,28},{28,24},{1,5},{5... | collective-permute-start | bytes 786440 | tf_op jit(solution)/shard_map/ppermute | solution.py:834
